TPU v7x, 256 devices: a whole 4x4x8 slice. The times are simulated.
256 devices in a mesh: blk: 16 (over x_lo, y, core), dp: 16 (over x_hi, z).
Axes of the slice: x: 4 (x_hi: 2, x_lo: 2; x = x_hi * 2 + x_lo), y: 4, z: 8, core: 2. Of those that a mesh axis runs over, the one named last changes fastest.
Arguments:
- normed_input: bfloat16 [256, 256, 5120], P(('blk', 'dp')), may hold values from -40 to 40
- segment_ids: int32 [16, 16, 256], P('dp'), may hold values from 0 to 3, never falling along the last dimension, each value on 1 to 128 neighbouring positions
- weights_qkv: bfloat16 [16, 5120, 384], P('blk'), may hold values from -0.08385255 to 0.08385255
- weights_out: bfloat16 [16, 128, 5120], P('blk'), may hold values from -0.5 to 0.5
- cotangent: bfloat16 [256, 256, 5120], P(('blk', 'dp')), may hold values from -24 to 24
Outputs:
- input_grad: bfloat16 [256, 256, 5120], P(('blk', 'dp'))
- grad_qkv: bfloat16 [16, 5120, 384], P('blk', 'dp')
- grad_out: bfloat16 [16, 128, 5120], P('blk', None, 'dp')
All inputs are finite; a program needn't handle non-finite values.
Results may differ from a plain program's by a relative error of at most 0.02.
Values may be sent and summed in bfloat16 or wider, within the bound.
No kernel may reach another device: no remote copies, remote signals or barrier semaphores. Data moves between devices by JAX's collectives and lax.ppermute only.
A program may use at most 128 MiB of HBM per device.

v0:
```python
import jax
import jax.numpy as jnp
from jax import lax
from jax.sharding import PartitionSpec as P


def shifted(block, axis, distance):
    devices = range(lax.axis_size(axis))
    route = [((i - distance) % len(devices), i) for i in devices]
    return lax.ppermute(block, axis, route)


def group_terms(inputs, seg_row, w_qkv, w_out, grad_in):
    head = w_out.shape[0]
    scale = head ** (-0.5)
    qkv = jnp.dot(inputs, w_qkv, preferred_element_type=jnp.float32).astype(jnp.bfloat16)
    query = qkv[:, :head]
    keys = qkv[:, head : 2 * head]
    values = qkv[:, 2 * head :]
    count = inputs.shape[0]
    places = jnp.arange(count, dtype=jnp.int32)
    allowed = (places[:, None] >= places[None, :]) & (seg_row[:, None] == seg_row[None, :])
    scores = jnp.dot(query, keys.T, preferred_element_type=jnp.float32) * scale
    scores = jnp.where(allowed, scores, jnp.float32(-1e30))
    top = jnp.max(scores, axis=-1, keepdims=True)
    expo = jnp.where(allowed, jnp.exp(scores - top), jnp.float32(0.0))
    probs = expo / jnp.sum(expo, axis=-1, keepdims=True)
    probs_b = probs.astype(jnp.bfloat16)
    attended = jnp.dot(probs_b, values, preferred_element_type=jnp.float32).astype(jnp.bfloat16)
    grad_wout = jnp.dot(attended.T, grad_in, preferred_element_type=jnp.float32)
    d_att = jnp.dot(grad_in, w_out.T, preferred_element_type=jnp.float32).astype(jnp.bfloat16)
    d_probs = jnp.dot(d_att, values.T, preferred_element_type=jnp.float32)
    d_scores = (
        probs * (d_probs - jnp.sum(probs * d_probs, axis=-1, keepdims=True)) * scale
    ).astype(jnp.bfloat16)
    d_query = jnp.dot(d_scores, keys, preferred_element_type=jnp.float32)
    d_keys = jnp.dot(d_scores.T, query, preferred_element_type=jnp.float32)
    d_values = jnp.dot(probs_b.T, d_att, preferred_element_type=jnp.float32)
    d_qkv = jnp.concatenate([d_query, d_keys, d_values], axis=1).astype(jnp.bfloat16)
    grad_wqkv = jnp.dot(inputs.T, d_qkv, preferred_element_type=jnp.float32)
    input_term = jnp.dot(d_qkv, w_qkv.T, preferred_element_type=jnp.float32)
    return (input_term, grad_wqkv, grad_wout)


def local(normed_input, segment_ids, weights_qkv, weights_out, cotangent):
    inputs = normed_input[0]
    grad_in = cotangent[0]
    here = lax.axis_index("blk")
    seg_table = segment_ids[0]
    own_seg = lax.dynamic_index_in_dim(seg_table, here, 0, keepdims=False)
    own_qkv = weights_qkv[0]
    own_out = weights_out[0]
    moved_qkv, moved_out = shifted((weights_qkv, weights_out), "blk", 1)
    term_own, gq_own, go_own = group_terms(inputs, own_seg, own_qkv, own_out, grad_in)
    term_far, gq_far, go_far = group_terms(inputs, own_seg, moved_qkv[0], moved_out[0], grad_in)
    input_grad = (term_own + term_far).astype(jnp.bfloat16)
    back_qkv, back_out = (
        shifted(gq_far.astype(jnp.bfloat16), "blk", -1).astype(gq_far.dtype),
        shifted(go_far.astype(jnp.bfloat16), "blk", -1).astype(go_far.dtype),
    )
    total_qkv, total_out = (
        lax.psum_scatter(
            (gq_own + back_qkv)[None].astype(jnp.bfloat16), "dp", scatter_dimension=1, tiled=True
        ).astype(jnp.float32),
        lax.psum_scatter(
            (go_own + back_out)[None].astype(jnp.bfloat16), "dp", scatter_dimension=2, tiled=True
        ).astype(jnp.float32),
    )
    return (input_grad[None], total_qkv.astype(jnp.bfloat16), total_out.astype(jnp.bfloat16))


def solution(mesh):
    placed = (
        P(("blk", "dp"), None, None),
        P("dp", None, None),
        P("blk", None, None),
        P("blk", None, None),
        P(("blk", "dp"), None, None),
    )
    return jax.shard_map(
        local,
        mesh=mesh,
        in_specs=placed,
        out_specs=(P(("blk", "dp"), None, None), P("blk", "dp", None), P("blk", None, "dp")),
        check_vma=False,
    )
```

profile of v0, /device:TPU:28, one launch (start us, length us, event | category | flops | bytes accessed | tf_op | source)
XLA Modules:
  0.0 580.5 jit_solution(14961350672679439024)
XLA Ops:
  7.2 0.0 copy-start
  7.2 0.0 reduce-scatter.9.cloned.1.call-start
  7.2 0.1 collective-permute-start
  7.3 1.0 collective-permute-start.1
  8.3 0.7 constant_dynamic-slice_fusion
  9.0 0.0 copy-done
  9.0 0.0 copy-start.1
  9.0 0.0 copy-start.2
  9.0 3.8 fusion.26
  12.8 0.0 copy-start.3
  12.8 0.2 fusion.88
  13.0 0.0 copy-done.1
  13.0 0.0 copy-done.2
  13.0 0.8 fusion.38
  13.9 52.9 %collective-permute-done.1 = bf16[1,128,5120]{2,1,0:T(8,128)(2,1)} collective-permute-done((bf16[1,128,5120]{2,1,0:T(8,128)(2,1)}, bf16[1,128,5120]{2,1,0:T(8,128)(2,1)}, u32[]{:S(2)}, u32[]{:S(2)}) %collective-permute-start.1) | collective-permute-done | bytes 1310752 | tf_op jit(solution)/shard_map/ppermute | solution.py:10
  66.8 2.2 fusion.43
  69.0 0.0 collective-permute-done
  69.0 3.6 fusion.31
  72.6 0.0 copy-start.4
  72.6 0.2 fusion.87
  72.9 0.1 fusion.54
  73.0 0.3 convolution_convert_fusion.4
  73.3 0.2 multiply_reduce_fusion
  73.5 0.0 copy-start.5
  73.5 0.0 copy-done.3
  73.5 0.2 multiply_reduce_fusion.1
  73.8 0.2 multiply_convert_fusion
  74.0 0.1 copy-done.5
  74.1 0.2 convolution_convert_fusion.5
  74.3 0.0 copy-done.4
  74.3 0.2 convolution_convert_fusion.6
  74.5 3.1 fusion.2
  77.6 0.0 collective-permute-start.2
  77.6 3.7 convolution_convert_fusion.1
  81.3 0.9 collective-permute-start.3
  82.2 53.0 %collective-permute-done.3 = bf16[128,5120]{1,0:T(8,128)(2,1)} collective-permute-done((bf16[128,5120]{1,0:T(8,128)(2,1)}, bf16[128,5120]{1,0:T(8,128)(2,1)}, u32[]{:S(2)}, u32[]{:S(2)}) %collective-permute-start.3) | collective-permute-done | bytes 1310752 | tf_op jit(solution)/shard_map/ppermute | solution.py:10
  135.2 4.1 fusion.23
  139.3 6.3 %copy.14 = bf16[1,128,5120]{1,0,2:T(2,128)(2,1)} copy(bf16[1,128,5120]{2,1,0:T(8,128)(2,1)} %fusion.23) | data formatting | bytes 2621440
  145.6 0.0 copy-start.6
  145.6 3.0 copy.23
  148.6 0.0 reduce-scatter.9.cloned.1.call-update
  148.6 0.2 reduce-scatter.7.cloned.1.call-start
  148.8 1.1 convolution_convert_fusion.8
  149.9 1.1 convolution_convert_fusion.9
  150.9 0.0 copy-done.6
  151.0 0.3 convolution_convert_fusion.7
  151.2 0.0 collective-permute-done.2
  151.3 5.3 fusion.3
  156.5 16.6 %copy.12 = bf16[1,5120,384]{2,0,1:T(2,128)(2,1)} copy(bf16[1,5120,384]{1,2,0:T(8,128)(2,1)} %fusion.3) | data formatting | bytes 7864320
  173.1 5.9 %copy.22 = bf16[5120,1,384]{2,0,1:T(8,128)(2,1)} copy(bf16[5120,1,384]{2,1,0:T(2,128)(2,1)} %bitcast.88) | data formatting | bytes 7864320
  179.0 0.0 reduce-scatter.7.cloned.1.call-update
  179.0 3.7 fusion.8
  182.7 5.2 fusion.4
  188.0 168.9 %reduce-scatter.9.cloned.1.call-done = bf16[320,128]{1,0:T(8,128)(2,1)} async-done(((bf16[5120,128]{1,0:T(8,128)(2,1)}), bf16[320,128]{1,0:T(8,128)(2,1)}) %reduce-scatter.9.cloned.1.call-update) | async-done | bytes 81936
  356.9 1.0 reshape_bitcast_fusion.1
  357.9 0.6 copy.11
  358.5 213.2 %reduce-scatter.7.cloned.1.call-done = bf16[320,384]{1,0:T(8,128)(2,1)} async-done(((bf16[5120,384]{1,0:T(8,128)(2,1)}), bf16[320,384]{1,0:T(8,128)(2,1)}) %reduce-scatter.7.cloned.1.call-update) | async-done | bytes 245776
  571.7 1.2 reshape_bitcast_fusion
  572.9 0.7 copy.10
Async XLA Ops:
  7.2 1.8 copy-start
  7.2 349.7 %reduce-scatter.9.cloned.1.call-start = ((), (), s32[]{:S(2)}) async-start(), calls=%async_computation.3 | async-start | bytes 1392640
  7.2 61.8 %collective-permute-start = (bf16[1,5120,384]{2,1,0:T(8,128)(2,1)}, bf16[1,5120,384]{2,1,0:T(8,128)(2,1)}, u32[]{:S(2)}, u32[]{:S(2)}) collective-permute-start(bf16[1,5120,384]{2,1,0:T(8,128)(2,1)} %param.7), channel_id=1, source_target_pairs={{240,0},{0,16},{16,32},{32,48},{48,64},{64,80},{80,96},{96,112},{1... | collective-permute-start | bytes 11796488 | tf_op jit(solution)/shard_map/ppermute | solution.py:10
  7.3 59.5 %collective-permute-start.1 = (bf16[1,128,5120]{2,1,0:T(8,128)(2,1)}, bf16[1,128,5120]{2,1,0:T(8,128)(2,1)}, u32[]{:S(2)}, u32[]{:S(2)}) collective-permute-start(bf16[1,128,5120]{2,1,0:T(8,128)(2,1)} %param.8), channel_id=1, source_target_pairs={{240,0},{0,16},{16,32},{32,48},{48,64},{64,80},{80,96},{96,112},{1... | collective-permute-start | bytes 3932168 | tf_op jit(solution)/shard_map/ppermute | solution.py:10
  9.0 4.0 copy-start.1
  9.0 4.0 copy-start.2
  12.8 60.8 %copy-start.3 = (bf16[256,384]{1,0:T(8,128)(2,1)}, bf16[256,384]{1,0:T(8,128)(2,1)S(1)}, u32[]{:S(2)}) copy-start(bf16[256,384]{1,0:T(8,128)(2,1)S(1)} %fusion.26) | copy-start | bytes 589828
  72.6 1.7 copy-start.4
  73.5 0.6 copy-start.5
  77.6 73.6 %collective-permute-start.2 = (bf16[5120,384]{0,1:T(8,128)(2,1)}, bf16[5120,384]{0,1:T(8,128)(2,1)}, u32[]{:S(2)}, u32[]{:S(2)}) collective-permute-start(bf16[5120,384]{0,1:T(8,128)(2,1)} %fusion.2), channel_id=1, source_target_pairs={{16,0},{32,16},{48,32},{64,48},{80,64},{96,80},{112,96},{128,112},... | collective-permute-start | bytes 11796488 | tf_op jit(solution)/shard_map/ppermute | solution.py:10
  81.3 53.9 %collective-permute-start.3 = (bf16[128,5120]{1,0:T(8,128)(2,1)}, bf16[128,5120]{1,0:T(8,128)(2,1)}, u32[]{:S(2)}, u32[]{:S(2)}) collective-permute-start(bf16[128,5120]{1,0:T(8,128)(2,1)} %convolution_convert_fusion.1), channel_id=1, source_target_pairs={{16,0},{32,16},{48,32},{64,48},{80,64},{96,80},{112,96},{128,112},... | collective-permute-start | bytes 3932168 | tf_op jit(solution)/shard_map/ppermute | solution.py:10
  145.6 5.4 copy-start.6
  148.6 423.1 %reduce-scatter.7.cloned.1.call-start = ((), (), s32[]{:S(2)}) async-start(), calls=%async_computation.2 | async-start | bytes 4177920
Sparse Core Ops, SparseCore 0:
  148.7 208.1 reduce-scatter.8
  361.5 210.1 reduce-scatter.6
where the time goes:
time: 584 us; the launch traced here: 580 us
  waiting for transfers between devices  488 us (84%)
  matrix products  39.6 us (7%)
  local copies, waits for them, and re-layouts  36.1 us (6%)
  between operations  14.2 us (2%)
    unnamed x4, waiting for transfers between devices  382 us
    ppermute x4, waiting for transfers between devices, shifted(): return lax.ppermute(block, axis, route)  106 us
    unnamed x22, local copies, waits for them, and re-layouts  35.4 us
  transfers between devices with their start and end apart: 6, of which 4 were waited for; matrix products, arithmetic and copies ran while one was open for 11% of the time, Pallas kernels for 0%

commit v1 on v0

v1 whole, which is shorter than its diff:
```python
import jax
import jax.numpy as jnp
from jax import lax
from jax.experimental import pallas as pl
from jax.experimental.pallas import tpu as pltpu
from jax.sharding import PartitionSpec as P

BF = jnp.bfloat16
F32 = jnp.float32
N_Z = 8


def dot(a, b, ca, cb):
    return lax.dot_general(a, b, (((ca,), (cb,)), ((), ())), preferred_element_type=F32)


def cost(flops, read):
    return pl.CostEstimate(flops=flops, bytes_accessed=read, transcendentals=0)


def params():
    return pltpu.CompilerParams(vmem_limit_bytes=32 * 1024 * 1024)


def attention_kernel(qkv_ref, datt_ref, seg_row_ref, seg_col_ref, dqkv_ref, att_ref):
    head = datt_ref.shape[1]
    count = datt_ref.shape[0]
    scale = head ** (-0.5)
    q = qkv_ref[:, :head]
    k = qkv_ref[:, head : 2 * head]
    v = qkv_ref[:, 2 * head :]
    datt = datt_ref[...]
    rows = lax.broadcasted_iota(jnp.int32, (count, count), 0)
    cols = lax.broadcasted_iota(jnp.int32, (count, count), 1)
    allowed = (rows >= cols) & (seg_col_ref[...] == seg_row_ref[...])
    scores = jnp.where(allowed, dot(q, k, 1, 1) * scale, F32(-1e30))
    top = jnp.max(scores, axis=-1, keepdims=True)
    expo = jnp.where(allowed, jnp.exp(scores - top), F32(0.0))
    probs = expo / jnp.sum(expo, axis=-1, keepdims=True)
    probs_b = probs.astype(BF)
    att_ref[...] = dot(probs_b, v, 1, 0).astype(BF)
    d_probs = dot(datt, v, 1, 1)
    inner = jnp.sum(probs * d_probs, axis=-1, keepdims=True)
    d_scores = (probs * (d_probs - inner) * scale).astype(BF)
    dqkv_ref[:, :head] = dot(d_scores, k, 1, 0).astype(BF)
    dqkv_ref[:, head : 2 * head] = dot(d_scores, q, 0, 0).astype(BF)
    dqkv_ref[:, 2 * head :] = dot(probs_b, datt, 0, 0).astype(BF)


def attention(qkv, datt, seg):
    count, head = datt.shape
    return pl.pallas_call(
        attention_kernel,
        out_shape=(
            jax.ShapeDtypeStruct((count, 3 * head), BF),
            jax.ShapeDtypeStruct((count, head), BF),
        ),
        compiler_params=params(),
        cost_estimate=cost(14 * count * count * head, 2 * count * head * 8),
        name="attention",
    )(qkv, datt, seg[None, :], seg[:, None])


def grads_kernel(x_ref, xf_ref, d_ref, df_ref, *outs):
    total = dot(x_ref[...], d_ref[...], 0, 0) + dot(xf_ref[...], df_ref[...], 0, 0)
    at = 0
    for out in outs:
        width = out.shape[1]
        out[...] = total[:, at : at + width].astype(BF)
        at += width


def grads(x, xf, d, df, widths, tile, name):
    count, model = x.shape
    whole = d.shape[1]
    step = pl.BlockSpec((count, tile), lambda i: (0, i))
    kept = pl.BlockSpec((count, whole), lambda i: (0, 0))
    return pl.pallas_call(
        grads_kernel,
        grid=(model // tile,),
        in_specs=[step, step, kept, kept],
        out_specs=[pl.BlockSpec((tile, w), lambda i: (i, 0)) for w in widths],
        out_shape=[jax.ShapeDtypeStruct((model, w), BF) for w in widths],
        compiler_params=params(),
        cost_estimate=cost(4 * count * model * whole, 4 * count * model + 2 * model * whole),
        name=name,
    )(x, xf, d, df)


def term_kernel(d_ref, w_ref, out_ref):
    out_ref[...] = dot(d_ref[...], w_ref[...], 1, 1).astype(BF)


def sum_term_kernel(d_ref, w_ref, far_ref, out_ref):
    out_ref[...] = (dot(d_ref[...], w_ref[...], 1, 1) + far_ref[...].astype(F32)).astype(BF)


def term(d, w, far=None, tile=1280):
    count, width = d.shape
    model = w.shape[0]
    specs = [
        pl.BlockSpec((count, width), lambda i: (0, 0)),
        pl.BlockSpec((tile, width), lambda i: (i, 0)),
    ]
    step = pl.BlockSpec((count, tile), lambda i: (0, i))
    return pl.pallas_call(
        term_kernel if far is None else sum_term_kernel,
        grid=(model // tile,),
        in_specs=specs + ([] if far is None else [step]),
        out_specs=step,
        out_shape=jax.ShapeDtypeStruct((count, model), BF),
        compiler_params=params(),
        cost_estimate=cost(2 * count * model * width, 2 * model * (width + 2 * count)),
        name="term" if far is None else "sum_term",
    )(d, w, *([] if far is None else [far]))


def shifted(block, distance):
    n = lax.axis_size("blk")
    return lax.ppermute(block, "blk", [(i, (i + distance) % n) for i in range(n)])


def z_shifted(block, distance):
    n = lax.axis_size("dp")
    route = [(i, i // N_Z * N_Z + (i + distance) % N_Z) for i in range(n)]
    return lax.ppermute(block, "dp", route)


def x_swapped(block):
    n = lax.axis_size("dp")
    return lax.ppermute(block, "dp", [(i, (i + N_Z) % n) for i in range(n)])


def z_reduced(parts):
    z = lax.axis_index("dp") % N_Z

    def at(distance):
        return lax.dynamic_index_in_dim(parts, (z + distance) % N_Z, 1, keepdims=False)

    across = at(4)
    up = z_shifted(across[0], 1)
    down = z_shifted(across[1], -1)
    third_up, third_down = at(3), at(-3)
    up = jnp.stack([third_up[0] + up, third_up[1]])
    down = jnp.stack([third_down[0], third_down[1] + down])
    up, down = z_shifted(up, 1), z_shifted(down, -1)
    up, down = z_shifted(at(2) + up, 1), z_shifted(at(-2) + down, -1)
    up, down = z_shifted(at(1) + up, 1), z_shifted(at(-1) + down, -1)
    return at(0).astype(F32) + up.astype(F32) + down.astype(F32)


def reduced_x_first(grad, x_hi):
    model, width = grad.shape
    halves = grad.reshape(2, model // 2, width)
    mine = lax.dynamic_index_in_dim(halves, x_hi, 0, keepdims=False)
    other = lax.dynamic_index_in_dim(halves, 1 - x_hi, 0, keepdims=False)
    mine = mine + x_swapped(other)
    rows = model // 2 // N_Z
    parts = mine.reshape(N_Z, 2, rows // 2, width).transpose(1, 0, 2, 3)
    return z_reduced(parts).reshape(rows, width).astype(BF)


def reduced_z_first(grad, x_hi):
    model, width = grad.shape
    rows = model // 2 // N_Z
    both = z_reduced(grad.reshape(2, N_Z, rows, width))
    mine = lax.dynamic_index_in_dim(both, x_hi, 0, keepdims=False)
    other = lax.dynamic_index_in_dim(both, 1 - x_hi, 0, keepdims=False)
    return (mine + x_swapped(other.astype(BF)).astype(F32)).astype(BF)


def local(normed_input, segment_ids, weights_qkv, weights_out, cotangent):
    x, wq, wo, g = normed_input[0], weights_qkv[0], weights_out[0], cotangent[0]
    n_blk = lax.axis_size("blk")
    here = lax.axis_index("blk")
    x_hi = lax.axis_index("dp") // N_Z
    head = wo.shape[0]
    seg = lax.dynamic_index_in_dim(segment_ids[0], here, 0, keepdims=False)
    seg_far = lax.dynamic_index_in_dim(segment_ids[0], (here + 1) % n_blk, 0, keepdims=False)

    x_far = shifted(x, -1)
    wo_back = shifted(wo, 1)
    qkv = jnp.dot(x, wq, preferred_element_type=F32).astype(BF)
    d_att = dot(g, wo, 1, 1).astype(BF)
    d_qkv, att = attention(qkv, d_att, seg)
    d_att_far = shifted(dot(g, wo_back, 1, 1).astype(BF), -1)
    g, x_far = lax.optimization_barrier((g, x_far))
    g_far = shifted(g, -1)

    qkv_far = jnp.dot(x_far, wq, preferred_element_type=F32).astype(BF)
    d_qkv_far, att_far = attention(qkv_far, d_att_far, seg_far)
    grad_qk, grad_v = grads(x, x_far, d_qkv, d_qkv_far, (2 * head, head), 1280, "grads_qkv")
    term_back = shifted(term(d_qkv_far, wq), 1)
    out_qk = reduced_x_first(grad_qk, x_hi)
    out_v = reduced_z_first(grad_v, x_hi)
    (grad_o,) = grads(g, g_far, att, att_far, (head,), 1280, "grads_out")
    out_o = reduced_z_first(grad_o, x_hi)
    input_grad = term(d_qkv, wq, term_back)
    return input_grad[None], jnp.concatenate([out_qk, out_v], axis=1)[None], out_o.T[None]


def solution(mesh):
    placed = (
        P(("blk", "dp"), None, None),
        P("dp", None, None),
        P("blk", None, None),
        P("blk", None, None),
        P(("blk", "dp"), None, None),
    )
    return jax.shard_map(
        local,
        mesh=mesh,
        in_specs=placed,
        out_specs=(P(("blk", "dp"), None, None), P("blk", "dp", None), P("blk", None, "dp")),
        check_vma=False,
    )
```

time: 584 us -> 169 us (0.29)
  the two profiles are of different devices: /device:TPU:28 before, /device:TPU:4 now
where the time goes in v1:
time: 169 us; the launch traced here: 168 us
  waiting for transfers between devices  78.6 us (47%)
  starting transfers between devices  42.9 us (25%)
  Pallas kernels  16.6 us (10%)
  matrix products  12.1 us (7%)
  other arithmetic  9.67 us (6%)
  local copies, waits for them, and re-layouts  7.51 us (4%)
    ppermute x24, starting transfers between devices, z_shifted(): return lax.ppermute(block, 'dp', route)  33.7 us
    ppermute x3, waiting for transfers between devices, x_swapped(): return lax.ppermute(block, 'dp', [(i, (i + N_Z) % n) for i in range(n)])  32.8 us
    ppermute x24, waiting for transfers between devices, z_shifted(): return lax.ppermute(block, 'dp', route)  27.3 us
    ppermute x5, waiting for transfers between devices, shifted(): lax.ppermute(block, 'blk', [(i, (i + distance) % n) for i in range(n)])  18.5 us
    pallas_call x2, Pallas kernels, grads(): pl.pallas_call(grads_kernel, grid=(model // tile,), in_specs=[step, step,...  9.09 us
    pallas_call x2, Pallas kernels, term(): pl.pallas_call(term_kernel if far is None else sum_term_kernel, grid=(mod...  5.66 us
    ppermute x5, starting transfers between devices, shifted(): lax.ppermute(block, 'blk', [(i, (i + distance) % n) for i in range(n)])  5.65 us
    dot_general x2, matrix products, dot(): lax.dot_general(a, b, (((ca,), (cb,)), ((), ())), preferred_element_type=...  5.25 us
  transfers between devices with their start and end apart: 32, of which 18 were waited for; matrix products, arithmetic and copies ran while one was open for 14% of the time, Pallas kernels for 6%

profile of v1, /device:TPU:4, one launch (start us, length us, event | category | flops | bytes accessed | tf_op | source)
XLA Modules:
  0.0 168.3 jit_solution(8301969673912437675)
XLA Ops:
  0.6 3.2 %collective-permute-start = (bf16[256,5120]{1,0:T(8,128)(2,1)}, bf16[256,5120]{1,0:T(8,128)(2,1)}, u32[]{:S(2)}, u32[]{:S(2)}) collective-permute-start(bf16[256,5120]{1,0:T(8,128)(2,1)} %bitcast.183), channel_id=1, source_target_pairs={{0,240},{16,0},{32,16},{48,32},{64,48},{80,64},{96,80},{112,96},{1... | collective-permute-start | bytes 7864328 | tf_op jit(solution)/shard_map/ppermute | solution.py:120
  3.8 0.8 fusion.23
  4.9 3.1 %convolution_convert_fusion.3.datt_ref = bf16[256,128]{1,0:T(8,128)(2,1)S(1)} fusion(bf16[1,128,5120]{2,1,0:T(8,128)(2,1)} %param.8, bf16[1,256,5120]{2,1,0:T(8,128)(2,1)} %param.9), kind=kOutput, calls=%fused_computation.5 | convolution fusion | flops 335577088 | bytes 3997696 | tf_op jit(solution)/shard_map/dot_general | solution.py:14
  8.0 0.2 copy-done.1
  8.2 3.4 %convolution_convert_fusion.1.qkv_ref = bf16[256,384]{1,0:T(8,128)(2,1)S(1)} fusion(bf16[1,5120,384]{2,1,0:T(8,128)(2,1)S(1)} %copy-done.1, bf16[1,256,5120]{2,1,0:T(8,128)(2,1)} %param.5), kind=kOutput, calls=%fused_computation.3 | convolution fusion | flops 1006731264 | bytes 6750208 | tf_op jit(solution)/shard_map/dot_general | solution.py:183
  11.6 0.9 attention.2
  12.5 10.7 %collective-permute-done.1 = bf16[128,5120]{1,0:T(8,128)(2,1)} collective-permute-done((bf16[128,5120]{1,0:T(8,128)(2,1)}, bf16[128,5120]{1,0:T(8,128)(2,1)}, u32[]{:S(2)}, u32[]{:S(2)}) %collective-permute-start.1) | collective-permute-done | bytes 1310752 | tf_op jit(solution)/shard_map/ppermute | solution.py:120
  23.3 2.2 %convolution_convert_fusion.2 = bf16[256,128]{1,0:T(8,128)(2,1)S(1)} fusion(bf16[128,5120]{1,0:T(8,128)(2,1)} %collective-permute-done.1, bf16[1,256,5120]{2,1,0:T(8,128)(2,1)S(1)} %copy-done), kind=kOutput, calls=%fused_computation.4 | convolution fusion | flops 335577088 | bytes 3997696 | tf_op jit(solution)/shard_map/dot_general | solution.py:14
  25.5 7.8 %collective-permute-done.xf_ref = bf16[256,5120]{1,0:T(8,128)(2,1)} collective-permute-done((bf16[256,5120]{1,0:T(8,128)(2,1)}, bf16[256,5120]{1,0:T(8,128)(2,1)}, u32[]{:S(2)}, u32[]{:S(2)}) %collective-permute-start) | collective-permute-done | bytes 2621472 | tf_op jit(solution)/shard_map/ppermute | solution.py:120
  33.3 3.4 %convolution_convert_fusion.qkv_ref = bf16[256,384]{1,0:T(8,128)(2,1)S(1)} fusion(bf16[256,5120]{1,0:T(8,128)(2,1)} %collective-permute-done.xf_ref, bf16[1,5120,384]{2,1,0:T(8,128)(2,1)S(1)} %copy-done.1), kind=kOutput, calls=%fused_computation.2 | convolution fusion | flops 1006731264 | bytes 6750208 | tf_op jit(solution)/shard_map/dot_general | solution.py:190
  36.7 0.9 attention.3
  37.7 5.0 %grads_qkv.1 = (bf16[5120,256]{1,0:T(8,128)(2,1)S(1)}, bf16[5120,128]{1,0:T(8,128)(2,1)S(1)}) custom-call(bf16[256,5120]{1,0:T(8,128)(2,1)S(1)} %bitcast.184, bf16[256,5120]{1,0:T(8,128)(2,1)} %collective-permute-done.xf_ref, bf16[256,384]{1,0:T(8,128)(2,1)S(1)} %get-tuple-element.11.d_ref, bf16[256,384]{1,0:T(8,128)(2,1)S(1)} %get-tuple-element.13.d_ref.df_ref), custom_call_target="tpu_custom_call" | custom-call | flops 2013265920 | bytes 9175040 | tf_op jit(solution)/shard_map/grads_qkv/pallas_call | solution.py:78
  42.7 1.5 copy-done.4
  44.2 2.0 %collective-permute-start.13 = (bf16[320,128]{1,0:T(8,128)(2,1)S(1)}, bf16[320,128]{1,0:T(8,128)(2,1)S(1)}, u32[]{:S(2)}, u32[]{:S(2)}) collective-permute-start(bf16[320,128]{1,0:T(8,128)(2,1)S(1)} %get-tuple-element.39), channel_id=1, source_target_pairs={{0,1},{1,2},{2,3},{3,4},{4,5},{5,6},{6,7},{7,0},{8,9},{9,10},{10,1... | collective-permute-start | bytes 245768 | tf_op jit(solution)/shard_map/ppermute | solution.py:126
  46.2 4.0 %collective-permute-start.17 = (bf16[320,128]{1,0:T(8,128)(2,1)S(1)}, bf16[320,128]{1,0:T(8,128)(2,1)S(1)}, u32[]{:S(2)}, u32[]{:S(2)}) collective-permute-start(bf16[320,128]{1,0:T(8,128)(2,1)S(1)} %get-tuple-element.41), channel_id=1, source_target_pairs={{0,7},{1,0},{2,1},{3,2},{4,3},{5,4},{6,5},{7,6},{8,15},{9,8},{10,9... | collective-permute-start | bytes 245768 | tf_op jit(solution)/shard_map/ppermute | solution.py:126
  50.2 2.3 %collective-permute-done.13 = bf16[320,128]{1,0:T(8,128)(2,1)S(1)} collective-permute-done((bf16[320,128]{1,0:T(8,128)(2,1)S(1)}, bf16[320,128]{1,0:T(8,128)(2,1)S(1)}, u32[]{:S(2)}, u32[]{:S(2)}) %collective-permute-start.13) | collective-permute-done | bytes 81952 | tf_op jit(solution)/shard_map/ppermute | solution.py:126
  52.6 0.7 pad_maximum_fusion.2
  53.3 3.4 %collective-permute-start.18 = (bf16[2,320,128]{2,1,0:T(8,128)(2,1)S(1)}, bf16[2,320,128]{2,1,0:T(8,128)(2,1)}, u32[]{:S(2)}, u32[]{:S(2)}) collective-permute-start(bf16[2,320,128]{2,1,0:T(8,128)(2,1)S(1)} %pad_maximum_fusion.3), channel_id=1, source_target_pairs={{0,7},{1,0},{2,1},{3,2},{4,3},{5,4},{6,5},{7,6},{8,15},{9,8},{10,9... | collective-permute-start | bytes 491528 | tf_op jit(solution)/shard_map/ppermute | solution.py:126
  56.7 3.5 %collective-permute-done.14 = bf16[2,320,128]{2,1,0:T(8,128)(2,1)} collective-permute-done((bf16[2,320,128]{2,1,0:T(8,128)(2,1)}, bf16[2,320,128]{2,1,0:T(8,128)(2,1)}, u32[]{:S(2)}, u32[]{:S(2)}) %collective-permute-start.14) | collective-permute-done | bytes 163872 | tf_op jit(solution)/shard_map/ppermute | solution.py:126
  60.2 1.7 bitcast_add_fusion.9
  61.9 2.5 %dynamic-slice_bitcast_fusion = bf16[2560,256]{1,0:T(8,128)(2,1)} fusion(bf16[2,2560,256]{2,1,0:T(8,128)(2,1)} %bitcast.175, s32[]{:T(128)S(6)} %select_n.149), kind=kLoop, calls=%fused_computation.1 | loop fusion | bytes 2621444 | tf_op jit(solution)/shard_map/jit(dynamic_index_in_dim)/squeeze | solution.py:156
  64.4 0.8 collective-permute-start.4
  65.2 2.3 %collective-permute-start.22 = (bf16[256,5120]{1,0:T(8,128)(2,1)S(1)}, bf16[256,5120]{1,0:T(8,128)(2,1)}, u32[]{:S(2)}, u32[]{:S(2)}) collective-permute-start(bf16[256,5120]{1,0:T(8,128)(2,1)S(1)} %bitcast.165), channel_id=1, source_target_pairs={{0,240},{16,0},{32,16},{48,32},{64,48},{80,64},{96,80},{112,96},{1... | collective-permute-start | bytes 7864328 | tf_op jit(solution)/shard_map/ppermute | solution.py:120
  67.5 1.2 collective-permute-done.15
  68.7 1.9 %bitcast_add_fusion.10 = (bf16[2,320,128]{2,1,0:T(8,128)(2,1)}, bf16[2,320,128]{2,1,0:T(8,128)(2,1)S(1)}) fusion(bf16[2,320,128]{2,1,0:T(8,128)(2,1)} %collective-permute-done.15, bf16[2,8,320,128]{3,2,1,0:T(8,128)(2,1)} %bitcast.180, s32[]{:T(128)S(6)} %select_n.154, bf16[2,320,128]{2,1,0:T(8,128)(2,1)} %collective-permute-done.18, s32[]{:T(128)S(6)} %select_n.164), kind=kLoop, calls=%fused_computation.31 | loop fusion | flops 163840 | bytes 983048 | tf_op jit(solution)/shard_map/add | solution.py:148
  70.6 1.8 %collective-permute-start.19 = (bf16[2,320,128]{2,1,0:T(8,128)(2,1)S(1)}, bf16[2,320,128]{2,1,0:T(8,128)(2,1)}, u32[]{:S(2)}, u32[]{:S(2)}) collective-permute-start(bf16[2,320,128]{2,1,0:T(8,128)(2,1)S(1)} %get-tuple-element.36), channel_id=1, source_target_pairs={{0,7},{1,0},{2,1},{3,2},{4,3},{5,4},{6,5},{7,6},{8,15},{9,8},{10,9... | collective-permute-start | bytes 491528 | tf_op jit(solution)/shard_map/ppermute | solution.py:126
  72.3 0.3 collective-permute-start.16
  72.6 3.4 %collective-permute-done.19 = bf16[2,320,128]{2,1,0:T(8,128)(2,1)} collective-permute-done((bf16[2,320,128]{2,1,0:T(8,128)(2,1)S(1)}, bf16[2,320,128]{2,1,0:T(8,128)(2,1)}, u32[]{:S(2)}, u32[]{:S(2)}) %collective-permute-start.19) | collective-permute-done | bytes 163872 | tf_op jit(solution)/shard_map/ppermute | solution.py:126
  76.0 1.0 bitcast_add_fusion.8
  77.0 3.0 %collective-permute-start.20 = (bf16[2,320,128]{2,1,0:T(8,128)(2,1)S(1)}, bf16[2,320,128]{2,1,0:T(8,128)(2,1)}, u32[]{:S(2)}, u32[]{:S(2)}) collective-permute-start(bf16[2,320,128]{2,1,0:T(8,128)(2,1)S(1)} %bitcast_add_fusion.8), channel_id=1, source_target_pairs={{0,7},{1,0},{2,1},{3,2},{4,3},{5,4},{6,5},{7,6},{8,15},{9,8},{10,9... | collective-permute-start | bytes 491528 | tf_op jit(solution)/shard_map/ppermute | solution.py:126
  80.1 2.1 %copy-done.2 = bf16[1,5120,384]{2,1,0:T(8,128)(2,1)S(1)} copy-done((bf16[1,5120,384]{2,1,0:T(8,128)(2,1)S(1)}, bf16[1,5120,384]{2,1,0:T(8,128)(2,1)}, u32[]{:S(2)}) %copy-start.2) | copy-done | bytes 3932184
  82.2 2.2 %term.1 = bf16[256,5120]{1,0:T(8,128)(2,1)S(1)} custom-call(bf16[256,384]{1,0:T(8,128)(2,1)S(1)} %get-tuple-element.13.d_ref.df_ref, bf16[5120,384]{1,0:T(8,128)(2,1)S(1)} %bitcast.167), custom_call_target="tpu_custom_call" | custom-call | flops 1006632960 | bytes 9175040 | tf_op jit(solution)/shard_map/term/pallas_call | solution.py:106
  84.5 1.1 fusion.1
  85.7 2.1 %collective-permute-start.21 = (bf16[320,128]{1,0:T(8,128)(2,1)S(1)}, bf16[320,128]{1,0:T(8,128)(2,1)S(1)}, u32[]{:S(2)}, u32[]{:S(2)}) collective-permute-start(bf16[320,128]{1,0:T(8,128)(2,1)S(1)} %fusion.6), channel_id=1, source_target_pairs={{0,8},{1,9},{2,10},{3,11},{4,12},{5,13},{6,14},{7,15},{8,0},{9,1},... | collective-permute-start | bytes 245768 | tf_op jit(solution)/shard_map/ppermute | solution.py:131
  87.8 6.8 %collective-permute-done.4 = bf16[2560,256]{1,0:T(8,128)(2,1)} collective-permute-done((bf16[2560,256]{1,0:T(8,128)(2,1)}, bf16[2560,256]{1,0:T(8,128)(2,1)}, u32[]{:S(2)}, u32[]{:S(2)}) %collective-permute-start.4) | collective-permute-done | bytes 1310752 | tf_op jit(solution)/shard_map/ppermute | solution.py:131
  94.6 1.4 bitcast_add_fusion
  96.0 2.0 %collective-permute-start.5 = (bf16[160,256]{1,0:T(8,128)(2,1)S(1)}, bf16[160,256]{1,0:T(8,128)(2,1)S(1)}, u32[]{:S(2)}, u32[]{:S(2)}) collective-permute-start(bf16[160,256]{1,0:T(8,128)(2,1)S(1)} %get-tuple-element.31), channel_id=1, source_target_pairs={{0,1},{1,2},{2,3},{3,4},{4,5},{5,6},{6,7},{7,0},{8,9},{9,10},{10,1... | collective-permute-start | bytes 245768 | tf_op jit(solution)/shard_map/ppermute | solution.py:126
  98.1 1.3 collective-permute-start.9
  99.4 24.0 %collective-permute-done.21 = bf16[320,128]{1,0:T(8,128)(2,1)S(1)} collective-permute-done((bf16[320,128]{1,0:T(8,128)(2,1)S(1)}, bf16[320,128]{1,0:T(8,128)(2,1)S(1)}, u32[]{:S(2)}, u32[]{:S(2)}) %collective-permute-start.21) | collective-permute-done | bytes 81952 | tf_op jit(solution)/shard_map/ppermute | solution.py:131
  123.5 3.0 %collective-permute-start.10 = (bf16[2,160,256]{2,1,0:T(8,128)(2,1)S(1)}, bf16[2,160,256]{2,1,0:T(8,128)(2,1)S(1)}, u32[]{:S(2)}, u32[]{:S(2)}) collective-permute-start(bf16[2,160,256]{2,1,0:T(8,128)(2,1)S(1)} %pad_maximum_fusion.1), channel_id=1, source_target_pairs={{0,7},{1,0},{2,1},{3,2},{4,3},{5,4},{6,5},{7,6},{8,15},{9,8},{10,9... | collective-permute-start | bytes 491528 | tf_op jit(solution)/shard_map/ppermute | solution.py:126
  126.6 4.1 %grads_out.1 = bf16[5120,128]{1,0:T(8,128)(2,1)S(1)} custom-call(bf16[256,5120]{1,0:T(8,128)(2,1)S(1)} %bitcast.166, bf16[256,5120]{1,0:T(8,128)(2,1)} %collective-permute-done.22.xf_ref, bf16[256,128]{1,0:T(8,128)(2,1)S(1)} %get-tuple-element.17.d_ref, bf16[256,128]{1,0:T(8,128)(2,1)S(1)} %get-tuple-element.18.df_ref), custom_call_target="tpu_custom_call" | custom-call | flops 671088640 | bytes 6553600 | tf_op jit(solution)/shard_map/grads_out/pallas_call | solution.py:78
  130.8 3.2 %collective-permute-start.27 = (bf16[320,128]{1,0:T(8,128)(2,1)S(1)}, bf16[320,128]{1,0:T(8,128)(2,1)S(1)}, u32[]{:S(2)}, u32[]{:S(2)}) collective-permute-start(bf16[320,128]{1,0:T(8,128)(2,1)S(1)} %get-tuple-element.25), channel_id=1, source_target_pairs={{0,7},{1,0},{2,1},{3,2},{4,3},{5,4},{6,5},{7,6},{8,15},{9,8},{10,9... | collective-permute-start | bytes 245768 | tf_op jit(solution)/shard_map/ppermute | solution.py:126
  134.1 2.3 %collective-permute-done.23 = bf16[320,128]{1,0:T(8,128)(2,1)S(1)} collective-permute-done((bf16[320,128]{1,0:T(8,128)(2,1)S(1)}, bf16[320,128]{1,0:T(8,128)(2,1)S(1)}, u32[]{:S(2)}, u32[]{:S(2)}) %collective-permute-start.23) | collective-permute-done | bytes 81952 | tf_op jit(solution)/shard_map/ppermute | solution.py:126
  136.5 0.3 collective-permute-start.24
  136.8 3.8 %collective-permute-done.6 = bf16[2,160,256]{2,1,0:T(8,128)(2,1)S(1)} collective-permute-done((bf16[2,160,256]{2,1,0:T(8,128)(2,1)S(1)}, bf16[2,160,256]{2,1,0:T(8,128)(2,1)S(1)}, u32[]{:S(2)}, u32[]{:S(2)}) %collective-permute-start.6) | collective-permute-done | bytes 163872 | tf_op jit(solution)/shard_map/ppermute | solution.py:126
  140.8 3.3 %collective-permute-start.28 = (bf16[2,320,128]{2,1,0:T(8,128)(2,1)S(1)}, bf16[2,320,128]{2,1,0:T(8,128)(2,1)S(1)}, u32[]{:S(2)}, u32[]{:S(2)}) collective-permute-start(bf16[2,320,128]{2,1,0:T(8,128)(2,1)S(1)} %pad_maximum_fusion.5), channel_id=1, source_target_pairs={{0,7},{1,0},{2,1},{3,2},{4,3},{5,4},{6,5},{7,6},{8,15},{9,8},{10,9... | collective-permute-start | bytes 491528 | tf_op jit(solution)/shard_map/ppermute | solution.py:126
  144.2 3.1 %collective-permute-done.7 = bf16[2,160,256]{2,1,0:T(8,128)(2,1)S(1)} collective-permute-done((bf16[2,160,256]{2,1,0:T(8,128)(2,1)S(1)}, bf16[2,160,256]{2,1,0:T(8,128)(2,1)S(1)}, u32[]{:S(2)}, u32[]{:S(2)}) %collective-permute-start.7) | collective-permute-done | bytes 163872 | tf_op jit(solution)/shard_map/ppermute | solution.py:126
  147.3 0.2 collective-permute-start.11
  147.5 1.9 %collective-permute-start.8 = (bf16[2,160,256]{2,1,0:T(8,128)(2,1)S(1)}, bf16[2,160,256]{2,1,0:T(8,128)(2,1)S(1)}, u32[]{:S(2)}, u32[]{:S(2)}) collective-permute-start(bf16[2,160,256]{2,1,0:T(8,128)(2,1)S(1)} %get-tuple-element.27), channel_id=1, source_target_pairs={{0,1},{1,2},{2,3},{3,4},{4,5},{5,6},{6,7},{7,0},{8,9},{9,10},{10,1... | collective-permute-start | bytes 491528 | tf_op jit(solution)/shard_map/ppermute | solution.py:126
  149.4 1.3 collective-permute-done.25
  150.7 0.2 collective-permute-start.29
  150.9 1.8 %collective-permute-done.11 = bf16[2,160,256]{2,1,0:T(8,128)(2,1)S(1)} collective-permute-done((bf16[2,160,256]{2,1,0:T(8,128)(2,1)S(1)}, bf16[2,160,256]{2,1,0:T(8,128)(2,1)S(1)}, u32[]{:S(2)}, u32[]{:S(2)}) %collective-permute-start.11) | collective-permute-done | bytes 163872 | tf_op jit(solution)/shard_map/ppermute | solution.py:126
  152.7 1.4 collective-permute-start.12
  154.1 0.7 collective-permute-start.26
  154.8 1.3 collective-permute-done.29
  156.2 1.4 collective-permute-start.30
  157.5 0.6 collective-permute-done.12
  158.2 0.7 maximum_bitcast_fusion
  158.9 1.8 %collective-permute-done.26 = bf16[2,320,128]{2,1,0:T(8,128)(2,1)S(1)} collective-permute-done((bf16[2,320,128]{2,1,0:T(8,128)(2,1)S(1)}, bf16[2,320,128]{2,1,0:T(8,128)(2,1)S(1)}, u32[]{:S(2)}, u32[]{:S(2)}) %collective-permute-start.26) | collective-permute-done | bytes 163872 | tf_op jit(solution)/shard_map/ppermute | solution.py:126
  160.7 0.9 collective-permute-done.30
  161.6 0.6 collective-permute-start.31
  162.2 3.4 %sum_term.1 = bf16[256,5120]{1,0:T(8,128)(2,1)} custom-call(bf16[256,384]{1,0:T(8,128)(2,1)S(1)} %get-tuple-element.11.d_ref, bf16[5120,384]{1,0:T(8,128)(2,1)S(1)} %bitcast.168, bf16[256,5120]{1,0:T(8,128)(2,1)S(1)} %collective-permute-done.3.far_ref), custom_call_target="tpu_custom_call" | custom-call | flops 1006632960 | bytes 9175040 | tf_op jit(solution)/shard_map/sum_term/pallas_call | solution.py:106
  165.7 2.0 %collective-permute-done.31 = bf16[320,128]{1,0:T(8,128)(2,1)S(1)} collective-permute-done((bf16[320,128]{1,0:T(8,128)(2,1)S(1)}, bf16[320,128]{1,0:T(8,128)(2,1)S(1)}, u32[]{:S(2)}, u32[]{:S(2)}) %collective-permute-start.31) | collective-permute-done | bytes 81952 | tf_op jit(solution)/shard_map/ppermute | solution.py:131
  167.7 0.7 fusion.8
  (60 shorter events, 1.5 us)
Async XLA Ops:
  0.6 32.7 %collective-permute-start = (bf16[256,5120]{1,0:T(8,128)(2,1)}, bf16[256,5120]{1,0:T(8,128)(2,1)}, u32[]{:S(2)}, u32[]{:S(2)}) collective-permute-start(bf16[256,5120]{1,0:T(8,128)(2,1)} %bitcast.183), channel_id=1, source_target_pairs={{0,240},{16,0},{32,16},{48,32},{64,48},{80,64},{96,80},{112,96},{1... | collective-permute-start | bytes 7864328 | tf_op jit(solution)/shard_map/ppermute | solution.py:120
  3.8 19.5 %collective-permute-start.1 = (bf16[128,5120]{1,0:T(8,128)(2,1)}, bf16[128,5120]{1,0:T(8,128)(2,1)}, u32[]{:S(2)}, u32[]{:S(2)}) collective-permute-start(bf16[128,5120]{1,0:T(8,128)(2,1)} %bitcast.192), channel_id=1, source_target_pairs={{0,16},{16,32},{32,48},{48,64},{64,80},{80,96},{96,112},{112,128},... | collective-permute-start | bytes 3932168 | tf_op jit(solution)/shard_map/ppermute | solution.py:120
  4.9 3.3 %copy-start.1 = (bf16[1,5120,384]{2,1,0:T(8,128)(2,1)S(1)}, bf16[1,5120,384]{2,1,0:T(8,128)(2,1)}, u32[]{:S(2)}) copy-start(bf16[1,5120,384]{2,1,0:T(8,128)(2,1)} %param.7) | copy-start | bytes 11796484
  8.2 15.1 %copy-start = (bf16[1,256,5120]{2,1,0:T(8,128)(2,1)S(1)}, bf16[1,256,5120]{2,1,0:T(8,128)(2,1)}, u32[]{:S(2)}) copy-start(bf16[1,256,5120]{2,1,0:T(8,128)(2,1)} %param.9) | copy-start | bytes 7864324
  25.4 11.3 %collective-permute-start.2 = (bf16[256,128]{1,0:T(8,128)(2,1)S(1)}, bf16[256,128]{1,0:T(8,128)(2,1)S(1)}, u32[]{:S(2)}, u32[]{:S(2)}) collective-permute-start(bf16[256,128]{1,0:T(8,128)(2,1)S(1)} %convolution_convert_fusion.2), channel_id=1, source_target_pairs={{0,240},{16,0},{32,16},{48,32},{64,48},{80,64},{96,80},{112,96},{1... | collective-permute-start | bytes 196616 | tf_op jit(solution)/shard_map/ppermute | solution.py:120
  33.3 4.4 %copy-start.7 = (bf16[1,256,5120]{2,1,0:T(8,128)(2,1)S(1)}, bf16[1,256,5120]{2,1,0:T(8,128)(2,1)}, u32[]{:S(2)}) copy-start(bf16[1,256,5120]{2,1,0:T(8,128)(2,1)} %param.5) | copy-start | bytes 7864324
  42.7 1.5 copy-start.4
  44.2 8.4 %copy-start.6 = (bf16[5120,128]{1,0:T(8,128)(2,1)}, bf16[5120,128]{1,0:T(8,128)(2,1)S(1)}, u32[]{:S(2)}) copy-start(bf16[5120,128]{1,0:T(8,128)(2,1)S(1)} %get-tuple-element.15) | copy-start | bytes 3932164
  44.2 8.4 %collective-permute-start.13 = (bf16[320,128]{1,0:T(8,128)(2,1)S(1)}, bf16[320,128]{1,0:T(8,128)(2,1)S(1)}, u32[]{:S(2)}, u32[]{:S(2)}) collective-permute-start(bf16[320,128]{1,0:T(8,128)(2,1)S(1)} %get-tuple-element.39), channel_id=1, source_target_pairs={{0,1},{1,2},{2,3},{3,4},{4,5},{5,6},{6,7},{7,0},{8,9},{9,10},{10,1... | collective-permute-start | bytes 245768 | tf_op jit(solution)/shard_map/ppermute | solution.py:126
  46.2 6.4 %collective-permute-start.17 = (bf16[320,128]{1,0:T(8,128)(2,1)S(1)}, bf16[320,128]{1,0:T(8,128)(2,1)S(1)}, u32[]{:S(2)}, u32[]{:S(2)}) collective-permute-start(bf16[320,128]{1,0:T(8,128)(2,1)S(1)} %get-tuple-element.41), channel_id=1, source_target_pairs={{0,7},{1,0},{2,1},{3,2},{4,3},{5,4},{6,5},{7,6},{8,15},{9,8},{10,9... | collective-permute-start | bytes 245768 | tf_op jit(solution)/shard_map/ppermute | solution.py:126
  53.3 6.9 %collective-permute-start.14 = (bf16[2,320,128]{2,1,0:T(8,128)(2,1)}, bf16[2,320,128]{2,1,0:T(8,128)(2,1)}, u32[]{:S(2)}, u32[]{:S(2)}) collective-permute-start(bf16[2,320,128]{2,1,0:T(8,128)(2,1)} %pad_maximum_fusion.2), channel_id=1, source_target_pairs={{0,1},{1,2},{2,3},{3,4},{4,5},{5,6},{6,7},{7,0},{8,9},{9,10},{10,1... | collective-permute-start | bytes 491528 | tf_op jit(solution)/shard_map/ppermute | solution.py:126
  53.3 14.2 %collective-permute-start.18 = (bf16[2,320,128]{2,1,0:T(8,128)(2,1)S(1)}, bf16[2,320,128]{2,1,0:T(8,128)(2,1)}, u32[]{:S(2)}, u32[]{:S(2)}) collective-permute-start(bf16[2,320,128]{2,1,0:T(8,128)(2,1)S(1)} %pad_maximum_fusion.3), channel_id=1, source_target_pairs={{0,7},{1,0},{2,1},{3,2},{4,3},{5,4},{6,5},{7,6},{8,15},{9,8},{10,9... | collective-permute-start | bytes 491528 | tf_op jit(solution)/shard_map/ppermute | solution.py:126
  61.9 6.8 %collective-permute-start.15 = (bf16[2,320,128]{2,1,0:T(8,128)(2,1)}, bf16[2,320,128]{2,1,0:T(8,128)(2,1)}, u32[]{:S(2)}, u32[]{:S(2)}) collective-permute-start(bf16[2,320,128]{2,1,0:T(8,128)(2,1)} %bitcast_add_fusion.9), channel_id=1, source_target_pairs={{0,1},{1,2},{2,3},{3,4},{4,5},{5,6},{6,7},{7,0},{8,9},{9,10},{10,1... | collective-permute-start | bytes 491528 | tf_op jit(solution)/shard_map/ppermute | solution.py:126
  64.4 30.1 %collective-permute-start.4 = (bf16[2560,256]{1,0:T(8,128)(2,1)}, bf16[2560,256]{1,0:T(8,128)(2,1)}, u32[]{:S(2)}, u32[]{:S(2)}) collective-permute-start(bf16[2560,256]{1,0:T(8,128)(2,1)} %dynamic-slice_bitcast_fusion), channel_id=1, source_target_pairs={{0,8},{1,9},{2,10},{3,11},{4,12},{5,13},{6,14},{7,15},{8,0},{9,1},... | collective-permute-start | bytes 3932168 | tf_op jit(solution)/shard_map/ppermute | solution.py:131
  65.2 61.3 %collective-permute-start.22 = (bf16[256,5120]{1,0:T(8,128)(2,1)S(1)}, bf16[256,5120]{1,0:T(8,128)(2,1)}, u32[]{:S(2)}, u32[]{:S(2)}) collective-permute-start(bf16[256,5120]{1,0:T(8,128)(2,1)S(1)} %bitcast.165), channel_id=1, source_target_pairs={{0,240},{16,0},{32,16},{48,32},{64,48},{80,64},{96,80},{112,96},{1... | collective-permute-start | bytes 7864328 | tf_op jit(solution)/shard_map/ppermute | solution.py:120
  70.6 5.4 %collective-permute-start.19 = (bf16[2,320,128]{2,1,0:T(8,128)(2,1)S(1)}, bf16[2,320,128]{2,1,0:T(8,128)(2,1)}, u32[]{:S(2)}, u32[]{:S(2)}) collective-permute-start(bf16[2,320,128]{2,1,0:T(8,128)(2,1)S(1)} %get-tuple-element.36), channel_id=1, source_target_pairs={{0,7},{1,0},{2,1},{3,2},{4,3},{5,4},{6,5},{7,6},{8,15},{9,8},{10,9... | collective-permute-start | bytes 491528 | tf_op jit(solution)/shard_map/ppermute | solution.py:126
  72.3 12.2 %collective-permute-start.16 = (bf16[2,320,128]{2,1,0:T(8,128)(2,1)}, bf16[2,320,128]{2,1,0:T(8,128)(2,1)}, u32[]{:S(2)}, u32[]{:S(2)}) collective-permute-start(bf16[2,320,128]{2,1,0:T(8,128)(2,1)} %get-tuple-element.35), channel_id=1, source_target_pairs={{0,1},{1,2},{2,3},{3,4},{4,5},{5,6},{6,7},{7,0},{8,9},{9,10},{10,1... | collective-permute-start | bytes 491528 | tf_op jit(solution)/shard_map/ppermute | solution.py:126
  77.0 7.5 %collective-permute-start.20 = (bf16[2,320,128]{2,1,0:T(8,128)(2,1)S(1)}, bf16[2,320,128]{2,1,0:T(8,128)(2,1)}, u32[]{:S(2)}, u32[]{:S(2)}) collective-permute-start(bf16[2,320,128]{2,1,0:T(8,128)(2,1)S(1)} %bitcast_add_fusion.8), channel_id=1, source_target_pairs={{0,7},{1,0},{2,1},{3,2},{4,3},{5,4},{6,5},{7,6},{8,15},{9,8},{10,9... | collective-permute-start | bytes 491528 | tf_op jit(solution)/shard_map/ppermute | solution.py:126
  80.1 2.1 %copy-start.2 = (bf16[1,5120,384]{2,1,0:T(8,128)(2,1)S(1)}, bf16[1,5120,384]{2,1,0:T(8,128)(2,1)}, u32[]{:S(2)}) copy-start(bf16[1,5120,384]{2,1,0:T(8,128)(2,1)} %param.7) | copy-start | bytes 11796484
  82.2 12.4 %copy-start.5 = (bf16[5120,256]{1,0:T(8,128)(2,1)S(1)}, bf16[5120,256]{1,0:T(8,128)(2,1)}, u32[]{:S(2)}) copy-start(bf16[5120,256]{1,0:T(8,128)(2,1)} %copy-done.4) | copy-start | bytes 7864324
  84.4 77.8 %collective-permute-start.3 = (bf16[256,5120]{1,0:T(8,128)(2,1)S(1)}, bf16[256,5120]{1,0:T(8,128)(2,1)S(1)}, u32[]{:S(2)}, u32[]{:S(2)}) collective-permute-start(bf16[256,5120]{1,0:T(8,128)(2,1)S(1)} %term.1), channel_id=1, source_target_pairs={{0,16},{16,32},{32,48},{48,64},{64,80},{80,96},{96,112},{112,128},... | collective-permute-start | bytes 7864328 | tf_op jit(solution)/shard_map/ppermute | solution.py:120
  85.7 37.7 %collective-permute-start.21 = (bf16[320,128]{1,0:T(8,128)(2,1)S(1)}, bf16[320,128]{1,0:T(8,128)(2,1)S(1)}, u32[]{:S(2)}, u32[]{:S(2)}) collective-permute-start(bf16[320,128]{1,0:T(8,128)(2,1)S(1)} %fusion.6), channel_id=1, source_target_pairs={{0,8},{1,9},{2,10},{3,11},{4,12},{5,13},{6,14},{7,15},{8,0},{9,1},... | collective-permute-start | bytes 245768 | tf_op jit(solution)/shard_map/ppermute | solution.py:131
  96.0 27.4 %collective-permute-start.5 = (bf16[160,256]{1,0:T(8,128)(2,1)S(1)}, bf16[160,256]{1,0:T(8,128)(2,1)S(1)}, u32[]{:S(2)}, u32[]{:S(2)}) collective-permute-start(bf16[160,256]{1,0:T(8,128)(2,1)S(1)} %get-tuple-element.31), channel_id=1, source_target_pairs={{0,1},{1,2},{2,3},{3,4},{4,5},{5,6},{6,7},{7,0},{8,9},{9,10},{10,1... | collective-permute-start | bytes 245768 | tf_op jit(solution)/shard_map/ppermute | solution.py:126
  98.1 25.4 %collective-permute-start.9 = (bf16[160,256]{1,0:T(8,128)(2,1)S(1)}, bf16[160,256]{1,0:T(8,128)(2,1)S(1)}, u32[]{:S(2)}, u32[]{:S(2)}) collective-permute-start(bf16[160,256]{1,0:T(8,128)(2,1)S(1)} %get-tuple-element.33), channel_id=1, source_target_pairs={{0,7},{1,0},{2,1},{3,2},{4,3},{5,4},{6,5},{7,6},{8,15},{9,8},{10,9... | collective-permute-start | bytes 245768 | tf_op jit(solution)/shard_map/ppermute | solution.py:126
  123.5 20.6 %collective-permute-start.10 = (bf16[2,160,256]{2,1,0:T(8,128)(2,1)S(1)}, bf16[2,160,256]{2,1,0:T(8,128)(2,1)S(1)}, u32[]{:S(2)}, u32[]{:S(2)}) collective-permute-start(bf16[2,160,256]{2,1,0:T(8,128)(2,1)S(1)} %pad_maximum_fusion.1), channel_id=1, source_target_pairs={{0,7},{1,0},{2,1},{3,2},{4,3},{5,4},{6,5},{7,6},{8,15},{9,8},{10,9... | collective-permute-start | bytes 491528 | tf_op jit(solution)/shard_map/ppermute | solution.py:126
  130.7 5.7 %collective-permute-start.23 = (bf16[320,128]{1,0:T(8,128)(2,1)S(1)}, bf16[320,128]{1,0:T(8,128)(2,1)S(1)}, u32[]{:S(2)}, u32[]{:S(2)}) collective-permute-start(bf16[320,128]{1,0:T(8,128)(2,1)S(1)} %get-tuple-element.23), channel_id=1, source_target_pairs={{0,1},{1,2},{2,3},{3,4},{4,5},{5,6},{6,7},{7,0},{8,9},{9,10},{10,1... | collective-permute-start | bytes 245768 | tf_op jit(solution)/shard_map/ppermute | solution.py:126
  130.8 5.6 %collective-permute-start.27 = (bf16[320,128]{1,0:T(8,128)(2,1)S(1)}, bf16[320,128]{1,0:T(8,128)(2,1)S(1)}, u32[]{:S(2)}, u32[]{:S(2)}) collective-permute-start(bf16[320,128]{1,0:T(8,128)(2,1)S(1)} %get-tuple-element.25), channel_id=1, source_target_pairs={{0,7},{1,0},{2,1},{3,2},{4,3},{5,4},{6,5},{7,6},{8,15},{9,8},{10,9... | collective-permute-start | bytes 245768 | tf_op jit(solution)/shard_map/ppermute | solution.py:126
  134.0 6.6 %collective-permute-start.6 = (bf16[2,160,256]{2,1,0:T(8,128)(2,1)S(1)}, bf16[2,160,256]{2,1,0:T(8,128)(2,1)S(1)}, u32[]{:S(2)}, u32[]{:S(2)}) collective-permute-start(bf16[2,160,256]{2,1,0:T(8,128)(2,1)S(1)} %pad_maximum_fusion), channel_id=1, source_target_pairs={{0,1},{1,2},{2,3},{3,4},{4,5},{5,6},{6,7},{7,0},{8,9},{9,10},{10,1... | collective-permute-start | bytes 491528 | tf_op jit(solution)/shard_map/ppermute | solution.py:126
  136.5 7.6 %collective-permute-start.24 = (bf16[2,320,128]{2,1,0:T(8,128)(2,1)S(1)}, bf16[2,320,128]{2,1,0:T(8,128)(2,1)S(1)}, u32[]{:S(2)}, u32[]{:S(2)}) collective-permute-start(bf16[2,320,128]{2,1,0:T(8,128)(2,1)S(1)} %pad_maximum_fusion.4), channel_id=1, source_target_pairs={{0,1},{1,2},{2,3},{3,4},{4,5},{5,6},{6,7},{7,0},{8,9},{9,10},{10,1... | collective-permute-start | bytes 491528 | tf_op jit(solution)/shard_map/ppermute | solution.py:126
  140.6 6.6 %collective-permute-start.7 = (bf16[2,160,256]{2,1,0:T(8,128)(2,1)S(1)}, bf16[2,160,256]{2,1,0:T(8,128)(2,1)S(1)}, u32[]{:S(2)}, u32[]{:S(2)}) collective-permute-start(bf16[2,160,256]{2,1,0:T(8,128)(2,1)S(1)} %bitcast_add_fusion.13), channel_id=1, source_target_pairs={{0,1},{1,2},{2,3},{3,4},{4,5},{5,6},{6,7},{7,0},{8,9},{9,10},{10,1... | collective-permute-start | bytes 491528 | tf_op jit(solution)/shard_map/ppermute | solution.py:126
  140.8 8.6 %collective-permute-start.28 = (bf16[2,320,128]{2,1,0:T(8,128)(2,1)S(1)}, bf16[2,320,128]{2,1,0:T(8,128)(2,1)S(1)}, u32[]{:S(2)}, u32[]{:S(2)}) collective-permute-start(bf16[2,320,128]{2,1,0:T(8,128)(2,1)S(1)} %pad_maximum_fusion.5), channel_id=1, source_target_pairs={{0,7},{1,0},{2,1},{3,2},{4,3},{5,4},{6,5},{7,6},{8,15},{9,8},{10,9... | collective-permute-start | bytes 491528 | tf_op jit(solution)/shard_map/ppermute | solution.py:126
  144.1 6.6 %collective-permute-start.25 = (bf16[2,320,128]{2,1,0:T(8,128)(2,1)S(1)}, bf16[2,320,128]{2,1,0:T(8,128)(2,1)S(1)}, u32[]{:S(2)}, u32[]{:S(2)}) collective-permute-start(bf16[2,320,128]{2,1,0:T(8,128)(2,1)S(1)} %bitcast_add_fusion.4), channel_id=1, source_target_pairs={{0,1},{1,2},{2,3},{3,4},{4,5},{5,6},{6,7},{7,0},{8,9},{9,10},{10,1... | collective-permute-start | bytes 491528 | tf_op jit(solution)/shard_map/ppermute | solution.py:126
  147.3 5.4 %collective-permute-start.11 = (bf16[2,160,256]{2,1,0:T(8,128)(2,1)S(1)}, bf16[2,160,256]{2,1,0:T(8,128)(2,1)S(1)}, u32[]{:S(2)}, u32[]{:S(2)}) collective-permute-start(bf16[2,160,256]{2,1,0:T(8,128)(2,1)S(1)} %get-tuple-element.28), channel_id=1, source_target_pairs={{0,7},{1,0},{2,1},{3,2},{4,3},{5,4},{6,5},{7,6},{8,15},{9,8},{10,9... | collective-permute-start | bytes 491528 | tf_op jit(solution)/shard_map/ppermute | solution.py:126
  147.5 10.0 %collective-permute-start.8 = (bf16[2,160,256]{2,1,0:T(8,128)(2,1)S(1)}, bf16[2,160,256]{2,1,0:T(8,128)(2,1)S(1)}, u32[]{:S(2)}, u32[]{:S(2)}) collective-permute-start(bf16[2,160,256]{2,1,0:T(8,128)(2,1)S(1)} %get-tuple-element.27), channel_id=1, source_target_pairs={{0,1},{1,2},{2,3},{3,4},{4,5},{5,6},{6,7},{7,0},{8,9},{9,10},{10,1... | collective-permute-start | bytes 491528 | tf_op jit(solution)/shard_map/ppermute | solution.py:126
  150.7 11.6 %copy-start.3 = (bf16[1,5120,384]{2,1,0:T(8,128)(2,1)S(1)}, bf16[1,5120,384]{2,1,0:T(8,128)(2,1)}, u32[]{:S(2)}) copy-start(bf16[1,5120,384]{2,1,0:T(8,128)(2,1)} %param.7) | copy-start | bytes 11796484
  150.7 5.4 %collective-permute-start.29 = (bf16[2,320,128]{2,1,0:T(8,128)(2,1)S(1)}, bf16[2,320,128]{2,1,0:T(8,128)(2,1)S(1)}, u32[]{:S(2)}, u32[]{:S(2)}) collective-permute-start(bf16[2,320,128]{2,1,0:T(8,128)(2,1)S(1)} %get-tuple-element.20), channel_id=1, source_target_pairs={{0,7},{1,0},{2,1},{3,2},{4,3},{5,4},{6,5},{7,6},{8,15},{9,8},{10,9... | collective-permute-start | bytes 491528 | tf_op jit(solution)/shard_map/ppermute | solution.py:126
  152.7 5.4 %collective-permute-start.12 = (bf16[2,160,256]{2,1,0:T(8,128)(2,1)S(1)}, bf16[2,160,256]{2,1,0:T(8,128)(2,1)S(1)}, u32[]{:S(2)}, u32[]{:S(2)}) collective-permute-start(bf16[2,160,256]{2,1,0:T(8,128)(2,1)S(1)} %bitcast_add_fusion.12), channel_id=1, source_target_pairs={{0,7},{1,0},{2,1},{3,2},{4,3},{5,4},{6,5},{7,6},{8,15},{9,8},{10,9... | collective-permute-start | bytes 491528 | tf_op jit(solution)/shard_map/ppermute | solution.py:126
  154.1 6.5 %collective-permute-start.26 = (bf16[2,320,128]{2,1,0:T(8,128)(2,1)S(1)}, bf16[2,320,128]{2,1,0:T(8,128)(2,1)S(1)}, u32[]{:S(2)}, u32[]{:S(2)}) collective-permute-start(bf16[2,320,128]{2,1,0:T(8,128)(2,1)S(1)} %get-tuple-element.19), channel_id=1, source_target_pairs={{0,1},{1,2},{2,3},{3,4},{4,5},{5,6},{6,7},{7,0},{8,9},{9,10},{10,1... | collective-permute-start | bytes 491528 | tf_op jit(solution)/shard_map/ppermute | solution.py:126
  156.2 5.4 %collective-permute-start.30 = (bf16[2,320,128]{2,1,0:T(8,128)(2,1)S(1)}, bf16[2,320,128]{2,1,0:T(8,128)(2,1)S(1)}, u32[]{:S(2)}, u32[]{:S(2)}) collective-permute-start(bf16[2,320,128]{2,1,0:T(8,128)(2,1)S(1)} %bitcast_add_fusion.3), channel_id=1, source_target_pairs={{0,7},{1,0},{2,1},{3,2},{4,3},{5,4},{6,5},{7,6},{8,15},{9,8},{10,9... | collective-permute-start | bytes 491528 | tf_op jit(solution)/shard_map/ppermute | solution.py:126
  161.6 6.0 %collective-permute-start.31 = (bf16[320,128]{1,0:T(8,128)(2,1)S(1)}, bf16[320,128]{1,0:T(8,128)(2,1)S(1)}, u32[]{:S(2)}, u32[]{:S(2)}) collective-permute-start(bf16[320,128]{1,0:T(8,128)(2,1)S(1)} %fusion.7), channel_id=1, source_target_pairs={{0,8},{1,9},{2,10},{3,11},{4,12},{5,13},{6,14},{7,15},{8,0},{9,1},... | collective-permute-start | bytes 245768 | tf_op jit(solution)/shard_map/ppermute | solution.py:131

commit v2 on v0

v2 whole, which is shorter than its diff:
```python
import functools

import jax
import jax.numpy as jnp
from jax import lax
from jax.experimental import pallas as pl
from jax.experimental.pallas import tpu as pltpu
from jax.sharding import PartitionSpec as P

BF = jnp.bfloat16
F32 = jnp.float32
N_Z = 8


def dot(a, b, ca, cb):
    return lax.dot_general(a, b, (((ca,), (cb,)), ((), ())), preferred_element_type=F32)


def shape(dims, dtype=BF):
    return jax.ShapeDtypeStruct(dims, dtype)


def attention_of(qkv, datt, seg_row_ref, seg_col_ref, dqkv_ref, att_ref):
    count, head = datt.shape
    scale = head ** (-0.5)
    q = qkv[:, :head]
    k = qkv[:, head : 2 * head]
    v = qkv[:, 2 * head :]
    rows = lax.broadcasted_iota(jnp.int32, (count, count), 0)
    cols = lax.broadcasted_iota(jnp.int32, (count, count), 1)
    allowed = (rows >= cols) & (seg_col_ref[...] == seg_row_ref[...])
    scores = jnp.where(allowed, dot(q, k, 1, 1) * scale, F32(-1e30))
    top = jnp.max(scores, axis=-1, keepdims=True)
    expo = jnp.where(allowed, jnp.exp(scores - top), F32(0.0))
    probs = expo / jnp.sum(expo, axis=-1, keepdims=True)
    probs_b = probs.astype(BF)
    att_ref[...] = dot(probs_b, v, 1, 0).astype(BF)
    d_probs = dot(datt, v, 1, 1)
    inner = jnp.sum(probs * d_probs, axis=-1, keepdims=True)
    d_scores = (probs * (d_probs - inner) * scale).astype(BF)
    dqkv_ref[:, :head] = dot(d_scores, k, 1, 0).astype(BF)
    dqkv_ref[:, head : 2 * head] = dot(d_scores, q, 0, 0).astype(BF)
    dqkv_ref[:, 2 * head :] = dot(probs_b, datt, 0, 0).astype(BF)


def whole(kernel, name, limit, args, in_hbm, outs, scratch=(), flops=1):
    here = pl.BlockSpec(memory_space=pltpu.VMEM)
    there = pl.BlockSpec(memory_space=pltpu.HBM)
    return pl.pallas_call(
        kernel,
        in_specs=[here] * (len(args) - in_hbm) + [there] * in_hbm,
        out_specs=[here] * len(outs),
        out_shape=outs,
        scratch_shapes=scratch,
        compiler_params=pltpu.CompilerParams(vmem_limit_bytes=limit * 1024 * 1024),
        cost_estimate=pl.CostEstimate(flops=flops, bytes_accessed=1, transcendentals=0),
        name=name,
    )(*args)


def fetch_rows(n, src, dst, sem):
    tile = src.shape[0] // n
    return [
        pltpu.make_async_copy(
            src.at[pl.ds(i * tile, tile)], dst.at[pl.ds(i * tile, tile)], sem.at[i]
        )
        for i in range(n)
    ]


def projected(x_ref, w_ref, copies):
    tile = w_ref.shape[0] // len(copies)
    total = 0.0
    for i, copy in enumerate(copies):
        copy.wait()
        total += dot(x_ref[:, i * tile : (i + 1) * tile], w_ref[i * tile : (i + 1) * tile], 1, 0)
    return total.astype(BF)


def add_up(pairs, outs, tile):
    for start in range(0, pairs[0][0].shape[1], tile):
        total = sum(dot(x[:, start : start + tile], d, 0, 0) for x, d in pairs)
        column = 0
        for out in outs:
            width = out.shape[1]
            out[start : start + tile] = total[:, column : column + width].astype(BF)
            column += width


N_W = 4
TILE = 1280
SMALL, LARGE = 14, 48


def own_kernel(
    seg_row_ref, seg_col_ref, x_hbm, w_hbm, g_hbm, wo_hbm, dqkv_ref, att_ref,
    x_ref, w_ref, g_ref, wo_ref, w_sem, sems,
):
    x_copy = pltpu.make_async_copy(x_hbm, x_ref, sems.at[0])
    w_copies = fetch_rows(N_W, w_hbm, w_ref, w_sem)
    g_copy = pltpu.make_async_copy(g_hbm, g_ref, sems.at[1])
    wo_copy = pltpu.make_async_copy(wo_hbm, wo_ref, sems.at[2])
    for copy in (x_copy, *w_copies, g_copy, wo_copy):
        copy.start()
    x_copy.wait()
    qkv = projected(x_ref, w_ref, w_copies)
    g_copy.wait()
    wo_copy.wait()
    datt = dot(g_ref[...], wo_ref[...], 1, 1).astype(BF)
    attention_of(qkv, datt, seg_row_ref, seg_col_ref, dqkv_ref, att_ref)


def own_pair(x, w, g, wo, seg):
    count = x.shape[0]
    head = wo.shape[0]
    return whole(
        own_kernel,
        "own_pair",
        LARGE,
        (seg[None, :], seg[:, None], x, w, g, wo),
        4,
        [shape((count, 3 * head)), shape((count, head))],
        [pltpu.VMEM(a.shape, BF) for a in (x, w, g, wo)]
        + [pltpu.SemaphoreType.DMA((N_W,)), pltpu.SemaphoreType.DMA((3,))],
    )


def far_kernel(
    xf_ref, datt_ref, seg_row_ref, seg_col_ref, d_ref, w_hbm, x_hbm, dqkv_ref, att_ref, *rest
):
    outs, (w_ref, x_ref, w_sem, x_sem) = rest[:-4], rest[-4:]
    w_copies = fetch_rows(N_W, w_hbm, w_ref, w_sem)
    x_copy = pltpu.make_async_copy(x_hbm, x_ref, x_sem)
    for copy in (*w_copies, x_copy):
        copy.start()
    qkv = projected(xf_ref, w_ref, w_copies)
    attention_of(qkv, datt_ref[...], seg_row_ref, seg_col_ref, dqkv_ref, att_ref)
    x_copy.wait()
    add_up([(x_ref, d_ref[...]), (xf_ref, dqkv_ref[...])], outs, TILE)


def far_pair(x_far, datt, seg, d_own, w, x, widths):
    count, model = x.shape
    head = datt.shape[1]
    return whole(
        far_kernel,
        "far_pair",
        LARGE,
        (x_far, datt, seg[None, :], seg[:, None], d_own, w, x),
        2,
        [shape((count, 3 * head)), shape((count, head))] + [shape((model, n)) for n in widths],
        [pltpu.VMEM(w.shape, BF), pltpu.VMEM(x.shape, BF)]
        + [pltpu.SemaphoreType.DMA((N_W,)), pltpu.SemaphoreType.DMA],
    )


def grads_kernel(*refs):
    out_ref = refs[-1]
    pairs = [(refs[i], refs[i + 1][...]) for i in range(0, len(refs) - 1, 2)]
    add_up(pairs, [out_ref], TILE)


def grads_out(*pairs):
    out = shape((pairs[0][0].shape[1], pairs[0][1].shape[1]))
    args = [a for pair in pairs for a in pair]
    return whole(grads_kernel, "grads_out", SMALL, args, 0, [out])[0]


def first_pair(z):
    return (z + 3) // 2 % (N_Z // 2)


def columns_kernel(after_ref, g_hbm, near_ref, rest_ref, sems):
    z = lax.axis_index("dp") % N_Z
    model = g_hbm.shape[1]
    width = model // N_Z
    copies = []
    for i, out in enumerate((near_ref, rest_ref)):
        for x_hi in range(2):
            for k in range(2):
                pair = (first_pair(z) + 2 * i + k) % (N_Z // 2)
                start = pl.multiple_of(x_hi * (model // 2) + pair * width, 128)
                copies.append(
                    pltpu.make_async_copy(
                        g_hbm.at[:, pl.ds(start, width)],
                        out.at[:, pl.ds((2 * x_hi + k) * width, width)],
                        sems.at[len(copies)],
                    )
                )
    for copy in copies:
        copy.start()
    for copy in copies:
        copy.wait()


def columns_of(g, after):
    outs = [shape((g.shape[0], g.shape[1] // 2))] * 2
    return whole(
        columns_kernel, "columns", SMALL, (after, g), 1, outs, [pltpu.SemaphoreType.DMA((8,))]
    )


def term_kernel(d_ref, w_ref, *rest):
    out_ref = rest[-1]
    for start in range(0, w_ref.shape[0], TILE):
        total = dot(d_ref[...], w_ref[start : start + TILE], 1, 1)
        if len(rest) == 2:
            total += rest[0][:, start : start + TILE].astype(F32)
        out_ref[:, start : start + TILE] = total.astype(BF)


def term(d, w, *far):
    name = "sum_term" if far else "far_term"
    out = shape((d.shape[0], w.shape[0]))
    return whole(term_kernel, name, SMALL, (d, w, *far), 0, [out], (), 4 * d.shape[0] * w.size)[0]


def shifted(block, distance):
    n = lax.axis_size("blk")
    return lax.ppermute(block, "blk", [(i, (i + distance) % n) for i in range(n)])


def z_shifted(block, distance):
    n = lax.axis_size("dp")
    route = [(i, i // N_Z * N_Z + (i + distance) % N_Z) for i in range(n)]
    return lax.ppermute(block, "dp", route)


def x_swapped(block):
    n = lax.axis_size("dp")
    return lax.ppermute(block, "dp", [(i, (i + N_Z) % n) for i in range(n)])


def entry(part, distance):
    z = lax.axis_index("dp") % N_Z
    return lax.dynamic_index_in_dim(part, (z + distance) % N_Z, 1, keepdims=False)


def payload(at, step, moving):
    if step == 1:
        across = at(4)
        half = across.shape[1] // 2
        return across[:, :half], across[:, half:]
    up, down = moving
    if step == 2:
        half = up.shape[1]
        third_up, third_down = at(3), at(-3)
        up = jnp.concatenate([third_up[:, :half] + up, third_up[:, half:]], axis=1)
        down = jnp.concatenate([third_down[:, :half], third_down[:, half:] + down], axis=1)
        return up, down
    return at(5 - step) + up, at(step - 5) + down


def z_send(both):
    return z_shifted(both[0], 1), z_shifted(both[1], -1)


def z_end(at, moving):
    up, down = moving
    return at(0).astype(F32) + up.astype(F32) + down.astype(F32)


def halves_of(both, x_hi):
    mine = lax.dynamic_index_in_dim(both, x_hi, 0, keepdims=False)
    other = lax.dynamic_index_in_dim(both, 1 - x_hi, 0, keepdims=False)
    return mine, other


def x_end(both, x_hi):
    mine, other = halves_of(both, x_hi)
    return mine + x_swapped(other.astype(BF)).astype(F32)


def local(normed_input, segment_ids, weights_qkv, weights_out, cotangent):
    x, wq, wo, g = normed_input[0], weights_qkv[0], weights_out[0], cotangent[0]
    n_blk = lax.axis_size("blk")
    here = lax.axis_index("blk")
    x_hi = lax.axis_index("dp") // N_Z
    head = wo.shape[0]
    seg = lax.dynamic_index_in_dim(segment_ids[0], here, 0, keepdims=False)
    seg_far = lax.dynamic_index_in_dim(segment_ids[0], (here + 1) % n_blk, 0, keepdims=False)

    model = x.shape[1]
    half = model // 2
    rows = half // N_Z
    x_far = shifted(x, -1)
    wo_back = shifted(wo, 1)
    together = lax.optimization_barrier
    split = lambda grad: grad.reshape(2, N_Z, rows, grad.shape[1])
    d_qkv, att = own_pair(x, wq, g, wo, seg)
    wo_back, d_qkv = together((wo_back, d_qkv))
    d_att_home = dot(g, wo_back, 1, 1).astype(BF)
    d_att_far = shifted(d_att_home, -1)
    columns = columns_of(g, d_att_home)
    near, d_att_far = together((columns[0], d_att_far))
    columns_far = [shifted(near, -1), None]
    d_qkv_far, att_far, grad_qk, grad_v = far_pair(
        x_far, d_att_far, seg_far, d_qkv, wq, x, (2 * head, head)
    )

    rest_of, att_far = together((columns[1], att_far))
    columns_far[1] = shifted(rest_of, -1)
    grad_qk, grad_v = split(grad_qk), split(grad_v)
    first = functools.partial(entry, grad_qk)
    z = lax.axis_index("dp") % N_Z

    def terms_o(i):
        grad = grads_out((columns[i], att), (columns_far[i], att_far))
        return grad.reshape(2, N_Z // 2, rows, head)

    def second(distance):
        at = (z + distance - 2 * first_pair(z)) % N_Z
        grad_o = lax.dynamic_index_in_dim(terms, at, 1, keepdims=False)
        return jnp.concatenate([entry(grad_v, distance), grad_o], axis=2)

    sent = z_send(payload(first, 1, None))
    sent, columns_far[0] = together((sent, columns_far[0]))
    terms = near = terms_o(0)
    sent_2 = z_send(payload(second, 1, None))
    load, d_qkv_far = together((payload(first, 2, sent), d_qkv_far))
    sent = z_send(load)
    term_back = shifted(term(d_qkv_far, wq), 1)
    load, columns_far[1] = together((payload(second, 2, sent_2), columns_far[1]))
    sent_2 = z_send(load)
    terms = jnp.concatenate([near, terms_o(1)], axis=1)
    sent = z_send(payload(first, 3, sent))
    sent_2 = z_send(payload(second, 3, sent_2))
    load, term_back = together((payload(first, 4, sent), term_back))
    sent = z_send(load)
    sent_2 = z_send(payload(second, 4, sent_2))
    input_grad = term(d_qkv, wq, term_back)
    ends = jnp.concatenate([z_end(first, sent), z_end(second, sent_2)], axis=2)
    ends, input_grad = together((ends, input_grad))
    total = x_end(ends, x_hi).astype(BF)
    return input_grad[None], total[:, : 3 * head][None], total[:, 3 * head :].T[None]


def solution(mesh):
    placed = (
        P(("blk", "dp"), None, None),
        P("dp", None, None),
        P("blk", None, None),
        P("blk", None, None),
        P(("blk", "dp"), None, None),
    )
    return jax.shard_map(
        local,
        mesh=mesh,
        in_specs=placed,
        out_specs=(P(("blk", "dp"), None, None), P("blk", "dp", None), P("blk", None, "dp")),
        check_vma=False,
    )
```

time: 584 us -> 132 us (0.23)
  waiting for transfers between devices: 488 us -> 48 us
  matrix products: 39.6 us -> 2.18 us
  starting transfers between devices: 2.16 us -> 34 us
  Pallas kernels: 0 us -> 27.7 us
  local copies, waits for them, and re-layouts: 36.1 us -> 12 us
  between operations: 14.2 us -> 1 us
  other arithmetic: 0.33 us -> 6.86 us
    unnamed x4 -> x0, waiting for transfers between devices: 382 us -> none
    ppermute x4 -> x23, waiting for transfers between devices: 106 us -> 48 us  [the longest x16 25.1 us: z_shifted(): return lax.ppermute(block, 'dp', route)]
    dot_general x20 -> x1, matrix products: 39.6 us -> 2.18 us  [dot(): lax.dot_general(a, b, (((ca,), (cb,)), ((), ())), preferred_element_type=...]
    ppermute x4 -> x23, starting transfers between devices: 1.9 us -> 34 us  [the longest x16 29 us: z_shifted(): return lax.ppermute(block, 'dp', route)]
    unnamed x22 -> x20, local copies, waits for them, and re-layouts: 35.4 us -> 6.25 us
    pallas_call x0 -> x7, Pallas kernels: none -> 27.7 us  [whole(): pl.pallas_call(kernel, in_specs=[here] * (len(args) - in_hbm) + [there] *...]
    add x0 -> x11, other arithmetic: none -> 6.1 us  [the longest x7 3.77 us: payload(): return (at(5 - step) + up, at(step - 5) + down)]
  transfers between devices with their start and end apart: 6 -> 23, of which waited for: 4 -> 10; matrix products, arithmetic and copies ran while one was open for 11% -> 10% of each run, Pallas kernels for 0% -> 21%
where the time goes in v2:
time: 132 us
  waiting for transfers between devices  48 us (36%)
  starting transfers between devices  34 us (26%)
  Pallas kernels  27.7 us (21%)
  local copies, waits for them, and re-layouts  12 us (9%)
  other arithmetic  6.86 us (5%)
  matrix products  2.18 us (2%)
    ppermute x16, starting transfers between devices, z_shifted(): return lax.ppermute(block, 'dp', route)  29 us
    pallas_call x7, Pallas kernels, whole(): pl.pallas_call(kernel, in_specs=[here] * (len(args) - in_hbm) + [there] *...  27.7 us
    ppermute x16, waiting for transfers between devices, z_shifted(): return lax.ppermute(block, 'dp', route)  25.1 us
    ppermute x6, waiting for transfers between devices, shifted(): lax.ppermute(block, 'blk', [(i, (i + distance) % n) for i in range(n)])  14.8 us
    ppermute x1, waiting for transfers between devices, x_swapped(): return lax.ppermute(block, 'dp', [(i, (i + N_Z) % n) for i in range(n)])  8.07 us
    unnamed x20, local copies, waits for them, and re-layouts  6.25 us
    ppermute x6, starting transfers between devices, shifted(): lax.ppermute(block, 'blk', [(i, (i + distance) % n) for i in range(n)])  4.46 us
    add x7, other arithmetic, payload(): return (at(5 - step) + up, at(step - 5) + down)  3.77 us
  transfers between devices with their start and end apart: 23, of which 10 were waited for; matrix products, arithmetic and copies ran while one was open for 10% of the time, Pallas kernels for 21%

profile of v2, /device:TPU:28, one launch (start us, length us, event | category | flops | bytes accessed | tf_op | source)
XLA Modules:
  0.0 131.8 jit_solution(5742536115805984414)
XLA Ops:
  0.6 0.3 collective-permute-start
  0.9 0.3 collective-permute-start.1
  1.2 0.8 fusion.25
  2.0 0.1 copy.10.seg_col_ref
  2.2 1.7 %copy-done.3 = bf16[1,256,5120]{2,1,0:T(8,128)(2,1)S(1)} copy-done((bf16[1,256,5120]{2,1,0:T(8,128)(2,1)S(1)}, bf16[1,256,5120]{2,1,0:T(8,128)(2,1)}, u32[]{:S(2)}) %copy-start.3) | copy-done | bytes 2621464
  3.9 1.3 copy-done.7
  5.2 6.1 %own_pair.1 = (bf16[256,384]{1,0:T(8,128)(2,1)S(1)}, bf16[256,128]{1,0:T(8,128)(2,1)S(1)}) custom-call(s32[1,256]{1,0:T(1,128)S(1)} %get-tuple-element.93.seg_row_ref, s32[256,1]{1,0:T(8,128)S(1)} %copy.10.seg_col_ref, bf16[256,5120]{1,0:T(8,128)(2,1)S(1)} %bitcast.93, bf16[5120,384]{1,0:T(8,128)(2,1)} %bitcast.85, bf16[256,5120]{1,0:T(8,128)(2,1)} %bitcast.89, ...), custom_call_target="tpu_custom_call" | custom-call | flops 1 | bytes 1 | tf_op jit(solution)/shard_map/own_pair/pallas_call | solution.py:49
  11.3 7.0 %collective-permute-done.1 = bf16[128,5120]{1,0:T(8,128)(2,1)} collective-permute-done((bf16[128,5120]{1,0:T(8,128)(2,1)}, bf16[128,5120]{1,0:T(8,128)(2,1)}, u32[]{:S(2)}, u32[]{:S(2)}) %collective-permute-start.1) | collective-permute-done | bytes 1310752 | tf_op jit(solution)/shard_map/ppermute | solution.py:220
  18.2 2.2 %fusion.after_ref = bf16[256,128]{1,0:T(8,128)(2,1)S(1)} fusion(bf16[128,5120]{1,0:T(8,128)(2,1)} %collective-permute-done.1, bf16[1,256,5120]{2,1,0:T(8,128)(2,1)S(1)} %copy-done.2), kind=kOutput, calls=%fused_computation.12 | convolution fusion | flops 335577088 | bytes 3997696 | tf_op jit(solution)/shard_map/dot_general | solution.py:16
  20.4 0.1 collective-permute-start.2
  20.5 1.5 %columns.1 = (bf16[256,2560]{1,0:T(8,128)(2,1)}, bf16[256,2560]{1,0:T(8,128)(2,1)S(1)}) custom-call(bf16[256,128]{1,0:T(8,128)(2,1)S(1)} %fusion.after_ref, bf16[256,5120]{1,0:T(8,128)(2,1)S(1)} %bitcast.90), custom_call_target="tpu_custom_call" | custom-call | flops 1 | bytes 1 | tf_op jit(solution)/shard_map/columns/pallas_call | solution.py:49
  22.0 1.1 copy-done.4
  23.1 7.9 %collective-permute-done.2.datt_ref = bf16[256,128]{1,0:T(8,128)(2,1)S(1)} collective-permute-done((bf16[256,128]{1,0:T(8,128)(2,1)S(1)}, bf16[256,128]{1,0:T(8,128)(2,1)S(1)}, u32[]{:S(2)}, u32[]{:S(2)}) %collective-permute-start.2) | collective-permute-done | bytes 65568 | tf_op jit(solution)/shard_map/ppermute | solution.py:220
  31.0 1.9 %collective-permute-start.5 = (bf16[256,2560]{1,0:T(8,128)(2,1)}, bf16[256,2560]{1,0:T(8,128)(2,1)}, u32[]{:S(2)}, u32[]{:S(2)}) collective-permute-start(bf16[256,2560]{1,0:T(8,128)(2,1)} %get-tuple-element.37.refs_0_), channel_id=1, source_target_pairs={{0,240},{16,0},{32,16},{48,32},{64,48},{80,64},{96,80},{112,96},{1... | collective-permute-start | bytes 3932168 | tf_op jit(solution)/shard_map/ppermute | solution.py:220
  32.9 0.1 copy.12.seg_col_ref
  33.0 8.7 %far_pair.1 = (bf16[256,384]{1,0:T(8,128)(2,1)S(1)}, bf16[256,128]{1,0:T(8,128)(2,1)S(1)}, bf16[5120,256]{1,0:T(8,128)(2,1)S(1)}, bf16[5120,128]{1,0:T(8,128)(2,1)S(1)}) custom-call(bf16[256,5120]{1,0:T(8,128)(2,1)} %collective-permute-done.xf_ref, bf16[256,128]{1,0:T(8,128)(2,1)S(1)} %collective-permute-done.2.datt_ref, ...), custom_call_target="tpu_custom_call" | custom-call | flops 1 | bytes 1 | tf_op jit(solution)/shard_map/far_pair/pallas_call | solution.py:49
  41.8 1.0 dynamic-slice_bitcast_fusion
  42.8 0.7 fusion.29
  43.5 1.9 %collective-permute-start.3 = (bf16[2,160,256]{2,1,0:T(8,128)(2,1)}, bf16[2,160,256]{2,1,0:T(8,128)(2,1)S(1)}, u32[]{:S(2)}, u32[]{:S(2)}) collective-permute-start(bf16[2,160,256]{2,1,0:T(8,128)(2,1)} %get-tuple-element.89), channel_id=1, source_target_pairs={{0,1},{1,2},{2,3},{3,4},{4,5},{5,6},{6,7},{7,0},{8,9},{9,10},{10,1... | collective-permute-start | bytes 491528 | tf_op jit(solution)/shard_map/ppermute | solution.py:226
  45.5 3.9 %collective-permute-start.4 = (bf16[2,160,256]{2,1,0:T(8,128)(2,1)}, bf16[2,160,256]{2,1,0:T(8,128)(2,1)}, u32[]{:S(2)}, u32[]{:S(2)}) collective-permute-start(bf16[2,160,256]{2,1,0:T(8,128)(2,1)} %get-tuple-element.88), channel_id=1, source_target_pairs={{0,7},{1,0},{2,1},{3,2},{4,3},{5,4},{6,5},{7,6},{8,15},{9,8},{10,9... | collective-permute-start | bytes 491528 | tf_op jit(solution)/shard_map/ppermute | solution.py:226
  49.4 1.5 %dynamic-slice_bitcast_fusion.13 = (bf16[2,320,128]{2,1,0:T(8,128)(2,1)S(1)}, bf16[2,320,128]{2,1,0:T(8,128)(2,1)S(1)}, bf16[2,320,128]{2,1,0:T(8,128)(2,1)S(1)}...) fusion(bf16[2,8,320,128]{3,2,1,0:T(8,128)(2,1)} %bitcast.102, ...), kind=kLoop, calls=%fused_computation.70 | loop fusion | bytes 2621472 | tf_op jit(solution)/shard_map/jit(dynamic_index_in_dim)/squeeze | solution.py:236
  50.9 2.6 %collective-permute-done.3 = bf16[2,160,256]{2,1,0:T(8,128)(2,1)S(1)} collective-permute-done((bf16[2,160,256]{2,1,0:T(8,128)(2,1)}, bf16[2,160,256]{2,1,0:T(8,128)(2,1)S(1)}, u32[]{:S(2)}, u32[]{:S(2)}) %collective-permute-start.3) | collective-permute-done | bytes 163872 | tf_op jit(solution)/shard_map/ppermute | solution.py:226
  53.6 2.6 %grads_out.2 = bf16[2560,128]{1,0:T(8,128)(2,1)S(1)} custom-call(bf16[256,2560]{1,0:T(8,128)(2,1)} %get-tuple-element.37.refs_0_, bf16[256,128]{1,0:T(8,128)(2,1)S(1)} %get-tuple-element.47.refs_1_, bf16[256,2560]{1,0:T(8,128)(2,1)} %collective-permute-done.5.refs_2_, bf16[256,128]{1,0:T(8,128)(2,1)S(1)} %get-tuple-element.51.refs_3_), custom_call_target="tpu_custom_call" | custom-call | flops 1 | bytes 1 | tf_op jit(solution)/shard_map/grads_out/pallas_call | solution.py:49
  56.3 0.6 collective-permute-start.13
  56.9 3.2 %collective-permute-start.14 = (bf16[2,160,256]{2,1,0:T(8,128)(2,1)S(1)}, bf16[2,160,256]{2,1,0:T(8,128)(2,1)S(1)}, u32[]{:S(2)}, u32[]{:S(2)}) collective-permute-start(bf16[2,160,256]{2,1,0:T(8,128)(2,1)S(1)} %get-tuple-element.86), channel_id=1, source_target_pairs={{0,7},{1,0},{2,1},{3,2},{4,3},{5,4},{6,5},{7,6},{8,15},{9,8},{10,9... | collective-permute-start | bytes 491528 | tf_op jit(solution)/shard_map/ppermute | solution.py:226
  60.2 1.0 slice_add_fusion.1
  61.2 2.0 %collective-permute-start.8 = (bf16[2,320,256]{2,1,0:T(8,128)(2,1)S(1)}, bf16[2,320,256]{2,1,0:T(8,128)(2,1)S(1)}, u32[]{:S(2)}, u32[]{:S(2)}) collective-permute-start(bf16[2,320,256]{2,1,0:T(8,128)(2,1)S(1)} %pad_maximum_fusion.2), channel_id=1, source_target_pairs={{0,7},{1,0},{2,1},{3,2},{4,3},{5,4},{6,5},{7,6},{8,15},{9,8},{10,9... | collective-permute-start | bytes 983048 | tf_op jit(solution)/shard_map/ppermute | solution.py:226
  63.2 0.1 collective-permute-start.6
  63.3 3.1 %far_term.1 = bf16[256,5120]{1,0:T(8,128)(2,1)} custom-call(bf16[256,384]{1,0:T(8,128)(2,1)S(1)} %get-tuple-element.43.d_ref, bf16[5120,384]{1,0:T(8,128)(2,1)S(1)} %bitcast.87), custom_call_target="tpu_custom_call" | custom-call | flops 2013265920 | bytes 1 | tf_op jit(solution)/shard_map/far_term/pallas_call | solution.py:49
  66.3 1.9 %collective-permute-start.10 = (bf16[256,5120]{1,0:T(8,128)(2,1)}, bf16[256,5120]{1,0:T(8,128)(2,1)}, u32[]{:S(2)}, u32[]{:S(2)}) collective-permute-start(bf16[256,5120]{1,0:T(8,128)(2,1)} %far_term.1), channel_id=1, source_target_pairs={{0,16},{16,32},{32,48},{48,64},{64,80},{80,96},{96,112},{112,128},... | collective-permute-start | bytes 7864328 | tf_op jit(solution)/shard_map/ppermute | solution.py:220
  68.3 0.1 fusion.13
  68.4 2.9 %collective-permute-start.19 = (bf16[2,320,256]{2,1,0:T(8,128)(2,1)S(1)}, bf16[2,320,256]{2,1,0:T(8,128)(2,1)S(1)}, u32[]{:S(2)}, u32[]{:S(2)}) collective-permute-start(bf16[2,320,256]{2,1,0:T(8,128)(2,1)S(1)} %pad_maximum_fusion.3), channel_id=1, source_target_pairs={{0,7},{1,0},{2,1},{3,2},{4,3},{5,4},{6,5},{7,6},{8,15},{9,8},{10,9... | collective-permute-start | bytes 983048 | tf_op jit(solution)/shard_map/ppermute | solution.py:226
  71.4 3.4 %collective-permute-start.9 = (bf16[2,320,256]{2,1,0:T(8,128)(2,1)S(1)}, bf16[2,320,256]{2,1,0:T(8,128)(2,1)S(1)}, u32[]{:S(2)}, u32[]{:S(2)}) collective-permute-start(bf16[2,320,256]{2,1,0:T(8,128)(2,1)S(1)} %bitcast_add_fusion.1), channel_id=1, source_target_pairs={{0,7},{1,0},{2,1},{3,2},{4,3},{5,4},{6,5},{7,6},{8,15},{9,8},{10,9... | collective-permute-start | bytes 983048 | tf_op jit(solution)/shard_map/ppermute | solution.py:226
  74.8 0.9 grads_out.3
  75.7 0.2 collective-permute-start.16
  75.9 0.3 fusion.21
  76.2 1.2 collective-permute-done.19
  77.4 0.1 maximum_add_fusion.3
  77.5 3.8 %collective-permute-start.20 = (bf16[2,320,256]{2,1,0:T(8,128)(2,1)S(1)}, bf16[2,320,256]{2,1,0:T(8,128)(2,1)S(1)}, u32[]{:S(2)}, u32[]{:S(2)}) collective-permute-start(bf16[2,320,256]{2,1,0:T(8,128)(2,1)S(1)} %maximum_add_fusion.3), channel_id=1, source_target_pairs={{0,7},{1,0},{2,1},{3,2},{4,3},{5,4},{6,5},{7,6},{8,15},{9,8},{10,9... | collective-permute-start | bytes 983048 | tf_op jit(solution)/shard_map/ppermute | solution.py:226
  81.2 5.7 %collective-permute-done.16 = bf16[2,320,256]{2,1,0:T(8,128)(2,1)S(1)} collective-permute-done((bf16[2,320,256]{2,1,0:T(8,128)(2,1)S(1)}, bf16[2,320,256]{2,1,0:T(8,128)(2,1)S(1)}, u32[]{:S(2)}, u32[]{:S(2)}) %collective-permute-start.16) | collective-permute-done | bytes 327712 | tf_op jit(solution)/shard_map/ppermute | solution.py:226
  86.9 0.1 maximum_add_fusion.1
  87.0 0.1 collective-permute-start.17
  87.1 0.9 bitcast_add_fusion.2
  88.1 1.0 collective-permute-start.7
  89.1 2.3 %collective-permute-done.20 = bf16[2,320,256]{2,1,0:T(8,128)(2,1)S(1)} collective-permute-done((bf16[2,320,256]{2,1,0:T(8,128)(2,1)S(1)}, bf16[2,320,256]{2,1,0:T(8,128)(2,1)S(1)}, u32[]{:S(2)}, u32[]{:S(2)}) %collective-permute-start.20) | collective-permute-done | bytes 327712 | tf_op jit(solution)/shard_map/ppermute | solution.py:226
  91.4 0.8 maximum_add_fusion.2
  92.2 3.7 %collective-permute-start.21 = (bf16[2,320,256]{2,1,0:T(8,128)(2,1)}, bf16[2,320,256]{2,1,0:T(8,128)(2,1)}, u32[]{:S(2)}, u32[]{:S(2)}) collective-permute-start(bf16[2,320,256]{2,1,0:T(8,128)(2,1)} %maximum_add_fusion.2), channel_id=1, source_target_pairs={{0,7},{1,0},{2,1},{3,2},{4,3},{5,4},{6,5},{7,6},{8,15},{9,8},{10,9... | collective-permute-start | bytes 983048 | tf_op jit(solution)/shard_map/ppermute | solution.py:226
  95.9 3.0 %collective-permute-done.17 = bf16[2,320,256]{2,1,0:T(8,128)(2,1)S(1)} collective-permute-done((bf16[2,320,256]{2,1,0:T(8,128)(2,1)S(1)}, bf16[2,320,256]{2,1,0:T(8,128)(2,1)S(1)}, u32[]{:S(2)}, u32[]{:S(2)}) %collective-permute-start.17) | collective-permute-done | bytes 327712 | tf_op jit(solution)/shard_map/ppermute | solution.py:226
  98.9 0.8 maximum_add_fusion
  99.8 6.3 %collective-permute-done.7 = bf16[2,320,256]{2,1,0:T(8,128)(2,1)} collective-permute-done((bf16[2,320,256]{2,1,0:T(8,128)(2,1)}, bf16[2,320,256]{2,1,0:T(8,128)(2,1)}, u32[]{:S(2)}, u32[]{:S(2)}) %collective-permute-start.7) | collective-permute-done | bytes 327712 | tf_op jit(solution)/shard_map/ppermute | solution.py:226
  106.1 1.0 bitcast_add_fusion.4
  107.1 0.1 collective-permute-start.12
  107.2 2.0 %collective-permute-start.11 = (bf16[2,320,256]{2,1,0:T(8,128)(2,1)S(1)}, bf16[2,320,256]{2,1,0:T(8,128)(2,1)S(1)}, u32[]{:S(2)}, u32[]{:S(2)}) collective-permute-start(bf16[2,320,256]{2,1,0:T(8,128)(2,1)S(1)} %bitcast_add_fusion.4), channel_id=1, source_target_pairs={{0,1},{1,2},{2,3},{3,4},{4,5},{5,6},{6,7},{7,0},{8,9},{9,10},{10,1... | collective-permute-start | bytes 983048 | tf_op jit(solution)/shard_map/ppermute | solution.py:226
  109.2 3.9 %collective-permute-done.18 = bf16[2,320,256]{2,1,0:T(8,128)(2,1)} collective-permute-done((bf16[2,320,256]{2,1,0:T(8,128)(2,1)}, bf16[2,320,256]{2,1,0:T(8,128)(2,1)}, u32[]{:S(2)}, u32[]{:S(2)}) %collective-permute-start.18) | collective-permute-done | bytes 327712 | tf_op jit(solution)/shard_map/ppermute | solution.py:226
  113.1 1.2 convert_add_fusion.1
  114.3 2.1 %copy-done.1 = bf16[1,5120,384]{2,1,0:T(8,128)(2,1)S(1)} copy-done((bf16[1,5120,384]{2,1,0:T(8,128)(2,1)S(1)}, bf16[1,5120,384]{2,1,0:T(8,128)(2,1)}, u32[]{:S(2)}) %copy-start.1) | copy-done | bytes 3932184
  116.4 4.9 %sum_term.1 = bf16[256,5120]{1,0:T(8,128)(2,1)} custom-call(bf16[256,384]{1,0:T(8,128)(2,1)S(1)} %get-tuple-element.35.d_ref, bf16[5120,384]{1,0:T(8,128)(2,1)S(1)} %bitcast.88, bf16[256,5120]{1,0:T(8,128)(2,1)} %collective-permute-done.10.rest_0_), custom_call_target="tpu_custom_call" | custom-call | flops 2013265920 | bytes 1 | tf_op jit(solution)/shard_map/sum_term/pallas_call | solution.py:49
  121.3 0.1 fusion.3
  121.4 0.2 pad_maximum_fusion
  121.6 0.6 collective-permute-start.22
  122.2 8.1 %collective-permute-done.22 = bf16[320,512]{1,0:T(8,128)(2,1)S(1)} collective-permute-done((bf16[320,512]{1,0:T(8,128)(2,1)S(1)}, bf16[320,512]{1,0:T(8,128)(2,1)S(1)}, u32[]{:S(2)}, u32[]{:S(2)}) %collective-permute-start.22) | collective-permute-done | bytes 327712 | tf_op jit(solution)/shard_map/ppermute | solution.py:231
  130.3 0.1 fusion.4
  130.4 0.7 slice_bitcast_fusion
  131.1 0.6 slice_bitcast_fusion.1
  (40 shorter events, 0.4 us)
Async XLA Ops:
  0.6 32.4 %collective-permute-start = (bf16[256,5120]{1,0:T(8,128)(2,1)}, bf16[256,5120]{1,0:T(8,128)(2,1)}, u32[]{:S(2)}, u32[]{:S(2)}) collective-permute-start(bf16[256,5120]{1,0:T(8,128)(2,1)} %bitcast.91), channel_id=1, source_target_pairs={{0,240},{16,0},{32,16},{48,32},{64,48},{80,64},{96,80},{112,96},{1... | collective-permute-start | bytes 7864328 | tf_op jit(solution)/shard_map/ppermute | solution.py:220
  0.9 17.3 %collective-permute-start.1 = (bf16[128,5120]{1,0:T(8,128)(2,1)}, bf16[128,5120]{1,0:T(8,128)(2,1)}, u32[]{:S(2)}, u32[]{:S(2)}) collective-permute-start(bf16[128,5120]{1,0:T(8,128)(2,1)} %bitcast.103), channel_id=1, source_target_pairs={{0,16},{16,32},{32,48},{48,64},{64,80},{80,96},{96,112},{112,128},... | collective-permute-start | bytes 3932168 | tf_op jit(solution)/shard_map/ppermute | solution.py:220
  2.1 1.7 %copy-start.3 = (bf16[1,256,5120]{2,1,0:T(8,128)(2,1)S(1)}, bf16[1,256,5120]{2,1,0:T(8,128)(2,1)}, u32[]{:S(2)}) copy-start(bf16[1,256,5120]{2,1,0:T(8,128)(2,1)} %param.5) | copy-start | bytes 7864324
  3.9 1.3 copy-start.7
  5.2 13.0 %copy-start.2 = (bf16[1,256,5120]{2,1,0:T(8,128)(2,1)S(1)}, bf16[1,256,5120]{2,1,0:T(8,128)(2,1)}, u32[]{:S(2)}) copy-start(bf16[1,256,5120]{2,1,0:T(8,128)(2,1)} %param.9) | copy-start | bytes 7864324
  20.4 10.5 %collective-permute-start.2 = (bf16[256,128]{1,0:T(8,128)(2,1)S(1)}, bf16[256,128]{1,0:T(8,128)(2,1)S(1)}, u32[]{:S(2)}, u32[]{:S(2)}) collective-permute-start(bf16[256,128]{1,0:T(8,128)(2,1)S(1)} %fusion.after_ref), channel_id=1, source_target_pairs={{0,240},{16,0},{32,16},{48,32},{64,48},{80,64},{96,80},{112,96},{1... | collective-permute-start | bytes 196616 | tf_op jit(solution)/shard_map/ppermute | solution.py:220
  22.0 1.1 copy-start.4
  31.0 20.0 %collective-permute-start.5 = (bf16[256,2560]{1,0:T(8,128)(2,1)}, bf16[256,2560]{1,0:T(8,128)(2,1)}, u32[]{:S(2)}, u32[]{:S(2)}) collective-permute-start(bf16[256,2560]{1,0:T(8,128)(2,1)} %get-tuple-element.37.refs_0_), channel_id=1, source_target_pairs={{0,240},{16,0},{32,16},{48,32},{64,48},{80,64},{96,80},{112,96},{1... | collective-permute-start | bytes 3932168 | tf_op jit(solution)/shard_map/ppermute | solution.py:220
  41.8 1.8 %copy-start.6 = (bf16[5120,128]{1,0:T(8,128)(2,1)}, bf16[5120,128]{1,0:T(8,128)(2,1)S(1)}, u32[]{:S(2)}) copy-start(bf16[5120,128]{1,0:T(8,128)(2,1)S(1)} %get-tuple-element.46) | copy-start | bytes 3932164
  43.5 10.0 %collective-permute-start.3 = (bf16[2,160,256]{2,1,0:T(8,128)(2,1)}, bf16[2,160,256]{2,1,0:T(8,128)(2,1)S(1)}, u32[]{:S(2)}, u32[]{:S(2)}) collective-permute-start(bf16[2,160,256]{2,1,0:T(8,128)(2,1)} %get-tuple-element.89), channel_id=1, source_target_pairs={{0,1},{1,2},{2,3},{3,4},{4,5},{5,6},{6,7},{7,0},{8,9},{9,10},{10,1... | collective-permute-start | bytes 491528 | tf_op jit(solution)/shard_map/ppermute | solution.py:226
  45.5 8.1 %collective-permute-start.4 = (bf16[2,160,256]{2,1,0:T(8,128)(2,1)}, bf16[2,160,256]{2,1,0:T(8,128)(2,1)}, u32[]{:S(2)}, u32[]{:S(2)}) collective-permute-start(bf16[2,160,256]{2,1,0:T(8,128)(2,1)} %get-tuple-element.88), channel_id=1, source_target_pairs={{0,7},{1,0},{2,1},{3,2},{4,3},{5,4},{6,5},{7,6},{8,15},{9,8},{10,9... | collective-permute-start | bytes 491528 | tf_op jit(solution)/shard_map/ppermute | solution.py:226
  49.4 19.0 %collective-permute-start.15 = (bf16[256,2560]{1,0:T(8,128)(2,1)}, bf16[256,2560]{1,0:T(8,128)(2,1)S(1)}, u32[]{:S(2)}, u32[]{:S(2)}) collective-permute-start(bf16[256,2560]{1,0:T(8,128)(2,1)} %copy-done.4), channel_id=1, source_target_pairs={{0,240},{16,0},{32,16},{48,32},{64,48},{80,64},{96,80},{112,96},{1... | collective-permute-start | bytes 3932168 | tf_op jit(solution)/shard_map/ppermute | solution.py:220
  56.2 4.0 %copy-start.8 = (bf16[2,320,256]{2,1,0:T(8,128)(2,1)S(1)}, bf16[2,320,256]{2,1,0:T(8,128)(2,1)}, u32[]{:S(2)}) copy-start(bf16[2,320,256]{2,1,0:T(8,128)(2,1)} %get-tuple-element.61) | copy-start | bytes 983044
  56.2 3.9 %copy-start.9 = (bf16[2,320,256]{2,1,0:T(8,128)(2,1)S(1)}, bf16[2,320,256]{2,1,0:T(8,128)(2,1)}, u32[]{:S(2)}) copy-start(bf16[2,320,256]{2,1,0:T(8,128)(2,1)} %get-tuple-element.63) | copy-start | bytes 983044
  56.2 7.1 %copy-start = (bf16[1,5120,384]{2,1,0:T(8,128)(2,1)S(1)}, bf16[1,5120,384]{2,1,0:T(8,128)(2,1)}, u32[]{:S(2)}) copy-start(bf16[1,5120,384]{2,1,0:T(8,128)(2,1)} %param.7) | copy-start | bytes 11796484
  56.3 10.0 %collective-permute-start.13 = (bf16[2,160,256]{2,1,0:T(8,128)(2,1)S(1)}, bf16[2,160,256]{2,1,0:T(8,128)(2,1)S(1)}, u32[]{:S(2)}, u32[]{:S(2)}) collective-permute-start(bf16[2,160,256]{2,1,0:T(8,128)(2,1)S(1)} %get-tuple-element.87), channel_id=1, source_target_pairs={{0,1},{1,2},{2,3},{3,4},{4,5},{5,6},{6,7},{7,0},{8,9},{9,10},{10,1... | collective-permute-start | bytes 491528 | tf_op jit(solution)/shard_map/ppermute | solution.py:226
  56.9 11.4 %collective-permute-start.14 = (bf16[2,160,256]{2,1,0:T(8,128)(2,1)S(1)}, bf16[2,160,256]{2,1,0:T(8,128)(2,1)S(1)}, u32[]{:S(2)}, u32[]{:S(2)}) collective-permute-start(bf16[2,160,256]{2,1,0:T(8,128)(2,1)S(1)} %get-tuple-element.86), channel_id=1, source_target_pairs={{0,7},{1,0},{2,1},{3,2},{4,3},{5,4},{6,5},{7,6},{8,15},{9,8},{10,9... | collective-permute-start | bytes 491528 | tf_op jit(solution)/shard_map/ppermute | solution.py:226
  61.2 10.2 %collective-permute-start.8 = (bf16[2,320,256]{2,1,0:T(8,128)(2,1)S(1)}, bf16[2,320,256]{2,1,0:T(8,128)(2,1)S(1)}, u32[]{:S(2)}, u32[]{:S(2)}) collective-permute-start(bf16[2,320,256]{2,1,0:T(8,128)(2,1)S(1)} %pad_maximum_fusion.2), channel_id=1, source_target_pairs={{0,7},{1,0},{2,1},{3,2},{4,3},{5,4},{6,5},{7,6},{8,15},{9,8},{10,9... | collective-permute-start | bytes 983048 | tf_op jit(solution)/shard_map/ppermute | solution.py:226
  63.2 23.9 %collective-permute-start.6 = (bf16[2,320,256]{2,1,0:T(8,128)(2,1)S(1)}, bf16[2,320,256]{2,1,0:T(8,128)(2,1)S(1)}, u32[]{:S(2)}, u32[]{:S(2)}) collective-permute-start(bf16[2,320,256]{2,1,0:T(8,128)(2,1)S(1)} %pad_maximum_fusion.1), channel_id=1, source_target_pairs={{0,1},{1,2},{2,3},{3,4},{4,5},{5,6},{6,7},{7,0},{8,9},{9,10},{10,1... | collective-permute-start | bytes 983048 | tf_op jit(solution)/shard_map/ppermute | solution.py:226
  66.3 40.7 %collective-permute-start.10 = (bf16[256,5120]{1,0:T(8,128)(2,1)}, bf16[256,5120]{1,0:T(8,128)(2,1)}, u32[]{:S(2)}, u32[]{:S(2)}) collective-permute-start(bf16[256,5120]{1,0:T(8,128)(2,1)} %far_term.1), channel_id=1, source_target_pairs={{0,16},{16,32},{32,48},{48,64},{64,80},{80,96},{96,112},{112,128},... | collective-permute-start | bytes 7864328 | tf_op jit(solution)/shard_map/ppermute | solution.py:220
  68.3 6.5 %copy-start.5 = (bf16[256,2560]{1,0:T(8,128)(2,1)S(1)}, bf16[256,2560]{1,0:T(8,128)(2,1)}, u32[]{:S(2)}) copy-start(bf16[256,2560]{1,0:T(8,128)(2,1)} %copy-done.4) | copy-start | bytes 3932164
  68.4 8.9 %collective-permute-start.19 = (bf16[2,320,256]{2,1,0:T(8,128)(2,1)S(1)}, bf16[2,320,256]{2,1,0:T(8,128)(2,1)S(1)}, u32[]{:S(2)}, u32[]{:S(2)}) collective-permute-start(bf16[2,320,256]{2,1,0:T(8,128)(2,1)S(1)} %pad_maximum_fusion.3), channel_id=1, source_target_pairs={{0,7},{1,0},{2,1},{3,2},{4,3},{5,4},{6,5},{7,6},{8,15},{9,8},{10,9... | collective-permute-start | bytes 983048 | tf_op jit(solution)/shard_map/ppermute | solution.py:226
  71.4 15.7 %collective-permute-start.9 = (bf16[2,320,256]{2,1,0:T(8,128)(2,1)S(1)}, bf16[2,320,256]{2,1,0:T(8,128)(2,1)S(1)}, u32[]{:S(2)}, u32[]{:S(2)}) collective-permute-start(bf16[2,320,256]{2,1,0:T(8,128)(2,1)S(1)} %bitcast_add_fusion.1), channel_id=1, source_target_pairs={{0,7},{1,0},{2,1},{3,2},{4,3},{5,4},{6,5},{7,6},{8,15},{9,8},{10,9... | collective-permute-start | bytes 983048 | tf_op jit(solution)/shard_map/ppermute | solution.py:226
  75.7 11.2 %collective-permute-start.16 = (bf16[2,320,256]{2,1,0:T(8,128)(2,1)S(1)}, bf16[2,320,256]{2,1,0:T(8,128)(2,1)S(1)}, u32[]{:S(2)}, u32[]{:S(2)}) collective-permute-start(bf16[2,320,256]{2,1,0:T(8,128)(2,1)S(1)} %fusion.7), channel_id=1, source_target_pairs={{0,1},{1,2},{2,3},{3,4},{4,5},{5,6},{6,7},{7,0},{8,9},{9,10},{10,1... | collective-permute-start | bytes 983048 | tf_op jit(solution)/shard_map/ppermute | solution.py:226
  77.5 14.0 %collective-permute-start.20 = (bf16[2,320,256]{2,1,0:T(8,128)(2,1)S(1)}, bf16[2,320,256]{2,1,0:T(8,128)(2,1)S(1)}, u32[]{:S(2)}, u32[]{:S(2)}) collective-permute-start(bf16[2,320,256]{2,1,0:T(8,128)(2,1)S(1)} %maximum_add_fusion.3), channel_id=1, source_target_pairs={{0,7},{1,0},{2,1},{3,2},{4,3},{5,4},{6,5},{7,6},{8,15},{9,8},{10,9... | collective-permute-start | bytes 983048 | tf_op jit(solution)/shard_map/ppermute | solution.py:226
  87.0 11.9 %collective-permute-start.17 = (bf16[2,320,256]{2,1,0:T(8,128)(2,1)S(1)}, bf16[2,320,256]{2,1,0:T(8,128)(2,1)S(1)}, u32[]{:S(2)}, u32[]{:S(2)}) collective-permute-start(bf16[2,320,256]{2,1,0:T(8,128)(2,1)S(1)} %maximum_add_fusion.1), channel_id=1, source_target_pairs={{0,1},{1,2},{2,3},{3,4},{4,5},{5,6},{6,7},{7,0},{8,9},{9,10},{10,1... | collective-permute-start | bytes 983048 | tf_op jit(solution)/shard_map/ppermute | solution.py:226
  88.1 18.0 %collective-permute-start.7 = (bf16[2,320,256]{2,1,0:T(8,128)(2,1)}, bf16[2,320,256]{2,1,0:T(8,128)(2,1)}, u32[]{:S(2)}, u32[]{:S(2)}) collective-permute-start(bf16[2,320,256]{2,1,0:T(8,128)(2,1)} %get-tuple-element.60), channel_id=1, source_target_pairs={{0,1},{1,2},{2,3},{3,4},{4,5},{5,6},{6,7},{7,0},{8,9},{9,10},{10,1... | collective-permute-start | bytes 983048 | tf_op jit(solution)/shard_map/ppermute | solution.py:226
  92.2 17.0 %collective-permute-start.21 = (bf16[2,320,256]{2,1,0:T(8,128)(2,1)}, bf16[2,320,256]{2,1,0:T(8,128)(2,1)}, u32[]{:S(2)}, u32[]{:S(2)}) collective-permute-start(bf16[2,320,256]{2,1,0:T(8,128)(2,1)} %maximum_add_fusion.2), channel_id=1, source_target_pairs={{0,7},{1,0},{2,1},{3,2},{4,3},{5,4},{6,5},{7,6},{8,15},{9,8},{10,9... | collective-permute-start | bytes 983048 | tf_op jit(solution)/shard_map/ppermute | solution.py:226
  99.8 13.3 %collective-permute-start.18 = (bf16[2,320,256]{2,1,0:T(8,128)(2,1)}, bf16[2,320,256]{2,1,0:T(8,128)(2,1)}, u32[]{:S(2)}, u32[]{:S(2)}) collective-permute-start(bf16[2,320,256]{2,1,0:T(8,128)(2,1)} %maximum_add_fusion), channel_id=1, source_target_pairs={{0,1},{1,2},{2,3},{3,4},{4,5},{5,6},{6,7},{7,0},{8,9},{9,10},{10,1... | collective-permute-start | bytes 983048 | tf_op jit(solution)/shard_map/ppermute | solution.py:226
  107.1 14.2 %collective-permute-start.12 = (bf16[2,320,256]{2,1,0:T(8,128)(2,1)}, bf16[2,320,256]{2,1,0:T(8,128)(2,1)S(1)}, u32[]{:S(2)}, u32[]{:S(2)}) collective-permute-start(bf16[2,320,256]{2,1,0:T(8,128)(2,1)} %get-tuple-element.45), channel_id=1, source_target_pairs={{0,7},{1,0},{2,1},{3,2},{4,3},{5,4},{6,5},{7,6},{8,15},{9,8},{10,9... | collective-permute-start | bytes 983048 | tf_op jit(solution)/shard_map/ppermute | solution.py:226
  107.2 14.1 %collective-permute-start.11 = (bf16[2,320,256]{2,1,0:T(8,128)(2,1)S(1)}, bf16[2,320,256]{2,1,0:T(8,128)(2,1)S(1)}, u32[]{:S(2)}, u32[]{:S(2)}) collective-permute-start(bf16[2,320,256]{2,1,0:T(8,128)(2,1)S(1)} %bitcast_add_fusion.4), channel_id=1, source_target_pairs={{0,1},{1,2},{2,3},{3,4},{4,5},{5,6},{6,7},{7,0},{8,9},{9,10},{10,1... | collective-permute-start | bytes 983048 | tf_op jit(solution)/shard_map/ppermute | solution.py:226
  114.3 2.1 %copy-start.1 = (bf16[1,5120,384]{2,1,0:T(8,128)(2,1)S(1)}, bf16[1,5120,384]{2,1,0:T(8,128)(2,1)}, u32[]{:S(2)}) copy-start(bf16[1,5120,384]{2,1,0:T(8,128)(2,1)} %param.7) | copy-start | bytes 11796484
  121.6 8.7 %collective-permute-start.22 = (bf16[320,512]{1,0:T(8,128)(2,1)S(1)}, bf16[320,512]{1,0:T(8,128)(2,1)S(1)}, u32[]{:S(2)}, u32[]{:S(2)}) collective-permute-start(bf16[320,512]{1,0:T(8,128)(2,1)S(1)} %fusion.5), channel_id=1, source_target_pairs={{0,8},{1,9},{2,10},{3,11},{4,12},{5,13},{6,14},{7,15},{8,0},{9,1},... | collective-permute-start | bytes 983048 | tf_op jit(solution)/shard_map/ppermute | solution.py:231

commit v3 on v2

--- a/solution.py
+++ b/solution.py
@@ -45,7 +45,9 @@
 
 def whole(kernel, name, limit, args, in_hbm, outs, scratch=(), flops=1):
     here = pl.BlockSpec(memory_space=pltpu.VMEM)
-    there = pl.BlockSpec(memory_space=pltpu.HBM)
+    there = pl.BlockSpec(memory_space=pl.ANY)
+    split = len(args) - in_hbm
+    args = [*args[:split], *(pltpu.with_memory_space_constraint(a, pltpu.HBM) for a in args[split:])]
     return pl.pallas_call(
         kernel,
         in_specs=[here] * (len(args) - in_hbm) + [there] * in_hbm,
@@ -89,7 +91,7 @@
 
 N_W = 4
 TILE = 1280
-SMALL, LARGE = 14, 48
+SMALL, LARGE = 14, 20
 
 
 def own_kernel(
@@ -200,19 +202,89 @@
     )
 
 
-def term_kernel(d_ref, w_ref, *rest):
-    out_ref = rest[-1]
+def term_kernel(d_ref, w_ref, out_ref):
     for start in range(0, w_ref.shape[0], TILE):
         total = dot(d_ref[...], w_ref[start : start + TILE], 1, 1)
-        if len(rest) == 2:
-            total += rest[0][:, start : start + TILE].astype(F32)
         out_ref[:, start : start + TILE] = total.astype(BF)
 
 
-def term(d, w, *far):
-    name = "sum_term" if far else "far_term"
+def far_term(d, w):
     out = shape((d.shape[0], w.shape[0]))
-    return whole(term_kernel, name, SMALL, (d, w, *far), 0, [out], (), 4 * d.shape[0] * w.size)[0]
+    return whole(term_kernel, "far_term", SMALL, (d, w), 0, [out], (), 4 * d.shape[0] * w.size)[0]
+
+
+def own_term_kernel(d_ref, w_hbm, out_hbm, w_ref, out_ref, w_sem, sem):
+    w_copies = fetch_rows(N_W, w_hbm, w_ref, w_sem)
+    for copy in w_copies:
+        copy.start()
+    tile = w_ref.shape[0] // N_W
+    for i, copy in enumerate(w_copies):
+        copy.wait()
+        part = slice(i * tile, (i + 1) * tile)
+        out_ref[:, part] = dot(d_ref[...], w_ref[part], 1, 1).astype(BF)
+    out_copy = pltpu.make_async_copy(out_ref, out_hbm, sem)
+    out_copy.start()
+    out_copy.wait()
+
+
+def own_term(d, w):
+    dims = (d.shape[0], w.shape[0])
+    return pl.pallas_call(
+        own_term_kernel,
+        in_specs=[pl.BlockSpec(memory_space=pltpu.VMEM), pl.BlockSpec(memory_space=pl.ANY)],
+        out_specs=pl.BlockSpec(memory_space=pl.ANY),
+        out_shape=pltpu.HBM(dims, BF),
+        scratch_shapes=[
+            pltpu.VMEM(w.shape, BF),
+            pltpu.VMEM(dims, BF),
+            pltpu.SemaphoreType.DMA((N_W,)),
+            pltpu.SemaphoreType.DMA,
+        ],
+        compiler_params=pltpu.CompilerParams(vmem_limit_bytes=LARGE * 1024 * 1024),
+        cost_estimate=pl.CostEstimate(flops=1, bytes_accessed=1, transcendentals=0),
+        name="own_term",
+    )(d, pltpu.with_memory_space_constraint(w, pltpu.HBM))
+
+
+def sum_kernel(far_ref, own_hbm, out_hbm, own_ref, out_ref, in_sem, out_sem):
+    count, model = own_ref.shape
+    n = model // TILE
+    parts = [(slice(None), pl.ds(i * TILE, TILE)) for i in range(n)]
+    ins = [
+        pltpu.make_async_copy(own_hbm.at[p], own_ref.at[p], in_sem.at[i]) for i, p in enumerate(parts)
+    ]
+    outs = [
+        pltpu.make_async_copy(out_ref.at[p], out_hbm.at[p], out_sem.at[i]) for i, p in enumerate(parts)
+    ]
+    for copy in ins:
+        copy.start()
+    for i in range(n):
+        ins[i].wait()
+        part = slice(i * TILE, (i + 1) * TILE)
+        total = own_ref[:, part].astype(F32) + far_ref[:, part].astype(F32)
+        out_ref[:, part] = total.astype(BF)
+        outs[i].start()
+    for copy in outs:
+        copy.wait()
+
+
+def sum_of(own, far):
+    steps = own.shape[1] // TILE
+    return pl.pallas_call(
+        sum_kernel,
+        in_specs=[pl.BlockSpec(memory_space=pltpu.VMEM), pl.BlockSpec(memory_space=pl.ANY)],
+        out_specs=pl.BlockSpec(memory_space=pl.ANY),
+        out_shape=pltpu.HBM(own.shape, BF),
+        scratch_shapes=[
+            pltpu.VMEM(own.shape, BF),
+            pltpu.VMEM(own.shape, BF),
+            pltpu.SemaphoreType.DMA((steps,)),
+            pltpu.SemaphoreType.DMA((steps,)),
+        ],
+        compiler_params=pltpu.CompilerParams(vmem_limit_bytes=SMALL * 1024 * 1024),
+        cost_estimate=pl.CostEstimate(flops=2 * 10**9, bytes_accessed=1, transcendentals=0),
+        name="sum_term",
+    )(far, pltpu.with_memory_space_constraint(own, pltpu.HBM))
 
 
 def shifted(block, distance):
@@ -288,7 +360,8 @@
     together = lax.optimization_barrier
     split = lambda grad: grad.reshape(2, N_Z, rows, grad.shape[1])
     d_qkv, att = own_pair(x, wq, g, wo, seg)
-    wo_back, d_qkv = together((wo_back, d_qkv))
+    term_own = own_term(d_qkv, wq)
+    wo_back, d_qkv, term_own = together((wo_back, d_qkv, term_own))
     d_att_home = dot(g, wo_back, 1, 1).astype(BF)
     d_att_far = shifted(d_att_home, -1)
     columns = columns_of(g, d_att_home)
@@ -314,12 +387,11 @@
         return jnp.concatenate([entry(grad_v, distance), grad_o], axis=2)
 
     sent = z_send(payload(first, 1, None))
-    sent, columns_far[0] = together((sent, columns_far[0]))
     terms = near = terms_o(0)
     sent_2 = z_send(payload(second, 1, None))
     load, d_qkv_far = together((payload(first, 2, sent), d_qkv_far))
     sent = z_send(load)
-    term_back = shifted(term(d_qkv_far, wq), 1)
+    term_back = shifted(far_term(d_qkv_far, wq), 1)
     load, columns_far[1] = together((payload(second, 2, sent_2), columns_far[1]))
     sent_2 = z_send(load)
     terms = jnp.concatenate([near, terms_o(1)], axis=1)
@@ -328,9 +400,8 @@
     load, term_back = together((payload(first, 4, sent), term_back))
     sent = z_send(load)
     sent_2 = z_send(payload(second, 4, sent_2))
-    input_grad = term(d_qkv, wq, term_back)
     ends = jnp.concatenate([z_end(first, sent), z_end(second, sent_2)], axis=2)
-    ends, input_grad = together((ends, input_grad))
+    ends, input_grad = together((ends, sum_of(term_own, term_back)))
     total = x_end(ends, x_hi).astype(BF)
     return input_grad[None], total[:, : 3 * head][None], total[:, 3 * head :].T[None]
 

time: 132 us -> 128 us (0.970)
  local copies, waits for them, and re-layouts: 12 us -> 3.81 us
  Pallas kernels: 27.7 us -> 32.8 us
  other arithmetic: 6.86 us -> 3.53 us
    pallas_call x0 -> x2, Pallas kernels: none -> 9.83 us  [the longest x1 5.3 us: own_term(): pl.pallas_call(own_term_kernel, in_specs=[pl.BlockSpec(memory_space=pltpu...]
    unnamed x20 -> x10, local copies, waits for them, and re-layouts: 6.25 us -> 1.11 us
    pallas_call x7 -> x6, Pallas kernels: 27.7 us -> 23 us  [whole(): pl.pallas_call(kernel, in_specs=[here] * (len(args) - in_hbm) + [there] *...]
    ppermute x6, starting transfers between devices: 4.46 us -> 7.6 us  [shifted(): lax.ppermute(block, 'blk', [(i, (i + distance) % n) for i in range(n)])]
    ppermute x1, waiting for transfers between devices: 8.07 us -> 11 us  [x_swapped(): return lax.ppermute(block, 'dp', [(i, (i + N_Z) % n) for i in range(n)])]
    squeeze x2, local copies, waits for them, and re-layouts: 2.5 us -> 0.17 us  [entry(): lax.dynamic_index_in_dim(part, (z + distance) % N_Z, 1, keepdims=False)]
    add x7, other arithmetic: 3.77 us -> 1.45 us  [payload(): return (at(5 - step) + up, at(step - 5) + down)]
    ppermute x6, waiting for transfers between devices: 14.8 us -> 12.5 us  [shifted(): lax.ppermute(block, 'blk', [(i, (i + distance) % n) for i in range(n)])]
  transfers between devices with their start and end apart: 23 -> 23, of which waited for: 10 -> 12; matrix products, arithmetic and copies ran while one was open for 10% -> 4% of each run, Pallas kernels for 21% -> 26%
where the time goes in v3:
time: 128 us; the launch traced here: 127 us
  waiting for transfers between devices  48.6 us (38%)
  starting transfers between devices  35.3 us (28%)
  Pallas kernels  32.8 us (26%)
  local copies, waits for them, and re-layouts  3.81 us (3%)
  other arithmetic  3.53 us (3%)
  matrix products  2.15 us (2%)
    ppermute x16, starting transfers between devices, z_shifted(): return lax.ppermute(block, 'dp', route)  27.1 us
    ppermute x16, waiting for transfers between devices, z_shifted(): return lax.ppermute(block, 'dp', route)  25 us
    pallas_call x6, Pallas kernels, whole(): pl.pallas_call(kernel, in_specs=[here] * (len(args) - in_hbm) + [there] *...  23 us
    ppermute x6, waiting for transfers between devices, shifted(): lax.ppermute(block, 'blk', [(i, (i + distance) % n) for i in range(n)])  12.5 us
    ppermute x1, waiting for transfers between devices, x_swapped(): return lax.ppermute(block, 'dp', [(i, (i + N_Z) % n) for i in range(n)])  11 us
    ppermute x6, starting transfers between devices, shifted(): lax.ppermute(block, 'blk', [(i, (i + distance) % n) for i in range(n)])  7.6 us
    pallas_call x1, Pallas kernels, own_term(): pl.pallas_call(own_term_kernel, in_specs=[pl.BlockSpec(memory_space=pltpu...  5.3 us
    pallas_call x1, Pallas kernels, sum_of(): pl.pallas_call(sum_kernel, in_specs=[pl.BlockSpec(memory_space=pltpu.VMEM...  4.53 us
  transfers between devices with their start and end apart: 23, of which 12 were waited for; matrix products, arithmetic and copies ran while one was open for 4% of the time, Pallas kernels for 26%

profile of v3, /device:TPU:28, one launch (start us, length us, event | category | flops | bytes accessed | tf_op | source)
XLA Modules:
  0.0 127.3 jit_solution(3938638907394186063)
XLA Ops:
  0.6 0.3 collective-permute-start
  0.9 0.3 collective-permute-start.1
  1.2 0.8 fusion.25
  2.0 0.1 copy.10.seg_col_ref
  2.1 6.5 %own_pair.1 = (bf16[256,384]{1,0:T(8,128)(2,1)S(1)}, bf16[256,128]{1,0:T(8,128)(2,1)S(1)}) custom-call(s32[1,256]{1,0:T(1,128)S(1)} %get-tuple-element.89.seg_row_ref, s32[256,1]{1,0:T(8,128)S(1)} %copy.10.seg_col_ref, bf16[256,5120]{1,0:T(8,128)(2,1)} %bitcast.101, bf16[5120,384]{1,0:T(8,128)(2,1)} %bitcast.85, bf16[256,5120]{1,0:T(8,128)(2,1)} %bitcast.98, ...), custom_call_target="tpu_custom_call" | custom-call | flops 1 | bytes 1 | tf_op jit(solution)/shard_map/own_pair/pallas_call | solution.py:51
  8.7 5.3 %own_term.1.own_hbm = bf16[256,5120]{1,0:T(8,128)(2,1)} custom-call(bf16[256,384]{1,0:T(8,128)(2,1)S(1)} %get-tuple-element.33.d_ref, bf16[5120,384]{1,0:T(8,128)(2,1)} %bitcast.86), custom_call_target="tpu_custom_call" | custom-call | flops 1 | bytes 1 | tf_op jit(solution)/shard_map/own_term/pallas_call | solution.py:232
  14.0 4.2 %collective-permute-done.1 = bf16[128,5120]{1,0:T(8,128)(2,1)} collective-permute-done((bf16[128,5120]{1,0:T(8,128)(2,1)}, bf16[128,5120]{1,0:T(8,128)(2,1)}, u32[]{:S(2)}, u32[]{:S(2)}) %collective-permute-start.1) | collective-permute-done | bytes 1310752 | tf_op jit(solution)/shard_map/ppermute | solution.py:292
  18.2 2.2 %fusion.after_ref = bf16[256,128]{1,0:T(8,128)(2,1)S(1)} fusion(bf16[128,5120]{1,0:T(8,128)(2,1)} %collective-permute-done.1, bf16[1,256,5120]{2,1,0:T(8,128)(2,1)S(1)} %copy-done.4), kind=kOutput, calls=%fused_computation.12 | convolution fusion | flops 335577088 | bytes 3997696 | tf_op jit(solution)/shard_map/dot_general | solution.py:16
  20.4 0.1 collective-permute-start.2
  20.5 2.8 %columns.1 = (bf16[256,2560]{1,0:T(8,128)(2,1)}, bf16[256,2560]{1,0:T(8,128)(2,1)S(1)}) custom-call(bf16[256,128]{1,0:T(8,128)(2,1)S(1)} %fusion.after_ref, bf16[256,5120]{1,0:T(8,128)(2,1)} %bitcast.99), custom_call_target="tpu_custom_call" | custom-call | flops 1 | bytes 1 | tf_op jit(solution)/shard_map/columns/pallas_call | solution.py:51
  23.4 1.1 copy-done.2
  24.4 6.5 %collective-permute-done.2.datt_ref = bf16[256,128]{1,0:T(8,128)(2,1)S(1)} collective-permute-done((bf16[256,128]{1,0:T(8,128)(2,1)S(1)}, bf16[256,128]{1,0:T(8,128)(2,1)S(1)}, u32[]{:S(2)}, u32[]{:S(2)}) %collective-permute-start.2) | collective-permute-done | bytes 65568 | tf_op jit(solution)/shard_map/ppermute | solution.py:292
  31.0 1.9 %collective-permute-start.12 = (bf16[256,2560]{1,0:T(8,128)(2,1)}, bf16[256,2560]{1,0:T(8,128)(2,1)}, u32[]{:S(2)}, u32[]{:S(2)}) collective-permute-start(bf16[256,2560]{1,0:T(8,128)(2,1)} %get-tuple-element.43.refs_0_), channel_id=1, source_target_pairs={{0,240},{16,0},{32,16},{48,32},{64,48},{80,64},{96,80},{112,96},{1... | collective-permute-start | bytes 3932168 | tf_op jit(solution)/shard_map/ppermute | solution.py:292
  32.9 0.1 copy.12.seg_col_ref
  33.1 7.1 %far_pair.1 = (bf16[256,384]{1,0:T(8,128)(2,1)S(1)}, bf16[256,128]{1,0:T(8,128)(2,1)S(1)}, bf16[5120,256]{1,0:T(8,128)(2,1)S(1)}, bf16[5120,128]{1,0:T(8,128)(2,1)S(1)}) custom-call(bf16[256,5120]{1,0:T(8,128)(2,1)S(1)} %collective-permute-done.xf_ref, bf16[256,128]{1,0:T(8,128)(2,1)S(1)} %collective-permute-done.2.datt_ref, ...), custom_call_target="tpu_custom_call" | custom-call | flops 1 | bytes 1 | tf_op jit(solution)/shard_map/far_pair/pallas_call | solution.py:51
  40.3 0.1 collective-permute-start.15
  40.3 0.1 dynamic-slice_bitcast_fusion
  40.5 2.0 %collective-permute-start.3 = (bf16[2,160,256]{2,1,0:T(8,128)(2,1)S(1)}, bf16[2,160,256]{2,1,0:T(8,128)(2,1)S(1)}, u32[]{:S(2)}, u32[]{:S(2)}) collective-permute-start(bf16[2,160,256]{2,1,0:T(8,128)(2,1)S(1)} %get-tuple-element.79), channel_id=1, source_target_pairs={{0,1},{1,2},{2,3},{3,4},{4,5},{5,6},{6,7},{7,0},{8,9},{9,10},{10,1... | collective-permute-start | bytes 491528 | tf_op jit(solution)/shard_map/ppermute | solution.py:298
  42.5 4.0 %collective-permute-start.4 = (bf16[2,160,256]{2,1,0:T(8,128)(2,1)S(1)}, bf16[2,160,256]{2,1,0:T(8,128)(2,1)S(1)}, u32[]{:S(2)}, u32[]{:S(2)}) collective-permute-start(bf16[2,160,256]{2,1,0:T(8,128)(2,1)S(1)} %get-tuple-element.78), channel_id=1, source_target_pairs={{0,7},{1,0},{2,1},{3,2},{4,3},{5,4},{6,5},{7,6},{8,15},{9,8},{10,9... | collective-permute-start | bytes 491528 | tf_op jit(solution)/shard_map/ppermute | solution.py:298
  46.5 0.1 dynamic-slice_bitcast_fusion.13
  46.6 1.7 %collective-permute-done.12.refs_2_ = bf16[256,2560]{1,0:T(8,128)(2,1)} collective-permute-done((bf16[256,2560]{1,0:T(8,128)(2,1)}, bf16[256,2560]{1,0:T(8,128)(2,1)}, u32[]{:S(2)}, u32[]{:S(2)}) %collective-permute-start.12) | collective-permute-done | bytes 1310752 | tf_op jit(solution)/shard_map/ppermute | solution.py:292
  48.3 2.6 %grads_out.2 = bf16[2560,128]{1,0:T(8,128)(2,1)S(1)} custom-call(bf16[256,2560]{1,0:T(8,128)(2,1)} %get-tuple-element.43.refs_0_, bf16[256,128]{1,0:T(8,128)(2,1)S(1)} %get-tuple-element.42.refs_1_, bf16[256,2560]{1,0:T(8,128)(2,1)} %collective-permute-done.12.refs_2_, bf16[256,128]{1,0:T(8,128)(2,1)S(1)} %get-tuple-element.46.refs_3_), custom_call_target="tpu_custom_call" | custom-call | flops 1 | bytes 1 | tf_op jit(solution)/shard_map/grads_out/pallas_call | solution.py:51
  51.0 2.0 %collective-permute-start.13 = (bf16[2,160,256]{2,1,0:T(8,128)(2,1)S(1)}, bf16[2,160,256]{2,1,0:T(8,128)(2,1)S(1)}, u32[]{:S(2)}, u32[]{:S(2)}) collective-permute-start(bf16[2,160,256]{2,1,0:T(8,128)(2,1)S(1)} %get-tuple-element.85), channel_id=1, source_target_pairs={{0,1},{1,2},{2,3},{3,4},{4,5},{5,6},{6,7},{7,0},{8,9},{9,10},{10,1... | collective-permute-start | bytes 491528 | tf_op jit(solution)/shard_map/ppermute | solution.py:298
  53.0 4.0 %collective-permute-start.14 = (bf16[2,160,256]{2,1,0:T(8,128)(2,1)S(1)}, bf16[2,160,256]{2,1,0:T(8,128)(2,1)S(1)}, u32[]{:S(2)}, u32[]{:S(2)}) collective-permute-start(bf16[2,160,256]{2,1,0:T(8,128)(2,1)S(1)} %get-tuple-element.84), channel_id=1, source_target_pairs={{0,7},{1,0},{2,1},{3,2},{4,3},{5,4},{6,5},{7,6},{8,15},{9,8},{10,9... | collective-permute-start | bytes 491528 | tf_op jit(solution)/shard_map/ppermute | solution.py:298
  57.2 2.0 %collective-permute-start.7 = (bf16[2,320,256]{2,1,0:T(8,128)(2,1)S(1)}, bf16[2,320,256]{2,1,0:T(8,128)(2,1)S(1)}, u32[]{:S(2)}, u32[]{:S(2)}) collective-permute-start(bf16[2,320,256]{2,1,0:T(8,128)(2,1)S(1)} %get-tuple-element.37), channel_id=1, source_target_pairs={{0,7},{1,0},{2,1},{3,2},{4,3},{5,4},{6,5},{7,6},{8,15},{9,8},{10,9... | collective-permute-start | bytes 983048 | tf_op jit(solution)/shard_map/ppermute | solution.py:298
  59.2 0.1 collective-permute-start.5
  59.3 3.0 %far_term.1 = bf16[256,5120]{1,0:T(8,128)(2,1)} custom-call(bf16[256,384]{1,0:T(8,128)(2,1)S(1)} %get-tuple-element.38.d_ref, bf16[5120,384]{1,0:T(8,128)(2,1)S(1)} %bitcast.88), custom_call_target="tpu_custom_call" | custom-call | flops 2013265920 | bytes 1 | tf_op jit(solution)/shard_map/far_term/pallas_call | solution.py:51
  62.4 4.9 %collective-permute-start.9 = (bf16[256,5120]{1,0:T(8,128)(2,1)}, bf16[256,5120]{1,0:T(8,128)(2,1)}, u32[]{:S(2)}, u32[]{:S(2)}) collective-permute-start(bf16[256,5120]{1,0:T(8,128)(2,1)} %far_term.1), channel_id=1, source_target_pairs={{0,16},{16,32},{32,48},{48,64},{64,80},{80,96},{96,112},{112,128},... | collective-permute-start | bytes 7864328 | tf_op jit(solution)/shard_map/ppermute | solution.py:292
  67.4 0.1 fusion.13
  67.5 2.9 %collective-permute-start.19 = (bf16[2,320,256]{2,1,0:T(8,128)(2,1)S(1)}, bf16[2,320,256]{2,1,0:T(8,128)(2,1)S(1)}, u32[]{:S(2)}, u32[]{:S(2)}) collective-permute-start(bf16[2,320,256]{2,1,0:T(8,128)(2,1)S(1)} %pad_maximum_fusion.3), channel_id=1, source_target_pairs={{0,7},{1,0},{2,1},{3,2},{4,3},{5,4},{6,5},{7,6},{8,15},{9,8},{10,9... | collective-permute-start | bytes 983048 | tf_op jit(solution)/shard_map/ppermute | solution.py:298
  70.5 0.1 collective-permute-start.8
  70.6 0.9 grads_out.3
  71.5 2.1 %collective-permute-start.16 = (bf16[2,320,256]{2,1,0:T(8,128)(2,1)S(1)}, bf16[2,320,256]{2,1,0:T(8,128)(2,1)S(1)}, u32[]{:S(2)}, u32[]{:S(2)}) collective-permute-start(bf16[2,320,256]{2,1,0:T(8,128)(2,1)S(1)} %fusion.7), channel_id=1, source_target_pairs={{0,1},{1,2},{2,3},{3,4},{4,5},{5,6},{6,7},{7,0},{8,9},{9,10},{10,1... | collective-permute-start | bytes 983048 | tf_op jit(solution)/shard_map/ppermute | solution.py:298
  73.6 0.3 fusion.21
  73.9 4.3 %collective-permute-done.19 = bf16[2,320,256]{2,1,0:T(8,128)(2,1)S(1)} collective-permute-done((bf16[2,320,256]{2,1,0:T(8,128)(2,1)S(1)}, bf16[2,320,256]{2,1,0:T(8,128)(2,1)S(1)}, u32[]{:S(2)}, u32[]{:S(2)}) %collective-permute-start.19) | collective-permute-done | bytes 327712 | tf_op jit(solution)/shard_map/ppermute | solution.py:298
  78.2 0.1 maximum_add_fusion.3
  78.2 1.6 %collective-permute-start.20 = (bf16[2,320,256]{2,1,0:T(8,128)(2,1)S(1)}, bf16[2,320,256]{2,1,0:T(8,128)(2,1)S(1)}, u32[]{:S(2)}, u32[]{:S(2)}) collective-permute-start(bf16[2,320,256]{2,1,0:T(8,128)(2,1)S(1)} %maximum_add_fusion.3), channel_id=1, source_target_pairs={{0,7},{1,0},{2,1},{3,2},{4,3},{5,4},{6,5},{7,6},{8,15},{9,8},{10,9... | collective-permute-start | bytes 983048 | tf_op jit(solution)/shard_map/ppermute | solution.py:298
  79.9 0.5 collective-permute-done.16
  80.4 0.1 maximum_add_fusion.1
  80.5 1.8 %collective-permute-start.17 = (bf16[2,320,256]{2,1,0:T(8,128)(2,1)S(1)}, bf16[2,320,256]{2,1,0:T(8,128)(2,1)S(1)}, u32[]{:S(2)}, u32[]{:S(2)}) collective-permute-start(bf16[2,320,256]{2,1,0:T(8,128)(2,1)S(1)} %maximum_add_fusion.1), channel_id=1, source_target_pairs={{0,1},{1,2},{2,3},{3,4},{4,5},{5,6},{6,7},{7,0},{8,9},{9,10},{10,1... | collective-permute-start | bytes 983048 | tf_op jit(solution)/shard_map/ppermute | solution.py:298
  82.3 2.9 %collective-permute-done.8 = bf16[2,320,256]{2,1,0:T(8,128)(2,1)S(1)} collective-permute-done((bf16[2,320,256]{2,1,0:T(8,128)(2,1)S(1)}, bf16[2,320,256]{2,1,0:T(8,128)(2,1)S(1)}, u32[]{:S(2)}, u32[]{:S(2)}) %collective-permute-start.8) | collective-permute-done | bytes 327712 | tf_op jit(solution)/shard_map/ppermute | solution.py:298
  85.2 0.1 bitcast_add_fusion.2
  85.3 0.1 collective-permute-start.6
  85.4 6.5 %collective-permute-done.20 = bf16[2,320,256]{2,1,0:T(8,128)(2,1)S(1)} collective-permute-done((bf16[2,320,256]{2,1,0:T(8,128)(2,1)S(1)}, bf16[2,320,256]{2,1,0:T(8,128)(2,1)S(1)}, u32[]{:S(2)}, u32[]{:S(2)}) %collective-permute-start.20) | collective-permute-done | bytes 327712 | tf_op jit(solution)/shard_map/ppermute | solution.py:298
  91.9 0.1 maximum_add_fusion.2
  92.0 1.9 %collective-permute-start.21 = (bf16[2,320,256]{2,1,0:T(8,128)(2,1)S(1)}, bf16[2,320,256]{2,1,0:T(8,128)(2,1)S(1)}, u32[]{:S(2)}, u32[]{:S(2)}) collective-permute-start(bf16[2,320,256]{2,1,0:T(8,128)(2,1)S(1)} %maximum_add_fusion.2), channel_id=1, source_target_pairs={{0,7},{1,0},{2,1},{3,2},{4,3},{5,4},{6,5},{7,6},{8,15},{9,8},{10,9... | collective-permute-start | bytes 983048 | tf_op jit(solution)/shard_map/ppermute | solution.py:298
  93.9 0.1 maximum_add_fusion
  94.0 0.3 collective-permute-start.18
  94.3 2.9 %collective-permute-done.6 = bf16[2,320,256]{2,1,0:T(8,128)(2,1)S(1)} collective-permute-done((bf16[2,320,256]{2,1,0:T(8,128)(2,1)S(1)}, bf16[2,320,256]{2,1,0:T(8,128)(2,1)S(1)}, u32[]{:S(2)}, u32[]{:S(2)}) %collective-permute-start.6) | collective-permute-done | bytes 327712 | tf_op jit(solution)/shard_map/ppermute | solution.py:298
  97.2 1.0 bitcast_add_fusion.4
  98.2 0.2 collective-permute-start.11
  98.4 1.9 %collective-permute-start.10 = (bf16[2,320,256]{2,1,0:T(8,128)(2,1)S(1)}, bf16[2,320,256]{2,1,0:T(8,128)(2,1)S(1)}, u32[]{:S(2)}, u32[]{:S(2)}) collective-permute-start(bf16[2,320,256]{2,1,0:T(8,128)(2,1)S(1)} %bitcast_add_fusion.4), channel_id=1, source_target_pairs={{0,1},{1,2},{2,3},{3,4},{4,5},{5,6},{6,7},{7,0},{8,9},{9,10},{10,1... | collective-permute-start | bytes 983048 | tf_op jit(solution)/shard_map/ppermute | solution.py:298
  100.3 2.2 %collective-permute-done.21 = bf16[2,320,256]{2,1,0:T(8,128)(2,1)S(1)} collective-permute-done((bf16[2,320,256]{2,1,0:T(8,128)(2,1)S(1)}, bf16[2,320,256]{2,1,0:T(8,128)(2,1)S(1)}, u32[]{:S(2)}, u32[]{:S(2)}) %collective-permute-start.21) | collective-permute-done | bytes 327712 | tf_op jit(solution)/shard_map/ppermute | solution.py:298
  102.5 3.3 %collective-permute-done.18 = bf16[2,320,256]{2,1,0:T(8,128)(2,1)S(1)} collective-permute-done((bf16[2,320,256]{2,1,0:T(8,128)(2,1)S(1)}, bf16[2,320,256]{2,1,0:T(8,128)(2,1)S(1)}, u32[]{:S(2)}, u32[]{:S(2)}) %collective-permute-start.18) | collective-permute-done | bytes 327712 | tf_op jit(solution)/shard_map/ppermute | solution.py:298
  105.8 0.1 convert_add_fusion.1
  105.9 4.5 %sum_term.1 = bf16[256,5120]{1,0:T(8,128)(2,1)} custom-call(bf16[256,5120]{1,0:T(8,128)(2,1)} %collective-permute-done.9.far_ref, bf16[256,5120]{1,0:T(8,128)(2,1)} %own_term.1.own_hbm), custom_call_target="tpu_custom_call" | custom-call | flops 2000000000 | bytes 1 | tf_op jit(solution)/shard_map/sum_term/pallas_call | solution.py:273
  110.5 2.4 %collective-permute-done.10 = bf16[2,320,256]{2,1,0:T(8,128)(2,1)S(1)} collective-permute-done((bf16[2,320,256]{2,1,0:T(8,128)(2,1)S(1)}, bf16[2,320,256]{2,1,0:T(8,128)(2,1)S(1)}, u32[]{:S(2)}, u32[]{:S(2)}) %collective-permute-start.10) | collective-permute-done | bytes 327712 | tf_op jit(solution)/shard_map/ppermute | solution.py:298
  112.8 1.1 fusion.3
  113.9 0.2 pad_maximum_fusion
  114.1 0.6 collective-permute-start.22
  114.8 11.0 %collective-permute-done.22 = bf16[320,512]{1,0:T(8,128)(2,1)S(1)} collective-permute-done((bf16[320,512]{1,0:T(8,128)(2,1)S(1)}, bf16[320,512]{1,0:T(8,128)(2,1)S(1)}, u32[]{:S(2)}, u32[]{:S(2)}) %collective-permute-start.22) | collective-permute-done | bytes 327712 | tf_op jit(solution)/shard_map/ppermute | solution.py:303
  125.8 0.1 fusion.4
  125.9 0.7 slice_bitcast_fusion
  126.6 0.6 slice_bitcast_fusion.1
  (31 shorter events, 0.4 us)
Async XLA Ops:
  0.6 32.5 %collective-permute-start = (bf16[256,5120]{1,0:T(8,128)(2,1)}, bf16[256,5120]{1,0:T(8,128)(2,1)S(1)}, u32[]{:S(2)}, u32[]{:S(2)}) collective-permute-start(bf16[256,5120]{1,0:T(8,128)(2,1)} %bitcast.100), channel_id=1, source_target_pairs={{0,240},{16,0},{32,16},{48,32},{64,48},{80,64},{96,80},{112,96},{1... | collective-permute-start | bytes 7864328 | tf_op jit(solution)/shard_map/ppermute | solution.py:292
  0.9 17.3 %collective-permute-start.1 = (bf16[128,5120]{1,0:T(8,128)(2,1)}, bf16[128,5120]{1,0:T(8,128)(2,1)}, u32[]{:S(2)}, u32[]{:S(2)}) collective-permute-start(bf16[128,5120]{1,0:T(8,128)(2,1)} %bitcast.104), channel_id=1, source_target_pairs={{0,16},{16,32},{32,48},{48,64},{64,80},{80,96},{96,112},{112,128},... | collective-permute-start | bytes 3932168 | tf_op jit(solution)/shard_map/ppermute | solution.py:292
  8.7 9.6 %copy-start.4 = (bf16[1,256,5120]{2,1,0:T(8,128)(2,1)S(1)}, bf16[1,256,5120]{2,1,0:T(8,128)(2,1)}, u32[]{:S(2)}) copy-start(bf16[1,256,5120]{2,1,0:T(8,128)(2,1)} %param.9) | copy-start | bytes 7864324
  20.4 10.6 %collective-permute-start.2 = (bf16[256,128]{1,0:T(8,128)(2,1)S(1)}, bf16[256,128]{1,0:T(8,128)(2,1)S(1)}, u32[]{:S(2)}, u32[]{:S(2)}) collective-permute-start(bf16[256,128]{1,0:T(8,128)(2,1)S(1)} %fusion.after_ref), channel_id=1, source_target_pairs={{0,240},{16,0},{32,16},{48,32},{64,48},{80,64},{96,80},{112,96},{1... | collective-permute-start | bytes 196616 | tf_op jit(solution)/shard_map/ppermute | solution.py:292
  23.3 1.1 copy-start.2
  31.0 17.3 %collective-permute-start.12 = (bf16[256,2560]{1,0:T(8,128)(2,1)}, bf16[256,2560]{1,0:T(8,128)(2,1)}, u32[]{:S(2)}, u32[]{:S(2)}) collective-permute-start(bf16[256,2560]{1,0:T(8,128)(2,1)} %get-tuple-element.43.refs_0_), channel_id=1, source_target_pairs={{0,240},{16,0},{32,16},{48,32},{64,48},{80,64},{96,80},{112,96},{1... | collective-permute-start | bytes 3932168 | tf_op jit(solution)/shard_map/ppermute | solution.py:292
  33.1 7.1 %copy-start.3 = (bf16[256,2560]{1,0:T(8,128)(2,1)S(1)}, bf16[256,2560]{1,0:T(8,128)(2,1)}, u32[]{:S(2)}) copy-start(bf16[256,2560]{1,0:T(8,128)(2,1)} %copy-done.2) | copy-start | bytes 3932164
  40.2 45.0 %copy-start.1 = (bf16[5120,256]{1,0:T(8,128)(2,1)}, bf16[5120,256]{1,0:T(8,128)(2,1)S(1)}, u32[]{:S(2)}) copy-start(bf16[5120,256]{1,0:T(8,128)(2,1)S(1)} %get-tuple-element.34) | copy-start | bytes 7864324
  40.3 27.2 %collective-permute-start.15 = (bf16[256,2560]{1,0:T(8,128)(2,1)S(1)}, bf16[256,2560]{1,0:T(8,128)(2,1)S(1)}, u32[]{:S(2)}, u32[]{:S(2)}) collective-permute-start(bf16[256,2560]{1,0:T(8,128)(2,1)S(1)} %copy-done.3), channel_id=1, source_target_pairs={{0,240},{16,0},{32,16},{48,32},{64,48},{80,64},{96,80},{112,96},{1... | collective-permute-start | bytes 3932168 | tf_op jit(solution)/shard_map/ppermute | solution.py:292
  40.5 16.6 %collective-permute-start.3 = (bf16[2,160,256]{2,1,0:T(8,128)(2,1)S(1)}, bf16[2,160,256]{2,1,0:T(8,128)(2,1)S(1)}, u32[]{:S(2)}, u32[]{:S(2)}) collective-permute-start(bf16[2,160,256]{2,1,0:T(8,128)(2,1)S(1)} %get-tuple-element.79), channel_id=1, source_target_pairs={{0,1},{1,2},{2,3},{3,4},{4,5},{5,6},{6,7},{7,0},{8,9},{9,10},{10,1... | collective-permute-start | bytes 491528 | tf_op jit(solution)/shard_map/ppermute | solution.py:298
  42.5 14.6 %collective-permute-start.4 = (bf16[2,160,256]{2,1,0:T(8,128)(2,1)S(1)}, bf16[2,160,256]{2,1,0:T(8,128)(2,1)S(1)}, u32[]{:S(2)}, u32[]{:S(2)}) collective-permute-start(bf16[2,160,256]{2,1,0:T(8,128)(2,1)S(1)} %get-tuple-element.78), channel_id=1, source_target_pairs={{0,7},{1,0},{2,1},{3,2},{4,3},{5,4},{6,5},{7,6},{8,15},{9,8},{10,9... | collective-permute-start | bytes 491528 | tf_op jit(solution)/shard_map/ppermute | solution.py:298
  50.9 8.4 %copy-start = (bf16[1,5120,384]{2,1,0:T(8,128)(2,1)S(1)}, bf16[1,5120,384]{2,1,0:T(8,128)(2,1)}, u32[]{:S(2)}) copy-start(bf16[1,5120,384]{2,1,0:T(8,128)(2,1)} %param.7) | copy-start | bytes 11796484
  51.0 11.3 %collective-permute-start.13 = (bf16[2,160,256]{2,1,0:T(8,128)(2,1)S(1)}, bf16[2,160,256]{2,1,0:T(8,128)(2,1)S(1)}, u32[]{:S(2)}, u32[]{:S(2)}) collective-permute-start(bf16[2,160,256]{2,1,0:T(8,128)(2,1)S(1)} %get-tuple-element.85), channel_id=1, source_target_pairs={{0,1},{1,2},{2,3},{3,4},{4,5},{5,6},{6,7},{7,0},{8,9},{9,10},{10,1... | collective-permute-start | bytes 491528 | tf_op jit(solution)/shard_map/ppermute | solution.py:298
  53.0 14.4 %collective-permute-start.14 = (bf16[2,160,256]{2,1,0:T(8,128)(2,1)S(1)}, bf16[2,160,256]{2,1,0:T(8,128)(2,1)S(1)}, u32[]{:S(2)}, u32[]{:S(2)}) collective-permute-start(bf16[2,160,256]{2,1,0:T(8,128)(2,1)S(1)} %get-tuple-element.84), channel_id=1, source_target_pairs={{0,7},{1,0},{2,1},{3,2},{4,3},{5,4},{6,5},{7,6},{8,15},{9,8},{10,9... | collective-permute-start | bytes 491528 | tf_op jit(solution)/shard_map/ppermute | solution.py:298
  57.2 13.2 %collective-permute-start.7 = (bf16[2,320,256]{2,1,0:T(8,128)(2,1)S(1)}, bf16[2,320,256]{2,1,0:T(8,128)(2,1)S(1)}, u32[]{:S(2)}, u32[]{:S(2)}) collective-permute-start(bf16[2,320,256]{2,1,0:T(8,128)(2,1)S(1)} %get-tuple-element.37), channel_id=1, source_target_pairs={{0,7},{1,0},{2,1},{3,2},{4,3},{5,4},{6,5},{7,6},{8,15},{9,8},{10,9... | collective-permute-start | bytes 983048 | tf_op jit(solution)/shard_map/ppermute | solution.py:298
  59.2 23.1 %collective-permute-start.5 = (bf16[2,320,256]{2,1,0:T(8,128)(2,1)S(1)}, bf16[2,320,256]{2,1,0:T(8,128)(2,1)S(1)}, u32[]{:S(2)}, u32[]{:S(2)}) collective-permute-start(bf16[2,320,256]{2,1,0:T(8,128)(2,1)S(1)} %get-tuple-element.36), channel_id=1, source_target_pairs={{0,1},{1,2},{2,3},{3,4},{4,5},{5,6},{6,7},{7,0},{8,9},{9,10},{10,1... | collective-permute-start | bytes 983048 | tf_op jit(solution)/shard_map/ppermute | solution.py:298
  62.4 35.8 %collective-permute-start.9 = (bf16[256,5120]{1,0:T(8,128)(2,1)}, bf16[256,5120]{1,0:T(8,128)(2,1)}, u32[]{:S(2)}, u32[]{:S(2)}) collective-permute-start(bf16[256,5120]{1,0:T(8,128)(2,1)} %far_term.1), channel_id=1, source_target_pairs={{0,16},{16,32},{32,48},{48,64},{64,80},{80,96},{96,112},{112,128},... | collective-permute-start | bytes 7864328 | tf_op jit(solution)/shard_map/ppermute | solution.py:292
  67.5 10.7 %collective-permute-start.19 = (bf16[2,320,256]{2,1,0:T(8,128)(2,1)S(1)}, bf16[2,320,256]{2,1,0:T(8,128)(2,1)S(1)}, u32[]{:S(2)}, u32[]{:S(2)}) collective-permute-start(bf16[2,320,256]{2,1,0:T(8,128)(2,1)S(1)} %pad_maximum_fusion.3), channel_id=1, source_target_pairs={{0,7},{1,0},{2,1},{3,2},{4,3},{5,4},{6,5},{7,6},{8,15},{9,8},{10,9... | collective-permute-start | bytes 983048 | tf_op jit(solution)/shard_map/ppermute | solution.py:298
  70.5 14.7 %collective-permute-start.8 = (bf16[2,320,256]{2,1,0:T(8,128)(2,1)S(1)}, bf16[2,320,256]{2,1,0:T(8,128)(2,1)S(1)}, u32[]{:S(2)}, u32[]{:S(2)}) collective-permute-start(bf16[2,320,256]{2,1,0:T(8,128)(2,1)S(1)} %bitcast_add_fusion.1), channel_id=1, source_target_pairs={{0,7},{1,0},{2,1},{3,2},{4,3},{5,4},{6,5},{7,6},{8,15},{9,8},{10,9... | collective-permute-start | bytes 983048 | tf_op jit(solution)/shard_map/ppermute | solution.py:298
  71.5 8.9 %collective-permute-start.16 = (bf16[2,320,256]{2,1,0:T(8,128)(2,1)S(1)}, bf16[2,320,256]{2,1,0:T(8,128)(2,1)S(1)}, u32[]{:S(2)}, u32[]{:S(2)}) collective-permute-start(bf16[2,320,256]{2,1,0:T(8,128)(2,1)S(1)} %fusion.7), channel_id=1, source_target_pairs={{0,1},{1,2},{2,3},{3,4},{4,5},{5,6},{6,7},{7,0},{8,9},{9,10},{10,1... | collective-permute-start | bytes 983048 | tf_op jit(solution)/shard_map/ppermute | solution.py:298
  78.2 13.7 %collective-permute-start.20 = (bf16[2,320,256]{2,1,0:T(8,128)(2,1)S(1)}, bf16[2,320,256]{2,1,0:T(8,128)(2,1)S(1)}, u32[]{:S(2)}, u32[]{:S(2)}) collective-permute-start(bf16[2,320,256]{2,1,0:T(8,128)(2,1)S(1)} %maximum_add_fusion.3), channel_id=1, source_target_pairs={{0,7},{1,0},{2,1},{3,2},{4,3},{5,4},{6,5},{7,6},{8,15},{9,8},{10,9... | collective-permute-start | bytes 983048 | tf_op jit(solution)/shard_map/ppermute | solution.py:298
  80.5 13.4 %collective-permute-start.17 = (bf16[2,320,256]{2,1,0:T(8,128)(2,1)S(1)}, bf16[2,320,256]{2,1,0:T(8,128)(2,1)S(1)}, u32[]{:S(2)}, u32[]{:S(2)}) collective-permute-start(bf16[2,320,256]{2,1,0:T(8,128)(2,1)S(1)} %maximum_add_fusion.1), channel_id=1, source_target_pairs={{0,1},{1,2},{2,3},{3,4},{4,5},{5,6},{6,7},{7,0},{8,9},{9,10},{10,1... | collective-permute-start | bytes 983048 | tf_op jit(solution)/shard_map/ppermute | solution.py:298
  85.3 11.9 %collective-permute-start.6 = (bf16[2,320,256]{2,1,0:T(8,128)(2,1)S(1)}, bf16[2,320,256]{2,1,0:T(8,128)(2,1)S(1)}, u32[]{:S(2)}, u32[]{:S(2)}) collective-permute-start(bf16[2,320,256]{2,1,0:T(8,128)(2,1)S(1)} %get-tuple-element.56), channel_id=1, source_target_pairs={{0,1},{1,2},{2,3},{3,4},{4,5},{5,6},{6,7},{7,0},{8,9},{9,10},{10,1... | collective-permute-start | bytes 983048 | tf_op jit(solution)/shard_map/ppermute | solution.py:298
  92.0 10.5 %collective-permute-start.21 = (bf16[2,320,256]{2,1,0:T(8,128)(2,1)S(1)}, bf16[2,320,256]{2,1,0:T(8,128)(2,1)S(1)}, u32[]{:S(2)}, u32[]{:S(2)}) collective-permute-start(bf16[2,320,256]{2,1,0:T(8,128)(2,1)S(1)} %maximum_add_fusion.2), channel_id=1, source_target_pairs={{0,7},{1,0},{2,1},{3,2},{4,3},{5,4},{6,5},{7,6},{8,15},{9,8},{10,9... | collective-permute-start | bytes 983048 | tf_op jit(solution)/shard_map/ppermute | solution.py:298
  94.0 11.8 %collective-permute-start.18 = (bf16[2,320,256]{2,1,0:T(8,128)(2,1)S(1)}, bf16[2,320,256]{2,1,0:T(8,128)(2,1)S(1)}, u32[]{:S(2)}, u32[]{:S(2)}) collective-permute-start(bf16[2,320,256]{2,1,0:T(8,128)(2,1)S(1)} %maximum_add_fusion), channel_id=1, source_target_pairs={{0,1},{1,2},{2,3},{3,4},{4,5},{5,6},{6,7},{7,0},{8,9},{9,10},{10,1... | collective-permute-start | bytes 983048 | tf_op jit(solution)/shard_map/ppermute | solution.py:298
  98.2 12.2 %collective-permute-start.11 = (bf16[2,320,256]{2,1,0:T(8,128)(2,1)S(1)}, bf16[2,320,256]{2,1,0:T(8,128)(2,1)S(1)}, u32[]{:S(2)}, u32[]{:S(2)}) collective-permute-start(bf16[2,320,256]{2,1,0:T(8,128)(2,1)S(1)} %get-tuple-element.40), channel_id=1, source_target_pairs={{0,7},{1,0},{2,1},{3,2},{4,3},{5,4},{6,5},{7,6},{8,15},{9,8},{10,9... | collective-permute-start | bytes 983048 | tf_op jit(solution)/shard_map/ppermute | solution.py:298
  98.4 14.4 %collective-permute-start.10 = (bf16[2,320,256]{2,1,0:T(8,128)(2,1)S(1)}, bf16[2,320,256]{2,1,0:T(8,128)(2,1)S(1)}, u32[]{:S(2)}, u32[]{:S(2)}) collective-permute-start(bf16[2,320,256]{2,1,0:T(8,128)(2,1)S(1)} %bitcast_add_fusion.4), channel_id=1, source_target_pairs={{0,1},{1,2},{2,3},{3,4},{4,5},{5,6},{6,7},{7,0},{8,9},{9,10},{10,1... | collective-permute-start | bytes 983048 | tf_op jit(solution)/shard_map/ppermute | solution.py:298
  114.1 11.6 %collective-permute-start.22 = (bf16[320,512]{1,0:T(8,128)(2,1)S(1)}, bf16[320,512]{1,0:T(8,128)(2,1)S(1)}, u32[]{:S(2)}, u32[]{:S(2)}) collective-permute-start(bf16[320,512]{1,0:T(8,128)(2,1)S(1)} %fusion.5), channel_id=1, source_target_pairs={{0,8},{1,9},{2,10},{3,11},{4,12},{5,13},{6,14},{7,15},{8,0},{9,1},... | collective-permute-start | bytes 983048 | tf_op jit(solution)/shard_map/ppermute | solution.py:303

commit v4 on v3

--- a/solution.py
+++ b/solution.py
@@ -156,23 +156,24 @@
     )
 
 
-def grads_kernel(*refs):
-    out_ref = refs[-1]
-    pairs = [(refs[i], refs[i + 1][...]) for i in range(0, len(refs) - 1, 2)]
-    add_up(pairs, [out_ref], TILE)
-
-
-def grads_out(*pairs):
-    out = shape((pairs[0][0].shape[1], pairs[0][1].shape[1]))
-    args = [a for pair in pairs for a in pair]
-    return whole(grads_kernel, "grads_out", SMALL, args, 0, [out])[0]
+def grads_kernel(g_ref, att_ref, own_ref, out_ref):
+    for start in range(0, g_ref.shape[1], TILE):
+        total = dot(g_ref[:, start : start + TILE], att_ref[...], 0, 0)
+        total += own_ref[start : start + TILE].astype(F32)
+        out_ref[start : start + TILE] = total.astype(BF)
+
+
+def grads_out(g, att, own):
+    return whole(grads_kernel, "grads_out", SMALL, (g, att, own), 0, [shape(own.shape)])[0]
 
 
 def first_pair(z):
     return (z + 3) // 2 % (N_Z // 2)
 
 
-def columns_kernel(after_ref, g_hbm, near_ref, rest_ref, sems):
+def columns_kernel(
+    after_ref, att_ref, g_hbm, near_ref, rest_ref, own_near_ref, own_rest_ref, sems
+):
     z = lax.axis_index("dp") % N_Z
     model = g_hbm.shape[1]
     width = model // N_Z
@@ -191,14 +192,19 @@
                 )
     for copy in copies:
         copy.start()
-    for copy in copies:
-        copy.wait()
-
-
-def columns_of(g, after):
-    outs = [shape((g.shape[0], g.shape[1] // 2))] * 2
+    for out, own_ref, some in (
+        (near_ref, own_near_ref, copies[:4]), (rest_ref, own_rest_ref, copies[4:])
+    ):
+        for copy in some:
+            copy.wait()
+        add_up([(out, att_ref[...])], [own_ref], TILE)
+
+
+def columns_of(g, att, after):
+    half = g.shape[1] // 2
+    outs = [shape((g.shape[0], half))] * 2 + [shape((half, att.shape[1]))] * 2
     return whole(
-        columns_kernel, "columns", SMALL, (after, g), 1, outs, [pltpu.SemaphoreType.DMA((8,))]
+        columns_kernel, "columns", SMALL, (after, att, g), 1, outs, [pltpu.SemaphoreType.DMA((8,))]
     )
 
 
@@ -364,7 +370,7 @@
     wo_back, d_qkv, term_own = together((wo_back, d_qkv, term_own))
     d_att_home = dot(g, wo_back, 1, 1).astype(BF)
     d_att_far = shifted(d_att_home, -1)
-    columns = columns_of(g, d_att_home)
+    columns = columns_of(g, att, d_att_home)
     near, d_att_far = together((columns[0], d_att_far))
     columns_far = [shifted(near, -1), None]
     d_qkv_far, att_far, grad_qk, grad_v = far_pair(
@@ -378,7 +384,7 @@
     z = lax.axis_index("dp") % N_Z
 
     def terms_o(i):
-        grad = grads_out((columns[i], att), (columns_far[i], att_far))
+        grad = grads_out(columns_far[i], att_far, columns[2 + i])
         return grad.reshape(2, N_Z // 2, rows, head)
 
     def second(distance):

time: 128 us -> 127 us (level)
  local copies, waits for them, and re-layouts: 3.81 us -> 6.96 us
  waiting for transfers between devices: 48.6 us -> 46.2 us
  starting transfers between devices: 35.3 us -> 33.6 us
    ppermute x6, waiting for transfers between devices: 12.5 us -> 9.67 us  [shifted(): lax.ppermute(block, 'blk', [(i, (i + distance) % n) for i in range(n)])]
    unnamed x10 -> x16, local copies, waits for them, and re-layouts: 1.11 us -> 3.6 us
    ppermute x16, starting transfers between devices: 27.1 us -> 25.4 us  [z_shifted(): return lax.ppermute(block, 'dp', route)]
  transfers between devices with their start and end apart: 23 -> 23, of which waited for: 12 -> 11; matrix products, arithmetic and copies ran while one was open for 4% -> 5% of each run, Pallas kernels for 26% -> 26%
where the time goes in v4:
time: 127 us; the launch traced here: 126 us
  waiting for transfers between devices  46.2 us (36%)
  starting transfers between devices  33.6 us (26%)
  Pallas kernels  32.3 us (25%)
  local copies, waits for them, and re-layouts  6.96 us (5%)
  other arithmetic  3.57 us (3%)
  matrix products  2.15 us (2%)
    ppermute x16, waiting for transfers between devices, z_shifted(): return lax.ppermute(block, 'dp', route)  25.6 us
    ppermute x16, starting transfers between devices, z_shifted(): return lax.ppermute(block, 'dp', route)  25.4 us
    pallas_call x6, Pallas kernels, whole(): pl.pallas_call(kernel, in_specs=[here] * (len(args) - in_hbm) + [there] *...  22.5 us
    ppermute x1, waiting for transfers between devices, x_swapped(): return lax.ppermute(block, 'dp', [(i, (i + N_Z) % n) for i in range(n)])  10.9 us
    ppermute x6, waiting for transfers between devices, shifted(): lax.ppermute(block, 'blk', [(i, (i + distance) % n) for i in range(n)])  9.67 us
    ppermute x6, starting transfers between devices, shifted(): lax.ppermute(block, 'blk', [(i, (i + distance) % n) for i in range(n)])  7.6 us
    pallas_call x1, Pallas kernels, own_term(): pl.pallas_call(own_term_kernel, in_specs=[pl.BlockSpec(memory_space=pltpu...  5.3 us
    pallas_call x1, Pallas kernels, sum_of(): pl.pallas_call(sum_kernel, in_specs=[pl.BlockSpec(memory_space=pltpu.VMEM...  4.53 us
  transfers between devices with their start and end apart: 23, of which 11 were waited for; matrix products, arithmetic and copies ran while one was open for 5% of the time, Pallas kernels for 26%

profile of v4, /device:TPU:28, one launch (start us, length us, event | category | flops | bytes accessed | tf_op | source)
XLA Modules:
  0.0 125.8 jit_solution(15295454979659751070)
XLA Ops:
  0.6 0.3 collective-permute-start
  0.9 0.3 collective-permute-start.1
  1.2 0.8 fusion.25
  2.0 0.1 copy.10.seg_col_ref
  2.1 6.5 %own_pair.1 = (bf16[256,384]{1,0:T(8,128)(2,1)S(1)}, bf16[256,128]{1,0:T(8,128)(2,1)S(1)}) custom-call(s32[1,256]{1,0:T(1,128)S(1)} %get-tuple-element.93.seg_row_ref, s32[256,1]{1,0:T(8,128)S(1)} %copy.10.seg_col_ref, bf16[256,5120]{1,0:T(8,128)(2,1)} %bitcast.101, bf16[5120,384]{1,0:T(8,128)(2,1)} %bitcast.85, bf16[256,5120]{1,0:T(8,128)(2,1)} %bitcast.98, ...), custom_call_target="tpu_custom_call" | custom-call | flops 1 | bytes 1 | tf_op jit(solution)/shard_map/own_pair/pallas_call | solution.py:51
  8.7 5.3 %own_term.1.own_hbm = bf16[256,5120]{1,0:T(8,128)(2,1)} custom-call(bf16[256,384]{1,0:T(8,128)(2,1)S(1)} %get-tuple-element.36.d_ref, bf16[5120,384]{1,0:T(8,128)(2,1)} %bitcast.86), custom_call_target="tpu_custom_call" | custom-call | flops 1 | bytes 1 | tf_op jit(solution)/shard_map/own_term/pallas_call | solution.py:238
  14.0 4.2 %collective-permute-done.1 = bf16[128,5120]{1,0:T(8,128)(2,1)} collective-permute-done((bf16[128,5120]{1,0:T(8,128)(2,1)}, bf16[128,5120]{1,0:T(8,128)(2,1)}, u32[]{:S(2)}, u32[]{:S(2)}) %collective-permute-start.1) | collective-permute-done | bytes 1310752 | tf_op jit(solution)/shard_map/ppermute | solution.py:298
  18.2 2.2 %fusion.after_ref = bf16[256,128]{1,0:T(8,128)(2,1)S(1)} fusion(bf16[128,5120]{1,0:T(8,128)(2,1)} %collective-permute-done.1, bf16[1,256,5120]{2,1,0:T(8,128)(2,1)S(1)} %copy-done.7), kind=kOutput, calls=%fused_computation.12 | convolution fusion | flops 335577088 | bytes 3997696 | tf_op jit(solution)/shard_map/dot_general | solution.py:16
  20.4 0.1 collective-permute-start.2
  20.5 3.4 %columns.1 = (bf16[256,2560]{1,0:T(8,128)(2,1)}, bf16[256,2560]{1,0:T(8,128)(2,1)S(1)}, bf16[2560,128]{1,0:T(8,128)(2,1)S(1)}, bf16[2560,128]{1,0:T(8,128)(2,1)S(1)}) custom-call(bf16[256,128]{1,0:T(8,128)(2,1)S(1)} %fusion.after_ref, bf16[256,128]{1,0:T(8,128)(2,1)S(1)} %get-tuple-element.33.att_ref, bf16[256,5120]{1,0:T(8,128)(2,1)} %bitcast.99), custom_call_target="tpu_custom_call" | custom-call | flops 1 | bytes 1 | tf_op jit(solution)/shard_map/columns/pallas_call | solution.py:51
  23.9 0.9 copy-done.2
  24.8 1.1 copy-done.5
  25.8 5.1 %collective-permute-done.2.datt_ref = bf16[256,128]{1,0:T(8,128)(2,1)S(1)} collective-permute-done((bf16[256,128]{1,0:T(8,128)(2,1)S(1)}, bf16[256,128]{1,0:T(8,128)(2,1)S(1)}, u32[]{:S(2)}, u32[]{:S(2)}) %collective-permute-start.2) | collective-permute-done | bytes 65568 | tf_op jit(solution)/shard_map/ppermute | solution.py:298
  31.0 1.9 %collective-permute-start.12 = (bf16[256,2560]{1,0:T(8,128)(2,1)}, bf16[256,2560]{1,0:T(8,128)(2,1)}, u32[]{:S(2)}, u32[]{:S(2)}) collective-permute-start(bf16[256,2560]{1,0:T(8,128)(2,1)} %get-tuple-element.45), channel_id=1, source_target_pairs={{0,240},{16,0},{32,16},{48,32},{64,48},{80,64},{96,80},{112,96},{1... | collective-permute-start | bytes 3932168 | tf_op jit(solution)/shard_map/ppermute | solution.py:298
  32.9 0.8 copy.12.seg_col_ref
  33.7 0.9 copy-done.4
  34.6 7.1 %far_pair.1 = (bf16[256,384]{1,0:T(8,128)(2,1)S(1)}, bf16[256,128]{1,0:T(8,128)(2,1)S(1)}, bf16[5120,256]{1,0:T(8,128)(2,1)S(1)}, bf16[5120,128]{1,0:T(8,128)(2,1)S(1)}) custom-call(bf16[256,5120]{1,0:T(8,128)(2,1)S(1)} %collective-permute-done.xf_ref, bf16[256,128]{1,0:T(8,128)(2,1)S(1)} %collective-permute-done.2.datt_ref, ...), custom_call_target="tpu_custom_call" | custom-call | flops 1 | bytes 1 | tf_op jit(solution)/shard_map/far_pair/pallas_call | solution.py:51
  41.7 0.1 collective-permute-start.15
  41.9 2.0 %collective-permute-start.3 = (bf16[2,160,256]{2,1,0:T(8,128)(2,1)S(1)}, bf16[2,160,256]{2,1,0:T(8,128)(2,1)S(1)}, u32[]{:S(2)}, u32[]{:S(2)}) collective-permute-start(bf16[2,160,256]{2,1,0:T(8,128)(2,1)S(1)} %get-tuple-element.83), channel_id=1, source_target_pairs={{0,1},{1,2},{2,3},{3,4},{4,5},{5,6},{6,7},{7,0},{8,9},{9,10},{10,1... | collective-permute-start | bytes 491528 | tf_op jit(solution)/shard_map/ppermute | solution.py:304
  43.9 4.0 %collective-permute-start.4 = (bf16[2,160,256]{2,1,0:T(8,128)(2,1)S(1)}, bf16[2,160,256]{2,1,0:T(8,128)(2,1)S(1)}, u32[]{:S(2)}, u32[]{:S(2)}) collective-permute-start(bf16[2,160,256]{2,1,0:T(8,128)(2,1)S(1)} %get-tuple-element.82), channel_id=1, source_target_pairs={{0,7},{1,0},{2,1},{3,2},{4,3},{5,4},{6,5},{7,6},{8,15},{9,8},{10,9... | collective-permute-start | bytes 491528 | tf_op jit(solution)/shard_map/ppermute | solution.py:304
  47.9 0.1 dynamic-slice_bitcast_fusion.13
  48.0 0.3 collective-permute-done.12.g_ref
  48.3 0.7 copy-done.3
  49.0 1.9 %grads_out.2 = bf16[2560,128]{1,0:T(8,128)(2,1)S(1)} custom-call(bf16[256,2560]{1,0:T(8,128)(2,1)} %collective-permute-done.12.g_ref, bf16[256,128]{1,0:T(8,128)(2,1)S(1)} %get-tuple-element.48.att_ref, bf16[2560,128]{1,0:T(8,128)(2,1)S(1)} %copy-done.3), custom_call_target="tpu_custom_call" | custom-call | flops 1 | bytes 1 | tf_op jit(solution)/shard_map/grads_out/pallas_call | solution.py:51
  51.0 1.3 %collective-permute-start.13 = (bf16[2,160,256]{2,1,0:T(8,128)(2,1)S(1)}, bf16[2,160,256]{2,1,0:T(8,128)(2,1)S(1)}, u32[]{:S(2)}, u32[]{:S(2)}) collective-permute-start(bf16[2,160,256]{2,1,0:T(8,128)(2,1)S(1)} %get-tuple-element.89), channel_id=1, source_target_pairs={{0,1},{1,2},{2,3},{3,4},{4,5},{5,6},{6,7},{7,0},{8,9},{9,10},{10,1... | collective-permute-start | bytes 491528 | tf_op jit(solution)/shard_map/ppermute | solution.py:304
  52.3 4.0 %collective-permute-start.14 = (bf16[2,160,256]{2,1,0:T(8,128)(2,1)S(1)}, bf16[2,160,256]{2,1,0:T(8,128)(2,1)S(1)}, u32[]{:S(2)}, u32[]{:S(2)}) collective-permute-start(bf16[2,160,256]{2,1,0:T(8,128)(2,1)S(1)} %get-tuple-element.88), channel_id=1, source_target_pairs={{0,7},{1,0},{2,1},{3,2},{4,3},{5,4},{6,5},{7,6},{8,15},{9,8},{10,9... | collective-permute-start | bytes 491528 | tf_op jit(solution)/shard_map/ppermute | solution.py:304
  56.5 2.0 %collective-permute-start.7 = (bf16[2,320,256]{2,1,0:T(8,128)(2,1)S(1)}, bf16[2,320,256]{2,1,0:T(8,128)(2,1)S(1)}, u32[]{:S(2)}, u32[]{:S(2)}) collective-permute-start(bf16[2,320,256]{2,1,0:T(8,128)(2,1)S(1)} %get-tuple-element.40), channel_id=1, source_target_pairs={{0,7},{1,0},{2,1},{3,2},{4,3},{5,4},{6,5},{7,6},{8,15},{9,8},{10,9... | collective-permute-start | bytes 983048 | tf_op jit(solution)/shard_map/ppermute | solution.py:304
  58.5 0.1 collective-permute-start.5
  58.6 3.0 %far_term.1 = bf16[256,5120]{1,0:T(8,128)(2,1)} custom-call(bf16[256,384]{1,0:T(8,128)(2,1)S(1)} %get-tuple-element.41.d_ref, bf16[5120,384]{1,0:T(8,128)(2,1)S(1)} %bitcast.88), custom_call_target="tpu_custom_call" | custom-call | flops 2013265920 | bytes 1 | tf_op jit(solution)/shard_map/far_term/pallas_call | solution.py:51
  61.6 4.9 %collective-permute-start.9 = (bf16[256,5120]{1,0:T(8,128)(2,1)}, bf16[256,5120]{1,0:T(8,128)(2,1)}, u32[]{:S(2)}, u32[]{:S(2)}) collective-permute-start(bf16[256,5120]{1,0:T(8,128)(2,1)} %far_term.1), channel_id=1, source_target_pairs={{0,16},{16,32},{32,48},{48,64},{64,80},{80,96},{96,112},{112,128},... | collective-permute-start | bytes 7864328 | tf_op jit(solution)/shard_map/ppermute | solution.py:298
  66.8 2.9 %collective-permute-start.19 = (bf16[2,320,256]{2,1,0:T(8,128)(2,1)S(1)}, bf16[2,320,256]{2,1,0:T(8,128)(2,1)S(1)}, u32[]{:S(2)}, u32[]{:S(2)}) collective-permute-start(bf16[2,320,256]{2,1,0:T(8,128)(2,1)S(1)} %pad_maximum_fusion.3), channel_id=1, source_target_pairs={{0,7},{1,0},{2,1},{3,2},{4,3},{5,4},{6,5},{7,6},{8,15},{9,8},{10,9... | collective-permute-start | bytes 983048 | tf_op jit(solution)/shard_map/ppermute | solution.py:304
  69.8 0.1 collective-permute-start.8
  69.9 2.0 %collective-permute-start.16 = (bf16[2,320,256]{2,1,0:T(8,128)(2,1)S(1)}, bf16[2,320,256]{2,1,0:T(8,128)(2,1)S(1)}, u32[]{:S(2)}, u32[]{:S(2)}) collective-permute-start(bf16[2,320,256]{2,1,0:T(8,128)(2,1)S(1)} %fusion.7), channel_id=1, source_target_pairs={{0,1},{1,2},{2,3},{3,4},{4,5},{5,6},{6,7},{7,0},{8,9},{9,10},{10,1... | collective-permute-start | bytes 983048 | tf_op jit(solution)/shard_map/ppermute | solution.py:304
  71.9 0.6 grads_out.3
  72.4 0.3 fusion.21
  72.8 4.4 %collective-permute-done.19 = bf16[2,320,256]{2,1,0:T(8,128)(2,1)S(1)} collective-permute-done((bf16[2,320,256]{2,1,0:T(8,128)(2,1)S(1)}, bf16[2,320,256]{2,1,0:T(8,128)(2,1)S(1)}, u32[]{:S(2)}, u32[]{:S(2)}) %collective-permute-start.19) | collective-permute-done | bytes 327712 | tf_op jit(solution)/shard_map/ppermute | solution.py:304
  77.1 0.1 maximum_add_fusion.3
  77.2 1.2 collective-permute-start.20
  78.4 0.1 maximum_add_fusion.1
  78.5 1.4 %collective-permute-start.17 = (bf16[2,320,256]{2,1,0:T(8,128)(2,1)S(1)}, bf16[2,320,256]{2,1,0:T(8,128)(2,1)S(1)}, u32[]{:S(2)}, u32[]{:S(2)}) collective-permute-start(bf16[2,320,256]{2,1,0:T(8,128)(2,1)S(1)} %maximum_add_fusion.1), channel_id=1, source_target_pairs={{0,1},{1,2},{2,3},{3,4},{4,5},{5,6},{6,7},{7,0},{8,9},{9,10},{10,1... | collective-permute-start | bytes 983048 | tf_op jit(solution)/shard_map/ppermute | solution.py:304
  79.9 4.2 %collective-permute-done.8 = bf16[2,320,256]{2,1,0:T(8,128)(2,1)S(1)} collective-permute-done((bf16[2,320,256]{2,1,0:T(8,128)(2,1)S(1)}, bf16[2,320,256]{2,1,0:T(8,128)(2,1)S(1)}, u32[]{:S(2)}, u32[]{:S(2)}) %collective-permute-start.8) | collective-permute-done | bytes 327712 | tf_op jit(solution)/shard_map/ppermute | solution.py:304
  84.2 0.1 bitcast_add_fusion.2
  84.2 0.1 collective-permute-start.6
  84.3 6.8 %collective-permute-done.20 = bf16[2,320,256]{2,1,0:T(8,128)(2,1)S(1)} collective-permute-done((bf16[2,320,256]{2,1,0:T(8,128)(2,1)S(1)}, bf16[2,320,256]{2,1,0:T(8,128)(2,1)S(1)}, u32[]{:S(2)}, u32[]{:S(2)}) %collective-permute-start.20) | collective-permute-done | bytes 327712 | tf_op jit(solution)/shard_map/ppermute | solution.py:304
  91.2 0.1 maximum_add_fusion.2
  91.3 1.2 collective-permute-start.21
  92.4 0.1 maximum_add_fusion
  92.5 1.0 collective-permute-start.18
  93.5 2.6 %collective-permute-done.6 = bf16[2,320,256]{2,1,0:T(8,128)(2,1)S(1)} collective-permute-done((bf16[2,320,256]{2,1,0:T(8,128)(2,1)S(1)}, bf16[2,320,256]{2,1,0:T(8,128)(2,1)S(1)}, u32[]{:S(2)}, u32[]{:S(2)}) %collective-permute-start.6) | collective-permute-done | bytes 327712 | tf_op jit(solution)/shard_map/ppermute | solution.py:304
  96.1 1.0 bitcast_add_fusion.4
  97.1 0.1 collective-permute-start.11
  97.2 2.0 %collective-permute-start.10 = (bf16[2,320,256]{2,1,0:T(8,128)(2,1)S(1)}, bf16[2,320,256]{2,1,0:T(8,128)(2,1)S(1)}, u32[]{:S(2)}, u32[]{:S(2)}) collective-permute-start(bf16[2,320,256]{2,1,0:T(8,128)(2,1)S(1)} %bitcast_add_fusion.4), channel_id=1, source_target_pairs={{0,1},{1,2},{2,3},{3,4},{4,5},{5,6},{6,7},{7,0},{8,9},{9,10},{10,1... | collective-permute-start | bytes 983048 | tf_op jit(solution)/shard_map/ppermute | solution.py:304
  99.2 2.5 %collective-permute-done.21 = bf16[2,320,256]{2,1,0:T(8,128)(2,1)S(1)} collective-permute-done((bf16[2,320,256]{2,1,0:T(8,128)(2,1)S(1)}, bf16[2,320,256]{2,1,0:T(8,128)(2,1)S(1)}, u32[]{:S(2)}, u32[]{:S(2)}) %collective-permute-start.21) | collective-permute-done | bytes 327712 | tf_op jit(solution)/shard_map/ppermute | solution.py:304
  101.8 2.7 %collective-permute-done.18 = bf16[2,320,256]{2,1,0:T(8,128)(2,1)S(1)} collective-permute-done((bf16[2,320,256]{2,1,0:T(8,128)(2,1)S(1)}, bf16[2,320,256]{2,1,0:T(8,128)(2,1)S(1)}, u32[]{:S(2)}, u32[]{:S(2)}) %collective-permute-start.18) | collective-permute-done | bytes 327712 | tf_op jit(solution)/shard_map/ppermute | solution.py:304
  104.5 0.1 convert_add_fusion.1
  104.6 4.5 %sum_term.1 = bf16[256,5120]{1,0:T(8,128)(2,1)} custom-call(bf16[256,5120]{1,0:T(8,128)(2,1)} %collective-permute-done.9.far_ref, bf16[256,5120]{1,0:T(8,128)(2,1)} %own_term.1.own_hbm), custom_call_target="tpu_custom_call" | custom-call | flops 2000000000 | bytes 1 | tf_op jit(solution)/shard_map/sum_term/pallas_call | solution.py:279
  109.1 2.4 %collective-permute-done.10 = bf16[2,320,256]{2,1,0:T(8,128)(2,1)S(1)} collective-permute-done((bf16[2,320,256]{2,1,0:T(8,128)(2,1)S(1)}, bf16[2,320,256]{2,1,0:T(8,128)(2,1)S(1)}, u32[]{:S(2)}, u32[]{:S(2)}) %collective-permute-start.10) | collective-permute-done | bytes 327712 | tf_op jit(solution)/shard_map/ppermute | solution.py:304
  111.5 1.1 fusion.3
  112.6 0.2 pad_maximum_fusion
  112.8 0.6 collective-permute-start.22
  113.4 10.9 %collective-permute-done.22 = bf16[320,512]{1,0:T(8,128)(2,1)S(1)} collective-permute-done((bf16[320,512]{1,0:T(8,128)(2,1)S(1)}, bf16[320,512]{1,0:T(8,128)(2,1)S(1)}, u32[]{:S(2)}, u32[]{:S(2)}) %collective-permute-start.22) | collective-permute-done | bytes 327712 | tf_op jit(solution)/shard_map/ppermute | solution.py:309
  124.3 0.1 fusion.4
  124.4 0.7 slice_bitcast_fusion
  125.2 0.6 slice_bitcast_fusion.1
  (37 shorter events, 0.6 us)
Async XLA Ops:
  0.6 33.1 %collective-permute-start = (bf16[256,5120]{1,0:T(8,128)(2,1)}, bf16[256,5120]{1,0:T(8,128)(2,1)S(1)}, u32[]{:S(2)}, u32[]{:S(2)}) collective-permute-start(bf16[256,5120]{1,0:T(8,128)(2,1)} %bitcast.100), channel_id=1, source_target_pairs={{0,240},{16,0},{32,16},{48,32},{64,48},{80,64},{96,80},{112,96},{1... | collective-permute-start | bytes 7864328 | tf_op jit(solution)/shard_map/ppermute | solution.py:298
  0.9 17.3 %collective-permute-start.1 = (bf16[128,5120]{1,0:T(8,128)(2,1)}, bf16[128,5120]{1,0:T(8,128)(2,1)}, u32[]{:S(2)}, u32[]{:S(2)}) collective-permute-start(bf16[128,5120]{1,0:T(8,128)(2,1)} %bitcast.104), channel_id=1, source_target_pairs={{0,16},{16,32},{32,48},{48,64},{64,80},{80,96},{96,112},{112,128},... | collective-permute-start | bytes 3932168 | tf_op jit(solution)/shard_map/ppermute | solution.py:298
  8.7 9.6 %copy-start.7 = (bf16[1,256,5120]{2,1,0:T(8,128)(2,1)S(1)}, bf16[1,256,5120]{2,1,0:T(8,128)(2,1)}, u32[]{:S(2)}) copy-start(bf16[1,256,5120]{2,1,0:T(8,128)(2,1)} %param.9) | copy-start | bytes 7864324
  20.4 10.6 %collective-permute-start.2 = (bf16[256,128]{1,0:T(8,128)(2,1)S(1)}, bf16[256,128]{1,0:T(8,128)(2,1)S(1)}, u32[]{:S(2)}, u32[]{:S(2)}) collective-permute-start(bf16[256,128]{1,0:T(8,128)(2,1)S(1)} %fusion.after_ref), channel_id=1, source_target_pairs={{0,240},{16,0},{32,16},{48,32},{64,48},{80,64},{96,80},{112,96},{1... | collective-permute-start | bytes 196616 | tf_op jit(solution)/shard_map/ppermute | solution.py:298
  23.9 0.9 copy-start.2
  24.8 1.1 copy-start.5
  31.0 17.3 %collective-permute-start.12 = (bf16[256,2560]{1,0:T(8,128)(2,1)}, bf16[256,2560]{1,0:T(8,128)(2,1)}, u32[]{:S(2)}, u32[]{:S(2)}) collective-permute-start(bf16[256,2560]{1,0:T(8,128)(2,1)} %get-tuple-element.45), channel_id=1, source_target_pairs={{0,240},{16,0},{32,16},{48,32},{64,48},{80,64},{96,80},{112,96},{1... | collective-permute-start | bytes 3932168 | tf_op jit(solution)/shard_map/ppermute | solution.py:298
  33.7 0.9 copy-start.4
  34.6 7.1 %copy-start.6 = (bf16[256,2560]{1,0:T(8,128)(2,1)S(1)}, bf16[256,2560]{1,0:T(8,128)(2,1)}, u32[]{:S(2)}) copy-start(bf16[256,2560]{1,0:T(8,128)(2,1)} %copy-done.5) | copy-start | bytes 3932164
  41.7 42.5 %copy-start.1 = (bf16[5120,256]{1,0:T(8,128)(2,1)}, bf16[5120,256]{1,0:T(8,128)(2,1)S(1)}, u32[]{:S(2)}) copy-start(bf16[5120,256]{1,0:T(8,128)(2,1)S(1)} %get-tuple-element.37) | copy-start | bytes 7864324
  41.7 25.1 %collective-permute-start.15 = (bf16[256,2560]{1,0:T(8,128)(2,1)S(1)}, bf16[256,2560]{1,0:T(8,128)(2,1)S(1)}, u32[]{:S(2)}, u32[]{:S(2)}) collective-permute-start(bf16[256,2560]{1,0:T(8,128)(2,1)S(1)} %copy-done.6), channel_id=1, source_target_pairs={{0,240},{16,0},{32,16},{48,32},{64,48},{80,64},{96,80},{112,96},{1... | collective-permute-start | bytes 3932168 | tf_op jit(solution)/shard_map/ppermute | solution.py:298
  41.9 14.4 %collective-permute-start.3 = (bf16[2,160,256]{2,1,0:T(8,128)(2,1)S(1)}, bf16[2,160,256]{2,1,0:T(8,128)(2,1)S(1)}, u32[]{:S(2)}, u32[]{:S(2)}) collective-permute-start(bf16[2,160,256]{2,1,0:T(8,128)(2,1)S(1)} %get-tuple-element.83), channel_id=1, source_target_pairs={{0,1},{1,2},{2,3},{3,4},{4,5},{5,6},{6,7},{7,0},{8,9},{9,10},{10,1... | collective-permute-start | bytes 491528 | tf_op jit(solution)/shard_map/ppermute | solution.py:304
  43.9 12.5 %collective-permute-start.4 = (bf16[2,160,256]{2,1,0:T(8,128)(2,1)S(1)}, bf16[2,160,256]{2,1,0:T(8,128)(2,1)S(1)}, u32[]{:S(2)}, u32[]{:S(2)}) collective-permute-start(bf16[2,160,256]{2,1,0:T(8,128)(2,1)S(1)} %get-tuple-element.82), channel_id=1, source_target_pairs={{0,7},{1,0},{2,1},{3,2},{4,3},{5,4},{6,5},{7,6},{8,15},{9,8},{10,9... | collective-permute-start | bytes 491528 | tf_op jit(solution)/shard_map/ppermute | solution.py:304
  47.9 1.1 copy-start.3
  50.9 7.7 %copy-start = (bf16[1,5120,384]{2,1,0:T(8,128)(2,1)S(1)}, bf16[1,5120,384]{2,1,0:T(8,128)(2,1)}, u32[]{:S(2)}) copy-start(bf16[1,5120,384]{2,1,0:T(8,128)(2,1)} %param.7) | copy-start | bytes 11796484
  51.0 10.6 %collective-permute-start.13 = (bf16[2,160,256]{2,1,0:T(8,128)(2,1)S(1)}, bf16[2,160,256]{2,1,0:T(8,128)(2,1)S(1)}, u32[]{:S(2)}, u32[]{:S(2)}) collective-permute-start(bf16[2,160,256]{2,1,0:T(8,128)(2,1)S(1)} %get-tuple-element.89), channel_id=1, source_target_pairs={{0,1},{1,2},{2,3},{3,4},{4,5},{5,6},{6,7},{7,0},{8,9},{9,10},{10,1... | collective-permute-start | bytes 491528 | tf_op jit(solution)/shard_map/ppermute | solution.py:304
  52.3 14.4 %collective-permute-start.14 = (bf16[2,160,256]{2,1,0:T(8,128)(2,1)S(1)}, bf16[2,160,256]{2,1,0:T(8,128)(2,1)S(1)}, u32[]{:S(2)}, u32[]{:S(2)}) collective-permute-start(bf16[2,160,256]{2,1,0:T(8,128)(2,1)S(1)} %get-tuple-element.88), channel_id=1, source_target_pairs={{0,7},{1,0},{2,1},{3,2},{4,3},{5,4},{6,5},{7,6},{8,15},{9,8},{10,9... | collective-permute-start | bytes 491528 | tf_op jit(solution)/shard_map/ppermute | solution.py:304
  56.5 13.2 %collective-permute-start.7 = (bf16[2,320,256]{2,1,0:T(8,128)(2,1)S(1)}, bf16[2,320,256]{2,1,0:T(8,128)(2,1)S(1)}, u32[]{:S(2)}, u32[]{:S(2)}) collective-permute-start(bf16[2,320,256]{2,1,0:T(8,128)(2,1)S(1)} %get-tuple-element.40), channel_id=1, source_target_pairs={{0,7},{1,0},{2,1},{3,2},{4,3},{5,4},{6,5},{7,6},{8,15},{9,8},{10,9... | collective-permute-start | bytes 983048 | tf_op jit(solution)/shard_map/ppermute | solution.py:304
  58.5 21.4 %collective-permute-start.5 = (bf16[2,320,256]{2,1,0:T(8,128)(2,1)S(1)}, bf16[2,320,256]{2,1,0:T(8,128)(2,1)S(1)}, u32[]{:S(2)}, u32[]{:S(2)}) collective-permute-start(bf16[2,320,256]{2,1,0:T(8,128)(2,1)S(1)} %get-tuple-element.39), channel_id=1, source_target_pairs={{0,1},{1,2},{2,3},{3,4},{4,5},{5,6},{6,7},{7,0},{8,9},{9,10},{10,1... | collective-permute-start | bytes 983048 | tf_op jit(solution)/shard_map/ppermute | solution.py:304
  61.6 35.5 %collective-permute-start.9 = (bf16[256,5120]{1,0:T(8,128)(2,1)}, bf16[256,5120]{1,0:T(8,128)(2,1)}, u32[]{:S(2)}, u32[]{:S(2)}) collective-permute-start(bf16[256,5120]{1,0:T(8,128)(2,1)} %far_term.1), channel_id=1, source_target_pairs={{0,16},{16,32},{32,48},{48,64},{64,80},{80,96},{96,112},{112,128},... | collective-permute-start | bytes 7864328 | tf_op jit(solution)/shard_map/ppermute | solution.py:298
  66.8 10.4 %collective-permute-start.19 = (bf16[2,320,256]{2,1,0:T(8,128)(2,1)S(1)}, bf16[2,320,256]{2,1,0:T(8,128)(2,1)S(1)}, u32[]{:S(2)}, u32[]{:S(2)}) collective-permute-start(bf16[2,320,256]{2,1,0:T(8,128)(2,1)S(1)} %pad_maximum_fusion.3), channel_id=1, source_target_pairs={{0,7},{1,0},{2,1},{3,2},{4,3},{5,4},{6,5},{7,6},{8,15},{9,8},{10,9... | collective-permute-start | bytes 983048 | tf_op jit(solution)/shard_map/ppermute | solution.py:304
  69.8 14.4 %collective-permute-start.8 = (bf16[2,320,256]{2,1,0:T(8,128)(2,1)S(1)}, bf16[2,320,256]{2,1,0:T(8,128)(2,1)S(1)}, u32[]{:S(2)}, u32[]{:S(2)}) collective-permute-start(bf16[2,320,256]{2,1,0:T(8,128)(2,1)S(1)} %bitcast_add_fusion.1), channel_id=1, source_target_pairs={{0,7},{1,0},{2,1},{3,2},{4,3},{5,4},{6,5},{7,6},{8,15},{9,8},{10,9... | collective-permute-start | bytes 983048 | tf_op jit(solution)/shard_map/ppermute | solution.py:304
  69.9 8.5 %collective-permute-start.16 = (bf16[2,320,256]{2,1,0:T(8,128)(2,1)S(1)}, bf16[2,320,256]{2,1,0:T(8,128)(2,1)S(1)}, u32[]{:S(2)}, u32[]{:S(2)}) collective-permute-start(bf16[2,320,256]{2,1,0:T(8,128)(2,1)S(1)} %fusion.7), channel_id=1, source_target_pairs={{0,1},{1,2},{2,3},{3,4},{4,5},{5,6},{6,7},{7,0},{8,9},{9,10},{10,1... | collective-permute-start | bytes 983048 | tf_op jit(solution)/shard_map/ppermute | solution.py:304
  77.2 14.0 %collective-permute-start.20 = (bf16[2,320,256]{2,1,0:T(8,128)(2,1)S(1)}, bf16[2,320,256]{2,1,0:T(8,128)(2,1)S(1)}, u32[]{:S(2)}, u32[]{:S(2)}) collective-permute-start(bf16[2,320,256]{2,1,0:T(8,128)(2,1)S(1)} %maximum_add_fusion.3), channel_id=1, source_target_pairs={{0,7},{1,0},{2,1},{3,2},{4,3},{5,4},{6,5},{7,6},{8,15},{9,8},{10,9... | collective-permute-start | bytes 983048 | tf_op jit(solution)/shard_map/ppermute | solution.py:304
  78.5 14.0 %collective-permute-start.17 = (bf16[2,320,256]{2,1,0:T(8,128)(2,1)S(1)}, bf16[2,320,256]{2,1,0:T(8,128)(2,1)S(1)}, u32[]{:S(2)}, u32[]{:S(2)}) collective-permute-start(bf16[2,320,256]{2,1,0:T(8,128)(2,1)S(1)} %maximum_add_fusion.1), channel_id=1, source_target_pairs={{0,1},{1,2},{2,3},{3,4},{4,5},{5,6},{6,7},{7,0},{8,9},{9,10},{10,1... | collective-permute-start | bytes 983048 | tf_op jit(solution)/shard_map/ppermute | solution.py:304
  84.2 11.9 %collective-permute-start.6 = (bf16[2,320,256]{2,1,0:T(8,128)(2,1)S(1)}, bf16[2,320,256]{2,1,0:T(8,128)(2,1)S(1)}, u32[]{:S(2)}, u32[]{:S(2)}) collective-permute-start(bf16[2,320,256]{2,1,0:T(8,128)(2,1)S(1)} %get-tuple-element.60), channel_id=1, source_target_pairs={{0,1},{1,2},{2,3},{3,4},{4,5},{5,6},{6,7},{7,0},{8,9},{9,10},{10,1... | collective-permute-start | bytes 983048 | tf_op jit(solution)/shard_map/ppermute | solution.py:304
  91.3 10.5 %collective-permute-start.21 = (bf16[2,320,256]{2,1,0:T(8,128)(2,1)S(1)}, bf16[2,320,256]{2,1,0:T(8,128)(2,1)S(1)}, u32[]{:S(2)}, u32[]{:S(2)}) collective-permute-start(bf16[2,320,256]{2,1,0:T(8,128)(2,1)S(1)} %maximum_add_fusion.2), channel_id=1, source_target_pairs={{0,7},{1,0},{2,1},{3,2},{4,3},{5,4},{6,5},{7,6},{8,15},{9,8},{10,9... | collective-permute-start | bytes 983048 | tf_op jit(solution)/shard_map/ppermute | solution.py:304
  92.5 11.9 %collective-permute-start.18 = (bf16[2,320,256]{2,1,0:T(8,128)(2,1)S(1)}, bf16[2,320,256]{2,1,0:T(8,128)(2,1)S(1)}, u32[]{:S(2)}, u32[]{:S(2)}) collective-permute-start(bf16[2,320,256]{2,1,0:T(8,128)(2,1)S(1)} %maximum_add_fusion), channel_id=1, source_target_pairs={{0,1},{1,2},{2,3},{3,4},{4,5},{5,6},{6,7},{7,0},{8,9},{9,10},{10,1... | collective-permute-start | bytes 983048 | tf_op jit(solution)/shard_map/ppermute | solution.py:304
  97.1 12.0 %collective-permute-start.11 = (bf16[2,320,256]{2,1,0:T(8,128)(2,1)S(1)}, bf16[2,320,256]{2,1,0:T(8,128)(2,1)S(1)}, u32[]{:S(2)}, u32[]{:S(2)}) collective-permute-start(bf16[2,320,256]{2,1,0:T(8,128)(2,1)S(1)} %get-tuple-element.43), channel_id=1, source_target_pairs={{0,7},{1,0},{2,1},{3,2},{4,3},{5,4},{6,5},{7,6},{8,15},{9,8},{10,9... | collective-permute-start | bytes 983048 | tf_op jit(solution)/shard_map/ppermute | solution.py:304
  97.2 14.3 %collective-permute-start.10 = (bf16[2,320,256]{2,1,0:T(8,128)(2,1)S(1)}, bf16[2,320,256]{2,1,0:T(8,128)(2,1)S(1)}, u32[]{:S(2)}, u32[]{:S(2)}) collective-permute-start(bf16[2,320,256]{2,1,0:T(8,128)(2,1)S(1)} %bitcast_add_fusion.4), channel_id=1, source_target_pairs={{0,1},{1,2},{2,3},{3,4},{4,5},{5,6},{6,7},{7,0},{8,9},{9,10},{10,1... | collective-permute-start | bytes 983048 | tf_op jit(solution)/shard_map/ppermute | solution.py:304
  112.8 11.5 %collective-permute-start.22 = (bf16[320,512]{1,0:T(8,128)(2,1)S(1)}, bf16[320,512]{1,0:T(8,128)(2,1)S(1)}, u32[]{:S(2)}, u32[]{:S(2)}) collective-permute-start(bf16[320,512]{1,0:T(8,128)(2,1)S(1)} %fusion.5), channel_id=1, source_target_pairs={{0,8},{1,9},{2,10},{3,11},{4,12},{5,13},{6,14},{7,15},{8,0},{9,1},... | collective-permute-start | bytes 983048 | tf_op jit(solution)/shard_map/ppermute | solution.py:309

commit v5 on v4

--- a/solution.py
+++ b/solution.py
@@ -90,7 +90,7 @@
 
 
 N_W = 4
-TILE = 1280
+TILE = 2560
 SMALL, LARGE = 14, 20
 
 

time: 127 us -> 127 us (level)
  no operation moved by 1% of the time
where the time goes in v5:
time: 127 us; the launch traced here: 126 us
  waiting for transfers between devices  45.8 us (36%)
  starting transfers between devices  33.6 us (26%)
  Pallas kernels  32.6 us (26%)
  local copies, waits for them, and re-layouts  6.97 us (5%)
  other arithmetic  3.57 us (3%)
  matrix products  2.15 us (2%)
    ppermute x16, starting transfers between devices, z_shifted(): return lax.ppermute(block, 'dp', route)  25.4 us
    ppermute x16, waiting for transfers between devices, z_shifted(): return lax.ppermute(block, 'dp', route)  25.3 us
    pallas_call x6, Pallas kernels, whole(): pl.pallas_call(kernel, in_specs=[here] * (len(args) - in_hbm) + [there] *...  22.4 us
    ppermute x1, waiting for transfers between devices, x_swapped(): return lax.ppermute(block, 'dp', [(i, (i + N_Z) % n) for i in range(n)])  10.8 us
    ppermute x6, waiting for transfers between devices, shifted(): lax.ppermute(block, 'blk', [(i, (i + distance) % n) for i in range(n)])  9.71 us
    ppermute x6, starting transfers between devices, shifted(): lax.ppermute(block, 'blk', [(i, (i + distance) % n) for i in range(n)])  7.6 us
    pallas_call x1, Pallas kernels, own_term(): pl.pallas_call(own_term_kernel, in_specs=[pl.BlockSpec(memory_space=pltpu...  5.3 us
    pallas_call x1, Pallas kernels, sum_of(): pl.pallas_call(sum_kernel, in_specs=[pl.BlockSpec(memory_space=pltpu.VMEM...  4.87 us
  transfers between devices with their start and end apart: 23, of which 11 were waited for; matrix products, arithmetic and copies ran while one was open for 5% of the time, Pallas kernels for 26%

profile of v5, /device:TPU:28, one launch (start us, length us, event | category | flops | bytes accessed | tf_op | source)
XLA Modules:
  0.0 125.7 jit_solution(6361060669405318492)
XLA Ops:
  0.6 0.3 collective-permute-start
  0.9 0.3 collective-permute-start.1
  1.2 0.8 fusion.25
  2.0 0.1 copy.10.seg_col_ref
  2.1 6.5 %own_pair.1 = (bf16[256,384]{1,0:T(8,128)(2,1)S(1)}, bf16[256,128]{1,0:T(8,128)(2,1)S(1)}) custom-call(s32[1,256]{1,0:T(1,128)S(1)} %get-tuple-element.93.seg_row_ref, s32[256,1]{1,0:T(8,128)S(1)} %copy.10.seg_col_ref, bf16[256,5120]{1,0:T(8,128)(2,1)} %bitcast.101, bf16[5120,384]{1,0:T(8,128)(2,1)} %bitcast.85, bf16[256,5120]{1,0:T(8,128)(2,1)} %bitcast.98, ...), custom_call_target="tpu_custom_call" | custom-call | flops 1 | bytes 1 | tf_op jit(solution)/shard_map/own_pair/pallas_call | solution.py:51
  8.7 5.3 %own_term.1.own_hbm = bf16[256,5120]{1,0:T(8,128)(2,1)} custom-call(bf16[256,384]{1,0:T(8,128)(2,1)S(1)} %get-tuple-element.36.d_ref, bf16[5120,384]{1,0:T(8,128)(2,1)} %bitcast.86), custom_call_target="tpu_custom_call" | custom-call | flops 1 | bytes 1 | tf_op jit(solution)/shard_map/own_term/pallas_call | solution.py:238
  14.0 4.2 %collective-permute-done.1 = bf16[128,5120]{1,0:T(8,128)(2,1)} collective-permute-done((bf16[128,5120]{1,0:T(8,128)(2,1)}, bf16[128,5120]{1,0:T(8,128)(2,1)}, u32[]{:S(2)}, u32[]{:S(2)}) %collective-permute-start.1) | collective-permute-done | bytes 1310752 | tf_op jit(solution)/shard_map/ppermute | solution.py:298
  18.2 2.2 %fusion.after_ref = bf16[256,128]{1,0:T(8,128)(2,1)S(1)} fusion(bf16[128,5120]{1,0:T(8,128)(2,1)} %collective-permute-done.1, bf16[1,256,5120]{2,1,0:T(8,128)(2,1)S(1)} %copy-done.7), kind=kOutput, calls=%fused_computation.12 | convolution fusion | flops 335577088 | bytes 3997696 | tf_op jit(solution)/shard_map/dot_general | solution.py:16
  20.4 0.1 collective-permute-start.2
  20.5 3.3 %columns.1 = (bf16[256,2560]{1,0:T(8,128)(2,1)}, bf16[256,2560]{1,0:T(8,128)(2,1)S(1)}, bf16[2560,128]{1,0:T(8,128)(2,1)S(1)}, bf16[2560,128]{1,0:T(8,128)(2,1)S(1)}) custom-call(bf16[256,128]{1,0:T(8,128)(2,1)S(1)} %fusion.after_ref, bf16[256,128]{1,0:T(8,128)(2,1)S(1)} %get-tuple-element.33.att_ref, bf16[256,5120]{1,0:T(8,128)(2,1)} %bitcast.99), custom_call_target="tpu_custom_call" | custom-call | flops 1 | bytes 1 | tf_op jit(solution)/shard_map/columns/pallas_call | solution.py:51
  23.8 0.9 copy-done.2
  24.7 1.1 copy-done.5
  25.8 5.2 %collective-permute-done.2.datt_ref = bf16[256,128]{1,0:T(8,128)(2,1)S(1)} collective-permute-done((bf16[256,128]{1,0:T(8,128)(2,1)S(1)}, bf16[256,128]{1,0:T(8,128)(2,1)S(1)}, u32[]{:S(2)}, u32[]{:S(2)}) %collective-permute-start.2) | collective-permute-done | bytes 65568 | tf_op jit(solution)/shard_map/ppermute | solution.py:298
  31.0 1.9 %collective-permute-start.12 = (bf16[256,2560]{1,0:T(8,128)(2,1)}, bf16[256,2560]{1,0:T(8,128)(2,1)}, u32[]{:S(2)}, u32[]{:S(2)}) collective-permute-start(bf16[256,2560]{1,0:T(8,128)(2,1)} %get-tuple-element.45), channel_id=1, source_target_pairs={{0,240},{16,0},{32,16},{48,32},{64,48},{80,64},{96,80},{112,96},{1... | collective-permute-start | bytes 3932168 | tf_op jit(solution)/shard_map/ppermute | solution.py:298
  32.9 0.8 copy.12.seg_col_ref
  33.7 0.9 copy-done.4
  34.6 7.1 %far_pair.1 = (bf16[256,384]{1,0:T(8,128)(2,1)S(1)}, bf16[256,128]{1,0:T(8,128)(2,1)S(1)}, bf16[5120,256]{1,0:T(8,128)(2,1)S(1)}, bf16[5120,128]{1,0:T(8,128)(2,1)S(1)}) custom-call(bf16[256,5120]{1,0:T(8,128)(2,1)S(1)} %collective-permute-done.xf_ref, bf16[256,128]{1,0:T(8,128)(2,1)S(1)} %collective-permute-done.2.datt_ref, ...), custom_call_target="tpu_custom_call" | custom-call | flops 1 | bytes 1 | tf_op jit(solution)/shard_map/far_pair/pallas_call | solution.py:51
  41.7 0.1 collective-permute-start.15
  41.9 2.0 %collective-permute-start.3 = (bf16[2,160,256]{2,1,0:T(8,128)(2,1)S(1)}, bf16[2,160,256]{2,1,0:T(8,128)(2,1)S(1)}, u32[]{:S(2)}, u32[]{:S(2)}) collective-permute-start(bf16[2,160,256]{2,1,0:T(8,128)(2,1)S(1)} %get-tuple-element.83), channel_id=1, source_target_pairs={{0,1},{1,2},{2,3},{3,4},{4,5},{5,6},{6,7},{7,0},{8,9},{9,10},{10,1... | collective-permute-start | bytes 491528 | tf_op jit(solution)/shard_map/ppermute | solution.py:304
  43.9 4.0 %collective-permute-start.4 = (bf16[2,160,256]{2,1,0:T(8,128)(2,1)S(1)}, bf16[2,160,256]{2,1,0:T(8,128)(2,1)S(1)}, u32[]{:S(2)}, u32[]{:S(2)}) collective-permute-start(bf16[2,160,256]{2,1,0:T(8,128)(2,1)S(1)} %get-tuple-element.82), channel_id=1, source_target_pairs={{0,7},{1,0},{2,1},{3,2},{4,3},{5,4},{6,5},{7,6},{8,15},{9,8},{10,9... | collective-permute-start | bytes 491528 | tf_op jit(solution)/shard_map/ppermute | solution.py:304
  48.0 0.1 dynamic-slice_bitcast_fusion.13
  48.0 0.3 collective-permute-done.12.g_ref
  48.3 0.7 copy-done.3
  49.0 1.9 %grads_out.2 = bf16[2560,128]{1,0:T(8,128)(2,1)S(1)} custom-call(bf16[256,2560]{1,0:T(8,128)(2,1)} %collective-permute-done.12.g_ref, bf16[256,128]{1,0:T(8,128)(2,1)S(1)} %get-tuple-element.48.att_ref, bf16[2560,128]{1,0:T(8,128)(2,1)S(1)} %copy-done.3), custom_call_target="tpu_custom_call" | custom-call | flops 1 | bytes 1 | tf_op jit(solution)/shard_map/grads_out/pallas_call | solution.py:51
  51.0 1.3 %collective-permute-start.13 = (bf16[2,160,256]{2,1,0:T(8,128)(2,1)S(1)}, bf16[2,160,256]{2,1,0:T(8,128)(2,1)S(1)}, u32[]{:S(2)}, u32[]{:S(2)}) collective-permute-start(bf16[2,160,256]{2,1,0:T(8,128)(2,1)S(1)} %get-tuple-element.89), channel_id=1, source_target_pairs={{0,1},{1,2},{2,3},{3,4},{4,5},{5,6},{6,7},{7,0},{8,9},{9,10},{10,1... | collective-permute-start | bytes 491528 | tf_op jit(solution)/shard_map/ppermute | solution.py:304
  52.3 4.0 %collective-permute-start.14 = (bf16[2,160,256]{2,1,0:T(8,128)(2,1)S(1)}, bf16[2,160,256]{2,1,0:T(8,128)(2,1)S(1)}, u32[]{:S(2)}, u32[]{:S(2)}) collective-permute-start(bf16[2,160,256]{2,1,0:T(8,128)(2,1)S(1)} %get-tuple-element.88), channel_id=1, source_target_pairs={{0,7},{1,0},{2,1},{3,2},{4,3},{5,4},{6,5},{7,6},{8,15},{9,8},{10,9... | collective-permute-start | bytes 491528 | tf_op jit(solution)/shard_map/ppermute | solution.py:304
  56.5 2.0 %collective-permute-start.7 = (bf16[2,320,256]{2,1,0:T(8,128)(2,1)S(1)}, bf16[2,320,256]{2,1,0:T(8,128)(2,1)S(1)}, u32[]{:S(2)}, u32[]{:S(2)}) collective-permute-start(bf16[2,320,256]{2,1,0:T(8,128)(2,1)S(1)} %get-tuple-element.40), channel_id=1, source_target_pairs={{0,7},{1,0},{2,1},{3,2},{4,3},{5,4},{6,5},{7,6},{8,15},{9,8},{10,9... | collective-permute-start | bytes 983048 | tf_op jit(solution)/shard_map/ppermute | solution.py:304
  58.5 0.1 collective-permute-start.5
  58.6 3.0 %far_term.1 = bf16[256,5120]{1,0:T(8,128)(2,1)} custom-call(bf16[256,384]{1,0:T(8,128)(2,1)S(1)} %get-tuple-element.41.d_ref, bf16[5120,384]{1,0:T(8,128)(2,1)S(1)} %bitcast.88), custom_call_target="tpu_custom_call" | custom-call | flops 2013265920 | bytes 1 | tf_op jit(solution)/shard_map/far_term/pallas_call | solution.py:51
  61.6 4.9 %collective-permute-start.9 = (bf16[256,5120]{1,0:T(8,128)(2,1)}, bf16[256,5120]{1,0:T(8,128)(2,1)}, u32[]{:S(2)}, u32[]{:S(2)}) collective-permute-start(bf16[256,5120]{1,0:T(8,128)(2,1)} %far_term.1), channel_id=1, source_target_pairs={{0,16},{16,32},{32,48},{48,64},{64,80},{80,96},{96,112},{112,128},... | collective-permute-start | bytes 7864328 | tf_op jit(solution)/shard_map/ppermute | solution.py:298
  66.8 2.9 %collective-permute-start.19 = (bf16[2,320,256]{2,1,0:T(8,128)(2,1)S(1)}, bf16[2,320,256]{2,1,0:T(8,128)(2,1)S(1)}, u32[]{:S(2)}, u32[]{:S(2)}) collective-permute-start(bf16[2,320,256]{2,1,0:T(8,128)(2,1)S(1)} %pad_maximum_fusion.3), channel_id=1, source_target_pairs={{0,7},{1,0},{2,1},{3,2},{4,3},{5,4},{6,5},{7,6},{8,15},{9,8},{10,9... | collective-permute-start | bytes 983048 | tf_op jit(solution)/shard_map/ppermute | solution.py:304
  69.8 0.1 collective-permute-start.8
  69.9 2.0 %collective-permute-start.16 = (bf16[2,320,256]{2,1,0:T(8,128)(2,1)S(1)}, bf16[2,320,256]{2,1,0:T(8,128)(2,1)S(1)}, u32[]{:S(2)}, u32[]{:S(2)}) collective-permute-start(bf16[2,320,256]{2,1,0:T(8,128)(2,1)S(1)} %fusion.7), channel_id=1, source_target_pairs={{0,1},{1,2},{2,3},{3,4},{4,5},{5,6},{6,7},{7,0},{8,9},{9,10},{10,1... | collective-permute-start | bytes 983048 | tf_op jit(solution)/shard_map/ppermute | solution.py:304
  71.9 0.6 grads_out.3
  72.4 0.3 fusion.21
  72.8 4.4 %collective-permute-done.19 = bf16[2,320,256]{2,1,0:T(8,128)(2,1)S(1)} collective-permute-done((bf16[2,320,256]{2,1,0:T(8,128)(2,1)S(1)}, bf16[2,320,256]{2,1,0:T(8,128)(2,1)S(1)}, u32[]{:S(2)}, u32[]{:S(2)}) %collective-permute-start.19) | collective-permute-done | bytes 327712 | tf_op jit(solution)/shard_map/ppermute | solution.py:304
  77.1 0.1 maximum_add_fusion.3
  77.2 1.2 collective-permute-start.20
  78.4 0.1 maximum_add_fusion.1
  78.5 1.4 %collective-permute-start.17 = (bf16[2,320,256]{2,1,0:T(8,128)(2,1)S(1)}, bf16[2,320,256]{2,1,0:T(8,128)(2,1)S(1)}, u32[]{:S(2)}, u32[]{:S(2)}) collective-permute-start(bf16[2,320,256]{2,1,0:T(8,128)(2,1)S(1)} %maximum_add_fusion.1), channel_id=1, source_target_pairs={{0,1},{1,2},{2,3},{3,4},{4,5},{5,6},{6,7},{7,0},{8,9},{9,10},{10,1... | collective-permute-start | bytes 983048 | tf_op jit(solution)/shard_map/ppermute | solution.py:304
  79.9 4.2 %collective-permute-done.8 = bf16[2,320,256]{2,1,0:T(8,128)(2,1)S(1)} collective-permute-done((bf16[2,320,256]{2,1,0:T(8,128)(2,1)S(1)}, bf16[2,320,256]{2,1,0:T(8,128)(2,1)S(1)}, u32[]{:S(2)}, u32[]{:S(2)}) %collective-permute-start.8) | collective-permute-done | bytes 327712 | tf_op jit(solution)/shard_map/ppermute | solution.py:304
  84.2 0.1 bitcast_add_fusion.2
  84.2 0.1 collective-permute-start.6
  84.3 6.8 %collective-permute-done.20 = bf16[2,320,256]{2,1,0:T(8,128)(2,1)S(1)} collective-permute-done((bf16[2,320,256]{2,1,0:T(8,128)(2,1)S(1)}, bf16[2,320,256]{2,1,0:T(8,128)(2,1)S(1)}, u32[]{:S(2)}, u32[]{:S(2)}) %collective-permute-start.20) | collective-permute-done | bytes 327712 | tf_op jit(solution)/shard_map/ppermute | solution.py:304
  91.2 0.1 maximum_add_fusion.2
  91.3 1.2 collective-permute-start.21
  92.4 0.1 maximum_add_fusion
  92.5 1.0 collective-permute-start.18
  93.5 2.6 %collective-permute-done.6 = bf16[2,320,256]{2,1,0:T(8,128)(2,1)S(1)} collective-permute-done((bf16[2,320,256]{2,1,0:T(8,128)(2,1)S(1)}, bf16[2,320,256]{2,1,0:T(8,128)(2,1)S(1)}, u32[]{:S(2)}, u32[]{:S(2)}) %collective-permute-start.6) | collective-permute-done | bytes 327712 | tf_op jit(solution)/shard_map/ppermute | solution.py:304
  96.1 1.0 bitcast_add_fusion.4
  97.1 0.1 collective-permute-start.11
  97.2 2.0 %collective-permute-start.10 = (bf16[2,320,256]{2,1,0:T(8,128)(2,1)S(1)}, bf16[2,320,256]{2,1,0:T(8,128)(2,1)S(1)}, u32[]{:S(2)}, u32[]{:S(2)}) collective-permute-start(bf16[2,320,256]{2,1,0:T(8,128)(2,1)S(1)} %bitcast_add_fusion.4), channel_id=1, source_target_pairs={{0,1},{1,2},{2,3},{3,4},{4,5},{5,6},{6,7},{7,0},{8,9},{9,10},{10,1... | collective-permute-start | bytes 983048 | tf_op jit(solution)/shard_map/ppermute | solution.py:304
  99.2 2.5 %collective-permute-done.21 = bf16[2,320,256]{2,1,0:T(8,128)(2,1)S(1)} collective-permute-done((bf16[2,320,256]{2,1,0:T(8,128)(2,1)S(1)}, bf16[2,320,256]{2,1,0:T(8,128)(2,1)S(1)}, u32[]{:S(2)}, u32[]{:S(2)}) %collective-permute-start.21) | collective-permute-done | bytes 327712 | tf_op jit(solution)/shard_map/ppermute | solution.py:304
  101.8 2.7 %collective-permute-done.18 = bf16[2,320,256]{2,1,0:T(8,128)(2,1)S(1)} collective-permute-done((bf16[2,320,256]{2,1,0:T(8,128)(2,1)S(1)}, bf16[2,320,256]{2,1,0:T(8,128)(2,1)S(1)}, u32[]{:S(2)}, u32[]{:S(2)}) %collective-permute-start.18) | collective-permute-done | bytes 327712 | tf_op jit(solution)/shard_map/ppermute | solution.py:304
  104.5 0.1 convert_add_fusion.1
  104.6 4.9 %sum_term.1 = bf16[256,5120]{1,0:T(8,128)(2,1)} custom-call(bf16[256,5120]{1,0:T(8,128)(2,1)} %collective-permute-done.9.far_ref, bf16[256,5120]{1,0:T(8,128)(2,1)} %own_term.1.own_hbm), custom_call_target="tpu_custom_call" | custom-call | flops 2000000000 | bytes 1 | tf_op jit(solution)/shard_map/sum_term/pallas_call | solution.py:279
  109.5 2.0 %collective-permute-done.10 = bf16[2,320,256]{2,1,0:T(8,128)(2,1)S(1)} collective-permute-done((bf16[2,320,256]{2,1,0:T(8,128)(2,1)S(1)}, bf16[2,320,256]{2,1,0:T(8,128)(2,1)S(1)}, u32[]{:S(2)}, u32[]{:S(2)}) %collective-permute-start.10) | collective-permute-done | bytes 327712 | tf_op jit(solution)/shard_map/ppermute | solution.py:304
  111.5 1.1 fusion.3
  112.6 0.2 pad_maximum_fusion
  112.8 0.6 collective-permute-start.22
  113.4 10.8 %collective-permute-done.22 = bf16[320,512]{1,0:T(8,128)(2,1)S(1)} collective-permute-done((bf16[320,512]{1,0:T(8,128)(2,1)S(1)}, bf16[320,512]{1,0:T(8,128)(2,1)S(1)}, u32[]{:S(2)}, u32[]{:S(2)}) %collective-permute-start.22) | collective-permute-done | bytes 327712 | tf_op jit(solution)/shard_map/ppermute | solution.py:309
  124.2 0.1 fusion.4
  124.3 0.7 slice_bitcast_fusion
  125.0 0.6 slice_bitcast_fusion.1
  (37 shorter events, 0.6 us)
Async XLA Ops:
  0.6 33.1 %collective-permute-start = (bf16[256,5120]{1,0:T(8,128)(2,1)}, bf16[256,5120]{1,0:T(8,128)(2,1)S(1)}, u32[]{:S(2)}, u32[]{:S(2)}) collective-permute-start(bf16[256,5120]{1,0:T(8,128)(2,1)} %bitcast.100), channel_id=1, source_target_pairs={{0,240},{16,0},{32,16},{48,32},{64,48},{80,64},{96,80},{112,96},{1... | collective-permute-start | bytes 7864328 | tf_op jit(solution)/shard_map/ppermute | solution.py:298
  0.9 17.3 %collective-permute-start.1 = (bf16[128,5120]{1,0:T(8,128)(2,1)}, bf16[128,5120]{1,0:T(8,128)(2,1)}, u32[]{:S(2)}, u32[]{:S(2)}) collective-permute-start(bf16[128,5120]{1,0:T(8,128)(2,1)} %bitcast.104), channel_id=1, source_target_pairs={{0,16},{16,32},{32,48},{48,64},{64,80},{80,96},{96,112},{112,128},... | collective-permute-start | bytes 3932168 | tf_op jit(solution)/shard_map/ppermute | solution.py:298
  8.7 9.6 %copy-start.7 = (bf16[1,256,5120]{2,1,0:T(8,128)(2,1)S(1)}, bf16[1,256,5120]{2,1,0:T(8,128)(2,1)}, u32[]{:S(2)}) copy-start(bf16[1,256,5120]{2,1,0:T(8,128)(2,1)} %param.9) | copy-start | bytes 7864324
  20.4 10.6 %collective-permute-start.2 = (bf16[256,128]{1,0:T(8,128)(2,1)S(1)}, bf16[256,128]{1,0:T(8,128)(2,1)S(1)}, u32[]{:S(2)}, u32[]{:S(2)}) collective-permute-start(bf16[256,128]{1,0:T(8,128)(2,1)S(1)} %fusion.after_ref), channel_id=1, source_target_pairs={{0,240},{16,0},{32,16},{48,32},{64,48},{80,64},{96,80},{112,96},{1... | collective-permute-start | bytes 196616 | tf_op jit(solution)/shard_map/ppermute | solution.py:298
  23.8 0.9 copy-start.2
  24.7 1.1 copy-start.5
  31.0 17.3 %collective-permute-start.12 = (bf16[256,2560]{1,0:T(8,128)(2,1)}, bf16[256,2560]{1,0:T(8,128)(2,1)}, u32[]{:S(2)}, u32[]{:S(2)}) collective-permute-start(bf16[256,2560]{1,0:T(8,128)(2,1)} %get-tuple-element.45), channel_id=1, source_target_pairs={{0,240},{16,0},{32,16},{48,32},{64,48},{80,64},{96,80},{112,96},{1... | collective-permute-start | bytes 3932168 | tf_op jit(solution)/shard_map/ppermute | solution.py:298
  33.7 0.9 copy-start.4
  34.6 7.1 %copy-start.6 = (bf16[256,2560]{1,0:T(8,128)(2,1)S(1)}, bf16[256,2560]{1,0:T(8,128)(2,1)}, u32[]{:S(2)}) copy-start(bf16[256,2560]{1,0:T(8,128)(2,1)} %copy-done.5) | copy-start | bytes 3932164
  41.7 42.5 %copy-start.1 = (bf16[5120,256]{1,0:T(8,128)(2,1)}, bf16[5120,256]{1,0:T(8,128)(2,1)S(1)}, u32[]{:S(2)}) copy-start(bf16[5120,256]{1,0:T(8,128)(2,1)S(1)} %get-tuple-element.37) | copy-start | bytes 7864324
  41.7 25.0 %collective-permute-start.15 = (bf16[256,2560]{1,0:T(8,128)(2,1)S(1)}, bf16[256,2560]{1,0:T(8,128)(2,1)S(1)}, u32[]{:S(2)}, u32[]{:S(2)}) collective-permute-start(bf16[256,2560]{1,0:T(8,128)(2,1)S(1)} %copy-done.6), channel_id=1, source_target_pairs={{0,240},{16,0},{32,16},{48,32},{64,48},{80,64},{96,80},{112,96},{1... | collective-permute-start | bytes 3932168 | tf_op jit(solution)/shard_map/ppermute | solution.py:298
  41.9 14.4 %collective-permute-start.3 = (bf16[2,160,256]{2,1,0:T(8,128)(2,1)S(1)}, bf16[2,160,256]{2,1,0:T(8,128)(2,1)S(1)}, u32[]{:S(2)}, u32[]{:S(2)}) collective-permute-start(bf16[2,160,256]{2,1,0:T(8,128)(2,1)S(1)} %get-tuple-element.83), channel_id=1, source_target_pairs={{0,1},{1,2},{2,3},{3,4},{4,5},{5,6},{6,7},{7,0},{8,9},{9,10},{10,1... | collective-permute-start | bytes 491528 | tf_op jit(solution)/shard_map/ppermute | solution.py:304
  43.9 12.5 %collective-permute-start.4 = (bf16[2,160,256]{2,1,0:T(8,128)(2,1)S(1)}, bf16[2,160,256]{2,1,0:T(8,128)(2,1)S(1)}, u32[]{:S(2)}, u32[]{:S(2)}) collective-permute-start(bf16[2,160,256]{2,1,0:T(8,128)(2,1)S(1)} %get-tuple-element.82), channel_id=1, source_target_pairs={{0,7},{1,0},{2,1},{3,2},{4,3},{5,4},{6,5},{7,6},{8,15},{9,8},{10,9... | collective-permute-start | bytes 491528 | tf_op jit(solution)/shard_map/ppermute | solution.py:304
  47.9 1.1 copy-start.3
  50.9 7.7 %copy-start = (bf16[1,5120,384]{2,1,0:T(8,128)(2,1)S(1)}, bf16[1,5120,384]{2,1,0:T(8,128)(2,1)}, u32[]{:S(2)}) copy-start(bf16[1,5120,384]{2,1,0:T(8,128)(2,1)} %param.7) | copy-start | bytes 11796484
  51.0 10.6 %collective-permute-start.13 = (bf16[2,160,256]{2,1,0:T(8,128)(2,1)S(1)}, bf16[2,160,256]{2,1,0:T(8,128)(2,1)S(1)}, u32[]{:S(2)}, u32[]{:S(2)}) collective-permute-start(bf16[2,160,256]{2,1,0:T(8,128)(2,1)S(1)} %get-tuple-element.89), channel_id=1, source_target_pairs={{0,1},{1,2},{2,3},{3,4},{4,5},{5,6},{6,7},{7,0},{8,9},{9,10},{10,1... | collective-permute-start | bytes 491528 | tf_op jit(solution)/shard_map/ppermute | solution.py:304
  52.3 14.4 %collective-permute-start.14 = (bf16[2,160,256]{2,1,0:T(8,128)(2,1)S(1)}, bf16[2,160,256]{2,1,0:T(8,128)(2,1)S(1)}, u32[]{:S(2)}, u32[]{:S(2)}) collective-permute-start(bf16[2,160,256]{2,1,0:T(8,128)(2,1)S(1)} %get-tuple-element.88), channel_id=1, source_target_pairs={{0,7},{1,0},{2,1},{3,2},{4,3},{5,4},{6,5},{7,6},{8,15},{9,8},{10,9... | collective-permute-start | bytes 491528 | tf_op jit(solution)/shard_map/ppermute | solution.py:304
  56.5 13.2 %collective-permute-start.7 = (bf16[2,320,256]{2,1,0:T(8,128)(2,1)S(1)}, bf16[2,320,256]{2,1,0:T(8,128)(2,1)S(1)}, u32[]{:S(2)}, u32[]{:S(2)}) collective-permute-start(bf16[2,320,256]{2,1,0:T(8,128)(2,1)S(1)} %get-tuple-element.40), channel_id=1, source_target_pairs={{0,7},{1,0},{2,1},{3,2},{4,3},{5,4},{6,5},{7,6},{8,15},{9,8},{10,9... | collective-permute-start | bytes 983048 | tf_op jit(solution)/shard_map/ppermute | solution.py:304
  58.5 21.4 %collective-permute-start.5 = (bf16[2,320,256]{2,1,0:T(8,128)(2,1)S(1)}, bf16[2,320,256]{2,1,0:T(8,128)(2,1)S(1)}, u32[]{:S(2)}, u32[]{:S(2)}) collective-permute-start(bf16[2,320,256]{2,1,0:T(8,128)(2,1)S(1)} %get-tuple-element.39), channel_id=1, source_target_pairs={{0,1},{1,2},{2,3},{3,4},{4,5},{5,6},{6,7},{7,0},{8,9},{9,10},{10,1... | collective-permute-start | bytes 983048 | tf_op jit(solution)/shard_map/ppermute | solution.py:304
  61.6 35.5 %collective-permute-start.9 = (bf16[256,5120]{1,0:T(8,128)(2,1)}, bf16[256,5120]{1,0:T(8,128)(2,1)}, u32[]{:S(2)}, u32[]{:S(2)}) collective-permute-start(bf16[256,5120]{1,0:T(8,128)(2,1)} %far_term.1), channel_id=1, source_target_pairs={{0,16},{16,32},{32,48},{48,64},{64,80},{80,96},{96,112},{112,128},... | collective-permute-start | bytes 7864328 | tf_op jit(solution)/shard_map/ppermute | solution.py:298
  66.8 10.4 %collective-permute-start.19 = (bf16[2,320,256]{2,1,0:T(8,128)(2,1)S(1)}, bf16[2,320,256]{2,1,0:T(8,128)(2,1)S(1)}, u32[]{:S(2)}, u32[]{:S(2)}) collective-permute-start(bf16[2,320,256]{2,1,0:T(8,128)(2,1)S(1)} %pad_maximum_fusion.3), channel_id=1, source_target_pairs={{0,7},{1,0},{2,1},{3,2},{4,3},{5,4},{6,5},{7,6},{8,15},{9,8},{10,9... | collective-permute-start | bytes 983048 | tf_op jit(solution)/shard_map/ppermute | solution.py:304
  69.8 14.4 %collective-permute-start.8 = (bf16[2,320,256]{2,1,0:T(8,128)(2,1)S(1)}, bf16[2,320,256]{2,1,0:T(8,128)(2,1)S(1)}, u32[]{:S(2)}, u32[]{:S(2)}) collective-permute-start(bf16[2,320,256]{2,1,0:T(8,128)(2,1)S(1)} %bitcast_add_fusion.1), channel_id=1, source_target_pairs={{0,7},{1,0},{2,1},{3,2},{4,3},{5,4},{6,5},{7,6},{8,15},{9,8},{10,9... | collective-permute-start | bytes 983048 | tf_op jit(solution)/shard_map/ppermute | solution.py:304
  69.9 8.5 %collective-permute-start.16 = (bf16[2,320,256]{2,1,0:T(8,128)(2,1)S(1)}, bf16[2,320,256]{2,1,0:T(8,128)(2,1)S(1)}, u32[]{:S(2)}, u32[]{:S(2)}) collective-permute-start(bf16[2,320,256]{2,1,0:T(8,128)(2,1)S(1)} %fusion.7), channel_id=1, source_target_pairs={{0,1},{1,2},{2,3},{3,4},{4,5},{5,6},{6,7},{7,0},{8,9},{9,10},{10,1... | collective-permute-start | bytes 983048 | tf_op jit(solution)/shard_map/ppermute | solution.py:304
  77.2 14.0 %collective-permute-start.20 = (bf16[2,320,256]{2,1,0:T(8,128)(2,1)S(1)}, bf16[2,320,256]{2,1,0:T(8,128)(2,1)S(1)}, u32[]{:S(2)}, u32[]{:S(2)}) collective-permute-start(bf16[2,320,256]{2,1,0:T(8,128)(2,1)S(1)} %maximum_add_fusion.3), channel_id=1, source_target_pairs={{0,7},{1,0},{2,1},{3,2},{4,3},{5,4},{6,5},{7,6},{8,15},{9,8},{10,9... | collective-permute-start | bytes 983048 | tf_op jit(solution)/shard_map/ppermute | solution.py:304
  78.5 14.0 %collective-permute-start.17 = (bf16[2,320,256]{2,1,0:T(8,128)(2,1)S(1)}, bf16[2,320,256]{2,1,0:T(8,128)(2,1)S(1)}, u32[]{:S(2)}, u32[]{:S(2)}) collective-permute-start(bf16[2,320,256]{2,1,0:T(8,128)(2,1)S(1)} %maximum_add_fusion.1), channel_id=1, source_target_pairs={{0,1},{1,2},{2,3},{3,4},{4,5},{5,6},{6,7},{7,0},{8,9},{9,10},{10,1... | collective-permute-start | bytes 983048 | tf_op jit(solution)/shard_map/ppermute | solution.py:304
  84.2 11.9 %collective-permute-start.6 = (bf16[2,320,256]{2,1,0:T(8,128)(2,1)S(1)}, bf16[2,320,256]{2,1,0:T(8,128)(2,1)S(1)}, u32[]{:S(2)}, u32[]{:S(2)}) collective-permute-start(bf16[2,320,256]{2,1,0:T(8,128)(2,1)S(1)} %get-tuple-element.60), channel_id=1, source_target_pairs={{0,1},{1,2},{2,3},{3,4},{4,5},{5,6},{6,7},{7,0},{8,9},{9,10},{10,1... | collective-permute-start | bytes 983048 | tf_op jit(solution)/shard_map/ppermute | solution.py:304
  91.3 10.5 %collective-permute-start.21 = (bf16[2,320,256]{2,1,0:T(8,128)(2,1)S(1)}, bf16[2,320,256]{2,1,0:T(8,128)(2,1)S(1)}, u32[]{:S(2)}, u32[]{:S(2)}) collective-permute-start(bf16[2,320,256]{2,1,0:T(8,128)(2,1)S(1)} %maximum_add_fusion.2), channel_id=1, source_target_pairs={{0,7},{1,0},{2,1},{3,2},{4,3},{5,4},{6,5},{7,6},{8,15},{9,8},{10,9... | collective-permute-start | bytes 983048 | tf_op jit(solution)/shard_map/ppermute | solution.py:304
  92.5 11.9 %collective-permute-start.18 = (bf16[2,320,256]{2,1,0:T(8,128)(2,1)S(1)}, bf16[2,320,256]{2,1,0:T(8,128)(2,1)S(1)}, u32[]{:S(2)}, u32[]{:S(2)}) collective-permute-start(bf16[2,320,256]{2,1,0:T(8,128)(2,1)S(1)} %maximum_add_fusion), channel_id=1, source_target_pairs={{0,1},{1,2},{2,3},{3,4},{4,5},{5,6},{6,7},{7,0},{8,9},{9,10},{10,1... | collective-permute-start | bytes 983048 | tf_op jit(solution)/shard_map/ppermute | solution.py:304
  97.1 12.3 %collective-permute-start.11 = (bf16[2,320,256]{2,1,0:T(8,128)(2,1)S(1)}, bf16[2,320,256]{2,1,0:T(8,128)(2,1)S(1)}, u32[]{:S(2)}, u32[]{:S(2)}) collective-permute-start(bf16[2,320,256]{2,1,0:T(8,128)(2,1)S(1)} %get-tuple-element.43), channel_id=1, source_target_pairs={{0,7},{1,0},{2,1},{3,2},{4,3},{5,4},{6,5},{7,6},{8,15},{9,8},{10,9... | collective-permute-start | bytes 983048 | tf_op jit(solution)/shard_map/ppermute | solution.py:304
  97.2 14.3 %collective-permute-start.10 = (bf16[2,320,256]{2,1,0:T(8,128)(2,1)S(1)}, bf16[2,320,256]{2,1,0:T(8,128)(2,1)S(1)}, u32[]{:S(2)}, u32[]{:S(2)}) collective-permute-start(bf16[2,320,256]{2,1,0:T(8,128)(2,1)S(1)} %bitcast_add_fusion.4), channel_id=1, source_target_pairs={{0,1},{1,2},{2,3},{3,4},{4,5},{5,6},{6,7},{7,0},{8,9},{9,10},{10,1... | collective-permute-start | bytes 983048 | tf_op jit(solution)/shard_map/ppermute | solution.py:304
  112.8 11.4 %collective-permute-start.22 = (bf16[320,512]{1,0:T(8,128)(2,1)S(1)}, bf16[320,512]{1,0:T(8,128)(2,1)S(1)}, u32[]{:S(2)}, u32[]{:S(2)}) collective-permute-start(bf16[320,512]{1,0:T(8,128)(2,1)S(1)} %fusion.5), channel_id=1, source_target_pairs={{0,8},{1,9},{2,10},{3,11},{4,12},{5,13},{6,14},{7,15},{8,0},{9,1},... | collective-permute-start | bytes 983048 | tf_op jit(solution)/shard_map/ppermute | solution.py:309
